TPU v7x, 32 devices: a whole 2x2x4 slice. The times are simulated.
32 devices in a mesh: dp: 2 (over core), gx: 4 (over y, x), gy: 4 (over z).
Axes of the slice: x: 2, y: 2, z: 4, core: 2. Of those that a mesh axis runs over, the one named last changes fastest.
Arguments:
- hidden_in: bfloat16 [2, 2048, 1088], P(None, ('dp', 'gy'), 'gx'), may hold values from -6 to 6
- segment_ids: int32 [2, 2048], P(None, 'dp'), may hold values from 0 to 31, as said below
- cotangent: bfloat16 [2, 2048, 1088], P(None, ('dp', 'gy'), 'gx'), may hold values from -6 to 6
- norm1_gain: bfloat16 [1088], replicated, may hold values from 0.5 to 1.5
- norm1_shift: bfloat16 [1088], replicated, may hold values from -1.75 to 1.75
- w_qkv: bfloat16 [1088, 3264], P('gx', 'gy'), may hold values from -0.1875 to 0.1875
- q_bias: bfloat16 [1088], replicated, may hold values from -1.75 to 1.75
- v_bias: bfloat16 [1088], replicated, may hold values from -0.1875 to 0.1875
- w_out: bfloat16 [1088, 1088], P('gy', 'gx'), may hold values from -1.5 to 1.5
- out_bias: bfloat16 [1088], replicated, may hold values from -1.75 to 1.75
- norm2_gain: bfloat16 [1088], replicated, may hold values from 0.5 to 1.5
- norm2_shift: bfloat16 [1088], replicated, may hold values from -1.75 to 1.75
- w_up: bfloat16 [1088, 4352], P('gx', 'gy'), may hold values from -0.1875 to 0.1875
- up_bias: bfloat16 [4352], replicated, may hold values from -1.75 to 1.75
- w_down: bfloat16 [4352, 1088], P('gy', 'gx'), may hold values from -0.09375 to 0.09375
- down_bias: bfloat16 [1088], replicated, may hold values from -1.75 to 1.75
Outputs:
- hidden_out: bfloat16 [2, 2048, 1088], P(None, ('dp', 'gy'), 'gx')
- grad_in: bfloat16 [2, 2048, 1088], P(None, ('dp', 'gy'), 'gx')
- grad_norm1_gain: float32 [1088], replicated
- grad_norm1_shift: float32 [1088], replicated
- grad_w_qkv: float32 [1088, 3264], P('gx', 'gy')
- grad_q_bias: float32 [1088], replicated
- grad_v_bias: float32 [1088], replicated
- grad_w_out: float32 [1088, 1088], P('gy', 'gx')
- grad_out_bias: float32 [1088], replicated
- grad_norm2_gain: float32 [1088], replicated
- grad_norm2_shift: float32 [1088], replicated
- grad_w_up: float32 [1088, 4352], P('gx', 'gy')
- grad_up_bias: float32 [4352], replicated
- grad_w_down: float32 [4352, 1088], P('gy', 'gx')
- grad_down_bias: float32 [1088], replicated
Inputs may be any that keep to these rules, and one draw needn't show every extreme that they name: `segment_ids`: documents never span two sequences of 1024 tokens; numbers rise along a sequence, its documents but the last are numbered upward from 8 times the sequence's place in the whole array, and its last document is numbered 8 times that place plus 7. Every document but the last of a sequence has 200 to 1000 tokens; the last is cut at the sequence's end, so a sequence holds 2 to 6 documents.
All inputs are finite; a program needn't handle non-finite values.
Results may differ from a plain program's by a relative error of at most 0.014.
Values may be sent and summed in bfloat16 or wider, within the bound.
No kernel may reach another device: no remote copies, remote signals or barrier semaphores. Data moves between devices by JAX's collectives and lax.ppermute only.
A program may use at most 128 MiB of HBM per device.

v0:
```python
import math

import jax
import jax.numpy as jnp
import numpy as np
from jax import lax
from jax.experimental import pallas as pl
from jax.experimental.pallas import tpu as pltpu
from jax.sharding import Mesh
from jax.sharding import PartitionSpec as P

HEAD_DIM = 64
PAIR = 2 * HEAD_DIM
EPSILON = 1e-05
BLOCKED = -1e30
BF = jnp.bfloat16
F32 = jnp.float32
PLANE = ("c", "gx")
EVERY = ("c", "gx", "gy")
ROOT = math.sqrt(2.0 / math.pi)
WINDOW = 128
TALL = WINDOW + 16
MIB = 1024 * 1024


def dot(left, right, dims):
    return lax.dot_general(left, right, (dims, ((), ())), preferred_element_type=F32)


def padded(shape, kind):
    size = jnp.dtype(kind).itemsize
    lines = 1 if len(shape) < 2 else -(-shape[-2] // 16) * 16
    return math.prod(shape[:-2]) * lines * (-(-shape[-1] // 128) * 128) * size


def kernel(body, outs, scratch, ids, *arrays, us=1.0, work=2, after=(), far=False):
    count, late = len(arrays), len(after)

    def run(*refs):
        body(*refs[: 1 + count], *refs[1 + count + late :])

    vmem = pl.BlockSpec(memory_space=pltpu.VMEM)
    total = sum(padded(a.shape, a.dtype) for a in arrays) + sum(padded(*o) for o in [*outs, *scratch])
    result = pl.pallas_call(
        run,
        name=body.__name__,
        out_shape=tuple(jax.ShapeDtypeStruct(shape, kind) for shape, kind in outs),
        in_specs=[pl.BlockSpec(memory_space=pltpu.SMEM)] + [vmem] * count + [pl.BlockSpec(memory_space=pl.ANY)] * late,
        out_specs=tuple(vmem for _ in outs),
        scratch_shapes=[pltpu.VMEM(shape, kind) for shape, kind in scratch],
        compiler_params=pltpu.CompilerParams(vmem_limit_bytes=60 * MIB if far else int(total * 1.02) + work * MIB),
        cost_estimate=pl.CostEstimate(flops=int(us * 5e9), bytes_accessed=int(us * 1e5), transcendentals=0),
    )(ids, *arrays, *after)
    return result if len(outs) > 1 else result[0]


def swap_core(value):
    return lax.ppermute(value, "c", [(0, 1), (1, 0)])


def from_peer(value, step):
    return lax.ppermute(value, "gx", [(i, i ^ step) for i in range(4)])


def from_below(value, step):
    return lax.ppermute(value, "gy", [(i, (i + step) % 4) for i in range(4)])


def gather_plane(own):
    near = [own] + [from_peer(own, k) for k in range(1, 4)]
    return near + [swap_core(piece) for piece in near]


def position(c, g, z):
    return (c * 4 + g) * 4 + z


def token_moves():
    moves = []
    for m in range(4):
        move = []
        for c in range(2):
            for g in range(4):
                for z in range(4):
                    t, mb = (m ^ g) >> 1, (m ^ g) & 1
                    move.append((position(c, g, z), position(z // 2, 2 * (z % 2) + t, 2 * mb + c)))
        moves.append(move)
    return moves


MOVES = token_moves()
BACK = [[(b, a) for a, b in move] for move in MOVES]


def run_table(width, cols):
    table = np.zeros((8, 4, 3), np.int32)
    for d in range(8):
        filled = 0
        for z in range(4):
            for t in range(3):
                low = max(width * t + PAIR * d, cols * z)
                high = min(width * t + PAIR * (d + 1), cols * (z + 1))
                if high > low:
                    table[d, z] = (low - cols * z, high - low, filled)
                    filled += high - low
            if table[d, z, 1] == 0:
                table[d, z, 2] = filled
    return table.reshape(-1)


def aligned(value, step):
    return pl.multiple_of(value, step)


def normed(rows):
    average = jnp.mean(rows, axis=1, keepdims=True)
    centered = rows - average
    inverse = lax.rsqrt(jnp.mean(centered * centered, axis=1, keepdims=True) + EPSILON)
    return centered * inverse, inverse


def norm_pull(upstream, centered, inverse, gain):
    scaled = upstream * gain
    return inverse * (
        scaled
        - jnp.mean(scaled, axis=1, keepdims=True)
        - centered * jnp.mean(scaled * centered, axis=1, keepdims=True)
    )


def column_sum(rows):
    return jnp.sum(rows, axis=0, keepdims=True)


def place(ids):
    return ids[0], ids[1], ids[2], ids[3]


def run_of(ids, d, z):
    at = 4 + d * 12 + z * 3
    return ids[at], ids[at + 1], ids[at + 2]


def lanes_of(half, rows):
    return pl.ds(aligned(half * rows, rows), rows)


def send_tokens(ids, x, g_in, *outs):
    g = ids[1]
    for m in range(4):
        v = m ^ g
        for t, src in enumerate((x, g_in)):
            outs[m][t] = src[v & 1, :, lanes_of(v >> 1, outs[m].shape[2])]


def own_rows(ids, blocks, held, which):
    e = 2 * (ids[1] & 1) + (ids[2] >> 1)
    for m in range(4):
        held[m ^ e] = blocks[m][which]
    return held[...].astype(F32).reshape(-1, held.shape[2]).T


def take_tokens(ids, b0, b1, b2, b3, out, held):
    out[...] = own_rows(ids, (b0, b1, b2, b3), held, 1).astype(BF)


def take_normed(ids, b0, b1, b2, b3, vectors, out, low, held):
    rows = own_rows(ids, (b0, b1, b2, b3), held, 0)
    out[...] = rows.astype(BF)
    low[...] = (normed(rows)[0] * vectors[0:1] + vectors[1:2]).astype(BF)


def land_tokens(ids, b0, b1, b2, b3, first, second):
    g = ids[1]
    for m, block in enumerate((b0, b1, b2, b3)):
        v = m ^ g
        for t, out in enumerate((first, second)):
            out[v & 1, :, lanes_of(v >> 1, block.shape[2])] = block[t]


def qkv_windows(ids, w, o0, o1, o2, o3, tall):
    c, g, z, d = place(ids)
    rows = w.shape[1]
    tall[:rows] = w[...].astype(F32).T
    tall[rows:] = jnp.zeros((tall.shape[0] - rows, tall.shape[1]), F32)
    for k, ref in enumerate((o0, o1, o2, o3)):
        start, _, _ = run_of(ids, c * 4 + (g ^ k), z)
        ref[...] = tall[pl.ds(aligned(start, 16), WINDOW)].astype(BF)


def join_lanes(ids, b0, b1, b2, b3, piece, out, held):
    g = ids[1]
    for k, block in enumerate((b0, b1, b2, b3)):
        held[g ^ k] = block[...]
    part = held.shape[2]
    lines = piece.shape[0] // 4
    for i in range(4):
        at = slice(i * part, (i + 1) * part)
        out[:WINDOW, at] = held[i]
        out[WINDOW:, at] = piece[i * lines : (i + 1) * lines]


def qkv_assemble(ids, b0, b1, b2, b3, out, row, held, tall):
    c, g, z, d = place(ids)
    for s, block in enumerate((b0, b1, b2, b3)):
        held[(z + 4 - s) & 3] = block[...]
    for i in range(4):
        _, _, filled = run_of(ids, d, i)
        tall[pl.ds(aligned(filled, 16), WINDOW)] = held[i, :WINDOW]
    out[...] = tall[: out.shape[0]]
    part = out.shape[1] // 4
    lines = held.shape[1] - WINDOW
    shared = []
    for i in range(4):
        for j in range(3):
            piece = held[i, WINDOW:, j * part : (j + 1) * part]
            row[j * lines : (j + 1) * lines, i * part : (i + 1) * part] = piece
        if i:
            piece = held[i, WINDOW:, 3 * part :].astype(F32)
            shared.append(jnp.concatenate([piece[8 * k : 8 * k + 8] for k in range(4)], 1))
    shared.append(jnp.zeros_like(shared[0]))
    row[TALL:] = jnp.concatenate(shared, 0).astype(BF)


def mlp_blocks(ids, up, down, bias, o0, o1, o2, o3, own_bias, held):
    c, g, z, d = place(ids)
    for t, w in enumerate((up, down)):
        held[t] = w[...].astype(F32).T.reshape(held.shape[1:])
    for k, ref in enumerate((o0, o1, o2, o3)):
        to = c * 4 + (g ^ k)
        ref[0] = held[0, to].astype(BF)
        ref[1] = held[1, to].astype(BF)
    own_bias[...] = jnp.concatenate([bias[i, pl.ds(d, 1)] for i in range(4)], 1)


def mlp_join(ids, b0, b1, b2, b3, up, down, held):
    g = ids[1]
    for k, block in enumerate((b0, b1, b2, b3)):
        held[g ^ k] = block[...]
    part = held.shape[3]
    for i in range(4):
        up[:, i * part : (i + 1) * part] = held[i, 0]
        down[:, i * part : (i + 1) * part] = held[i, 1]


def out_half(ids, w, wq, out, tall):
    c, _, z, _ = place(ids)
    tall[: w.shape[1]] = w[...].astype(F32).T
    out[:TALL] = tall[pl.ds(aligned(c * WINDOW, 8), TALL)].astype(BF)
    tall[: wq.shape[1]] = wq[...].astype(F32).T
    at = jnp.maximum(272 * z - HEAD_DIM, 0) + c * (HEAD_DIM // 2)
    shared = tall[pl.ds(aligned(at, 8), HEAD_DIM // 2)]
    out[TALL:] = jnp.concatenate([shared, jnp.zeros((16, shared.shape[1]), F32)], 0).astype(BF)


def out_whole(ids, *refs):
    pieces, out, w16, held = refs[:8], refs[8], refs[9], refs[10]
    d = ids[3]
    part = held.shape[5]
    for r in range(8):
        owner = r ^ d
        core, quarter = owner >> 2, owner & 3
        out[pl.ds(aligned(272 * quarter + WINDOW * core, 16), TALL)] = pieces[r][:TALL]
        shared = pieces[r][TALL:].astype(F32)
        for t in range(3):
            for i in range(4):
                held[quarter, t, core, i] = shared[8 * t : 8 * t + 8, i * part : (i + 1) * part]
    for q in range(4):
        w16[:, q * part : (q + 1) * part] = held[q].reshape(3 * HEAD_DIM, part).astype(BF)


def lane_head(shape):
    return lax.broadcasted_iota(jnp.int32, shape, len(shape) - 1) < HEAD_DIM


def only_head(value, head):
    low = lane_head(value.shape)
    zero = jnp.zeros_like(value)
    return jnp.where(low, value, zero) if head == 0 else jnp.where(low, zero, value)


def softmax_down(scores, allowed):
    masked = jnp.where(allowed, scores, BLOCKED)
    weights = jnp.exp(masked - jnp.max(masked, axis=0, keepdims=True))
    return (weights * (1.0 / jnp.sum(weights, axis=0, keepdims=True))).astype(BF)


def causal_mask(shape, first):
    return lax.broadcasted_iota(jnp.int32, shape, 0) <= lax.broadcasted_iota(jnp.int32, shape, 1) + first


def segments_of(ids, mine, theirs):
    c, _, z, _ = place(ids)
    second = (z >> 1) == 1
    near = jnp.where(second, mine[1:2], mine[0:1])
    far = jnp.where(second, theirs[1:2], theirs[0:1])
    return jnp.where((z & 1) == c, near, far).astype(F32)


def upright(seg_row):
    return jnp.broadcast_to(seg_row, (8, seg_row.shape[1])).T[:, :1]


def attend(ids, *refs):
    n, refs = refs[:8], refs[8:]
    w, vectors, mine, theirs, n_abs, q_out, k_out, v_out, probs, att_abs = refs
    d = ids[3]
    rows = n_abs.shape[1]
    seq = 8 * rows
    for r in range(8):
        n_abs[r ^ d] = n[r][...]
    tokens = n_abs[...].reshape(seq, n_abs.shape[2])
    pair = aligned(d * PAIR, PAIR)
    projected = dot(tokens, w[...], ((1,), (1,)))
    q = (projected[:, :PAIR] + vectors[6:7, pl.ds(pair, PAIR)]).astype(BF) * BF(HEAD_DIM**-0.5)
    k = projected[:, PAIR : 2 * PAIR].astype(BF)
    v = (projected[:, 2 * PAIR :] + vectors[7:8, pl.ds(pair, PAIR)]).astype(BF)
    q_out[...] = q
    k_out[...] = k
    v_out[...] = v
    seg_row = segments_of(ids, mine, theirs)
    seg_col = upright(seg_row)
    v_t = v.astype(F32).T.astype(BF)
    keys = [only_head(k, h) for h in range(2)]
    step = 2 * rows
    for b in range(4):
        seen = (b + 1) * step
        at = slice(b * step, seen)
        allowed = (seg_col[:seen] == seg_row[:, at]) & causal_mask((seen, step), b * step)
        turned = []
        for h in range(2):
            p = softmax_down(dot(keys[h][:seen], q[at], ((1,), (1,))), allowed)
            probs[h, :seen, at] = p
            turned.append(dot(v_t[h * HEAD_DIM : (h + 1) * HEAD_DIM, :seen], p, ((1,), (0,))))
        attended = jnp.concatenate(turned, 0).T.astype(BF)
        att_abs[2 * b] = attended[:rows]
        att_abs[2 * b + 1] = attended[rows:]


def attend_shared(ids, n_abs, n_own, w16, vectors, mine, theirs, kv_out, qs_out, probs_s, att_s, seg_row):
    d = ids[3]
    rows, width = n_abs.shape[1], n_abs.shape[2]
    seq = 8 * rows
    w16_rows = w16[...]
    nothing = jnp.zeros((1, HEAD_DIM), F32)
    shared_v = jnp.concatenate([nothing, vectors[7:8, 8 * PAIR :]], 1)
    shared_q = vectors[6:7, 8 * PAIR :]
    kv = (dot(n_abs[...].reshape(seq, width), w16_rows[HEAD_DIM:], ((1,), (1,))) + shared_v).astype(BF)
    qs = (dot(n_own[...], w16_rows[:HEAD_DIM], ((1,), (1,))) + shared_q).astype(BF) * BF(HEAD_DIM**-0.5)
    qs = jnp.concatenate([qs, jnp.zeros_like(qs)], 1)
    kv_out[...] = kv
    qs_out[...] = qs
    first = aligned(d * rows, rows)
    seg_row[...] = segments_of(ids, mine, theirs)
    allowed = (upright(seg_row[...]) == seg_row[:, pl.ds(first, rows)]) & causal_mask((seq, rows), first)
    p = softmax_down(dot(only_head(kv, 0), qs, ((1,), (1,))), allowed)
    probs_s[...] = p
    kv_t = kv.astype(F32).T.astype(BF)
    att_s[...] = dot(kv_t[HEAD_DIM:], p, ((1,), (0,))).T.astype(BF)


def out_norm(ids, got, att_s, wo, x_own, vectors, middle, low):
    attended = jnp.concatenate([got[a] for a in range(8)] + [att_s[...]], 1)
    rows = x_own[...].astype(F32) + (dot(attended, wo[...], ((1,), (1,))) + vectors[4:5])
    middle[...] = rows
    low[...] = (normed(rows)[0] * vectors[2:3] + vectors[3:4]).astype(BF)


def weighted(sums, w):
    high = sums.astype(BF)
    low = (sums - high.astype(F32)).astype(BF)
    return dot(high, w, ((1,), (0,))) + dot(low, w, ((1,), (0,)))


def attend_back(ids, g_in, gs_in, q_in, k_in, v_in, kv_in, qs_in, probs, probs_s, w, w16, n_abs, *refs):
    grad_kv, grad_qs, sums, moments, near = refs[:5]
    far, windows, grads, grads_rel, tall = refs[5:9], refs[9:13], *refs[13:]
    d = ids[3]
    rows = g_in.shape[1]
    seq = 8 * rows
    g_all = g_in[...].reshape(seq, PAIR)
    g_s = gs_in[...]
    q, k, v, kv, qs = q_in[...], k_in[...], v_in[...], kv_in[...], qs_in[...]
    scale = HEAD_DIM**-0.5
    k_t = k.astype(F32).T.astype(BF)
    values = [only_head(v, h) for h in range(2)]
    step = 2 * rows
    grad_q = []
    grad_k = [[jnp.zeros((step, PAIR), F32) for _ in range(4)] for _ in range(2)]
    grad_v = [[jnp.zeros((step, PAIR), F32) for _ in range(4)] for _ in range(2)]
    for b in range(4):
        seen = (b + 1) * step
        at = slice(b * step, seen)
        turned = []
        for h in range(2):
            p_low = probs[h, :seen, at]
            p = p_low.astype(F32)
            gp = dot(values[h][:seen], g_all[at], ((1,), (1,)))
            inner = jnp.sum(p * gp, axis=0, keepdims=True)
            gs = (p * (gp - inner)).astype(BF)
            turned.append(dot(k_t[h * HEAD_DIM : (h + 1) * HEAD_DIM, :seen], gs, ((1,), (0,))) * scale)
            dk = dot(gs, q[at], ((1,), (0,)))
            dv = dot(p_low, g_all[at], ((1,), (0,)))
            for i in range(b + 1):
                grad_k[h][i] = grad_k[h][i] + dk[i * step : (i + 1) * step]
                grad_v[h][i] = grad_v[h][i] + dv[i * step : (i + 1) * step]
        grad_q.append(jnp.concatenate(turned, 0).T)
    low = lane_head((step, PAIR))
    qsum = jnp.zeros((1, PAIR), F32)
    ksum = jnp.zeros((1, PAIR), F32)
    vsum = jnp.zeros((1, PAIR), F32)
    for i in range(4):
        dq = grad_q[i].astype(BF)
        dk = jnp.where(low, grad_k[0][i], grad_k[1][i]).astype(BF)
        dv = jnp.where(low, grad_v[0][i], grad_v[1][i]).astype(BF)
        qsum = qsum + column_sum(dq.astype(F32))
        ksum = ksum + column_sum(dk.astype(F32))
        vsum = vsum + column_sum(dv.astype(F32))
        for j in range(2):
            part = slice(j * rows, (j + 1) * rows)
            grads[2 * i + j, :, :PAIR] = dq[part]
            grads[2 * i + j, :, PAIR : 2 * PAIR] = dk[part]
            grads[2 * i + j, :, 2 * PAIR : 3 * PAIR] = dv[part]

    p_low = probs_s[...]
    p = p_low.astype(F32)
    v_s = jnp.concatenate([kv[:, HEAD_DIM:], jnp.zeros((seq, HEAD_DIM), BF)], 1)
    g_pad = jnp.concatenate([g_s, jnp.zeros((rows, HEAD_DIM), BF)], 1)
    gp = dot(v_s, g_pad, ((1,), (1,)))
    inner = jnp.sum(p * gp, axis=0, keepdims=True)
    gs = (p * (gp - inner)).astype(BF)
    kv_t = kv.astype(F32).T.astype(BF)
    dq = (dot(kv_t[:HEAD_DIM], gs, ((1,), (0,))) * scale).T.astype(BF)
    grad_qs[...] = dq
    dk = dot(gs, qs, ((1,), (0,)))[:, :HEAD_DIM]
    dv = dot(p_low, g_pad, ((1,), (0,)))[:, :HEAD_DIM]
    dkv = jnp.concatenate([dk, dv], 1).astype(BF)
    for r in range(8):
        grads[r, :, 3 * PAIR :] = dkv[r * rows : (r + 1) * rows]
    last = jnp.concatenate([column_sum(dq.astype(F32)), column_sum(dv.astype(BF).astype(F32))], 1)
    sums[...] = jnp.concatenate([qsum, vsum, last, jnp.zeros((5, PAIR), F32)], 0)

    grad_kv[...] = dkv
    joined = jnp.concatenate([w[...], w16[HEAD_DIM:]], 0)
    for r in range(8):
        grads_rel[r] = grads[r ^ d]
    out = dot(grads_rel[4:].reshape(4 * rows, 4 * PAIR), joined, ((1,), (0,)))
    for k, ref in enumerate(far):
        ref[...] = out[k * rows : (k + 1) * rows].astype(BF)

    width = n_abs.shape[2]
    tokens = n_abs[...].reshape(seq, width)
    pairs = dot(grads[:, :, : 3 * PAIR].reshape(seq, 3 * PAIR), tokens, ((0,), (0,)))
    tall[: 3 * PAIR] = pairs
    tall[3 * PAIR :] = jnp.zeros((WINDOW, width), F32)
    z = ids[2]
    line = lax.broadcasted_iota(jnp.int32, (WINDOW, width), 0)
    for s, ref in enumerate(windows):
        _, length, filled = run_of(ids, d, (z + s) & 3)
        window = tall[pl.ds(aligned(filled, 16), WINDOW)]
        ref[...] = jnp.where(line < length, window, 0.0).astype(BF)
    pair_sums = jnp.concatenate([qsum, ksum, vsum], 1)
    moments[...] = jnp.concatenate(
        [column_sum(pairs * w[...].astype(F32)), weighted(jnp.broadcast_to(pair_sums, (8, 3 * PAIR)), w[...])[:1]], 0
    )

    out = dot(grads_rel[:4].reshape(4 * rows, 4 * PAIR), joined, ((1,), (0,)))
    near[...] = out.astype(BF)
    near[:rows] = (out[:rows] + dot(dq, w16[:HEAD_DIM], ((1,), (0,)))).astype(BF)


def out_grads(ids, *refs):
    gb, att_abs, att_s, grad_kv, grad_qs, n_abs, n_own, w16, out, moments, gb_abs = refs[:8], *refs[8:]
    d = ids[3]
    rows, width = gb_abs.shape[1], gb_abs.shape[2]
    seq = 8 * rows
    for r in range(8):
        gb_abs[r ^ d] = gb[r][...]
    pair = dot(att_abs[...].reshape(seq, PAIR), gb_abs[...].reshape(seq, width), ((0,), (0,)))
    shared = dot(att_s[...], gb[0][...], ((0,), (0,)))
    q_part = dot(grad_qs[...], n_own[...], ((0,), (0,)))
    kv_part = dot(grad_kv[...], n_abs[...].reshape(seq, width), ((0,), (0,)))
    projections = jnp.concatenate([q_part, kv_part], 0)
    sums = jnp.concatenate([column_sum(grad_qs[...].astype(F32)), column_sum(grad_kv[...].astype(F32))], 1)
    moments[...] = jnp.concatenate(
        [
            column_sum(projections * w16[...].astype(F32)),
            weighted(jnp.broadcast_to(sums, (8, 3 * HEAD_DIM)), w16[...])[:1],
        ],
        0,
    )
    tall = jnp.concatenate([pair, shared, projections], 0).T
    part = out.shape[1]
    for core in range(2):
        for quarter in range(4):
            at = slice((2 * quarter + core) * part, (2 * quarter + core + 1) * part)
            out[core * 4 + quarter] = tall[at].astype(BF)


def add_far(ids, near, f0, f1, f2, f3, s0, s1, s2, s3):
    rows = s0.shape[0]
    for k, (far, ref) in enumerate(((f0, s0), (f1, s1), (f2, s2), (f3, s3))):
        ref[...] = (near[k * rows : (k + 1) * rows].astype(F32) + far[...].astype(F32)).astype(ref.dtype)


def total_of(s0, r1, r2, r3):
    return s0[...] + r1[...].astype(F32) + r2[...].astype(F32) + r3[...].astype(F32)


def middle_back(ids, s0, r1, r2, r3, middle, g_own, wo, vectors, grad_middle, low, sums, back, back_s):
    upstream = total_of(s0, r1, r2, r3)
    centered, inverse = normed(middle[...])
    g = g_own[...].astype(F32)
    grad = g + norm_pull(upstream, centered, inverse, vectors[2:3])
    grad_middle[...] = grad
    rounded = grad.astype(BF)
    low[...] = rounded
    attended = dot(rounded, wo[...], ((1,), (0,))).astype(BF)
    for a in range(8):
        back[a] = attended[:, a * PAIR : (a + 1) * PAIR]
    back_s[...] = attended[:, 8 * PAIR :]
    sums[...] = jnp.concatenate(
        [
            column_sum(rounded.astype(F32)),
            column_sum(upstream * centered),
            column_sum(upstream),
            column_sum(g),
        ],
        0,
    )


def split_features(ids, rows, held, outs, which):
    e = 2 * (ids[1] & 1) + (ids[2] >> 1)
    held[...] = rows.T.reshape(held.shape).astype(BF)
    for m in range(4):
        outs[m][which] = held[m ^ e]


def finish(ids, s0, r1, r2, r3, t0, u1, u2, u3, middle, grad_middle, x_own, vectors, *refs):
    outs, held = refs[:4], refs[4]
    rows = middle[...] + (total_of(t0, u1, u2, u3) + vectors[5:6])
    split_features(ids, rows, held, outs, 0)
    upstream = total_of(s0, r1, r2, r3)
    centered, inverse = normed(x_own[...].astype(F32))
    rows = grad_middle[...] + norm_pull(upstream, centered, inverse, vectors[0:1])
    split_features(ids, rows, held, outs, 1)


def grad_activated(ids, *refs):
    g, down, g_rel, out = refs[:8], refs[8], refs[9], refs[10]
    rows = g_rel.shape[1]
    for r in range(8):
        g_rel[r] = g[r][...]
    for b in range(4):
        block = g_rel[2 * b : 2 * b + 2].reshape(2 * rows, g_rel.shape[2])
        out[b * 2 * rows : (b + 1) * 2 * rows] = dot(block, down[...], ((1,), (1,)))


def feed_forward(ids, *refs):
    n, refs = refs[:8], refs[8:]
    up, grad_act, bias, n_rel, act, grad_pre, bias_sum = refs[:7]
    far, near = refs[7:11], refs[11]
    rows = n_rel.shape[1]
    for r in range(8):
        n_rel[r] = n[r][...]
    total = jnp.zeros(bias_sum.shape, F32)
    for b in (2, 3, 0, 1):
        at = slice(b * 2 * rows, (b + 1) * 2 * rows)
        block = n_rel[2 * b : 2 * b + 2].reshape(2 * rows, n_rel.shape[2])
        pre = dot(block, up[...], ((1,), (1,))) + bias[...]
        square = pre * pre
        bent = jnp.tanh(ROOT * pre * (1.0 + 0.044715 * square))
        half = 0.5 * (1.0 + bent)
        act[at] = (pre * half).astype(BF)
        slope = half + 0.5 * pre * (1.0 - bent * bent) * (ROOT + ROOT * 3.0 * 0.044715 * square)
        low = (grad_act[at] * slope).astype(BF)
        grad_pre[at] = low
        total = total + column_sum(low.astype(F32))
        out = dot(low, up[...], ((1,), (0,))).astype(BF)
        if b >= 2:
            far[2 * b - 4][...] = out[:rows]
            far[2 * b - 3][...] = out[rows:]
        else:
            near[2 * rows * b : 2 * rows * (b + 1)] = out
    bias_sum[...] = total


def feed_out(ids, act, down, *refs):
    far, near = refs[:4], refs[4]
    half = near.shape[0]
    out = dot(act[half:], down[...], ((1,), (0,))).astype(BF)
    rows = half // 4
    for k, ref in enumerate(far):
        ref[...] = out[k * rows : (k + 1) * rows]
    near[...] = dot(act[:half], down[...], ((1,), (0,))).astype(BF)


def mlp_grads(ids, act, grad_pre, n_rel, g_rel, out):
    rows, width = n_rel.shape[1], n_rel.shape[2]
    part = out.shape[2]
    up = dot(grad_pre[...], n_rel[...].reshape(8 * rows, width), ((0,), (0,)))
    for i in range(4):
        out[i, 0] = up[i * part : (i + 1) * part].astype(BF)
    down = dot(act[...], g_rel[...].reshape(8 * rows, width), ((0,), (0,)))
    for i in range(4):
        out[i, 1] = down[i * part : (i + 1) * part].astype(BF)


def mlp_lanes(ids, summed, o0, o1, o2, o3, held):
    g = ids[1]
    part = held.shape[3]
    for i in range(4):
        held[i] = summed[:, :, i * part : (i + 1) * part]
    for k, ref in enumerate((o0, o1, o2, o3)):
        ref[...] = held[g ^ k]


def mlp_land(ids, *refs):
    blocks, up, down, held = refs[:8], refs[8], refs[9], refs[10]
    d = ids[3]
    for r in range(8):
        held[r ^ d] = blocks[r][...].astype(F32)
    up[...] = held[:, 0].reshape(-1, held.shape[3]).T
    down[...] = held[:, 1].reshape(-1, held.shape[3]).T


def qkv_lanes(ids, b0, b1, b2, b3, o0, o1, o2, o3, held):
    g = ids[1]
    part = held.shape[2]
    window = sum(ref[...].astype(F32) for ref in (b0, b1, b2, b3))
    for i in range(4):
        held[i] = window[:, i * part : (i + 1) * part].astype(BF)
    for k, ref in enumerate((o0, o1, o2, o3)):
        ref[...] = held[g ^ k]


def qkv_land(ids, *refs):
    blocks, mine, theirs, out, tall, held = refs[:8], *refs[8:]
    c, g, z, d = place(ids)
    tall[...] = jnp.zeros(tall.shape, F32)
    for r in range(8):
        start, _, _ = run_of(ids, r ^ d, z)
        at = pl.ds(aligned(start, 16), WINDOW)
        tall[at] = tall[at] + blocks[r][...].astype(F32)
    held[c] = mine[:, 272:].astype(F32)
    held[1 - c] = theirs[:, 272:].astype(F32)
    shared = held[...].reshape(-1, HEAD_DIM).T
    keep = jnp.where(z > 0, 1.0, 0.0)
    at = pl.ds(aligned(jnp.maximum(272 * z - HEAD_DIM, 0), 8), HEAD_DIM)
    tall[at] = tall[at] + shared * keep
    out[...] = tall[: out.shape[1]].T


def out_split(ids, got, o0, o1, o2, o3, wide, held):
    z = ids[2]
    part = wide.shape[1] // 4
    shared = jnp.zeros((got.shape[1], 4 * HEAD_DIM), F32)
    for a in range(8):
        wide[:, a * PAIR : (a + 1) * PAIR] = got[a, :, :PAIR].astype(F32)
        shared = shared + got[a, :, PAIR:].astype(F32)
    wide[:, 8 * PAIR :] = shared[:, :HEAD_DIM]
    for i in range(4):
        at = max(i, 1) * HEAD_DIM
        held[i] = jnp.concatenate(
            [wide[:, i * part : (i + 1) * part], shared[:, at : at + HEAD_DIM]], 1
        ).astype(BF)
    for s, ref in enumerate((o0, o1, o2, o3)):
        ref[...] = held[(z + s) & 3]


def sum_four(ids, b0, b1, b2, b3, out):
    out[...] = sum(ref[...].astype(F32) for ref in (b0, b1, b2, b3)).astype(BF)


def out_land(ids, mine, theirs, out, held):
    c = ids[0]
    held[c] = mine[:, :272].astype(F32)
    held[1 - c] = theirs[:, :272].astype(F32)
    out[...] = held[...].reshape(-1, held.shape[2]).T


def join_sums(ids, first, second, qkv, middle, up, out):
    d = ids[3]
    out[:2] = first[...] + second[...]
    out[2:4] = jnp.zeros((2, out.shape[1]), F32)
    at = pl.ds(aligned(d * PAIR, PAIR), PAIR)
    out[2:3, at] = qkv[0:1]
    out[3:4, at] = qkv[1:2]
    out[2:3, 8 * PAIR :] = qkv[2:3, :HEAD_DIM]
    out[3:4, 8 * PAIR :] = qkv[2:3, HEAD_DIM:]
    out[4:8] = middle[...]
    part = up.shape[1] // 4
    for i in range(4):
        piece = up[:, i * part : (i + 1) * part]
        out[8 + i : 9 + i] = jnp.concatenate([jnp.where(d == a, piece, 0.0) for a in range(8)], 1)


def keep(ids, *refs):
    count = len(refs) // 2
    for source, target in zip(refs[:count], refs[count:], strict=True):
        target[...] = source[...]


def add_two(ids, a, b, out):
    out[...] = a[...] + b[...]


def split_sums(ids, a, b, vectors, out):
    total = a[...] + b[...]
    out[...] = total
    out[0:1] = (total[0:1] - vectors[1:2] * total[1:2]) / vectors[0:1]


def shards(
    hidden_in,
    segment_ids,
    cotangent,
    norm1_gain,
    norm1_shift,
    w_qkv,
    q_bias,
    v_bias,
    w_out,
    out_bias,
    norm2_gain,
    norm2_shift,
    w_up,
    up_bias,
    w_down,
    down_bias,
):
    c = lax.axis_index("c")
    g = lax.axis_index("gx")
    z = lax.axis_index("gy")
    d = c * 4 + g
    width = norm1_gain.shape[0]
    hidden = up_bias.shape[0]
    quarter = hidden_in.shape[2]
    half = quarter // 2
    part = hidden // 32
    own_hidden = hidden // 8
    cols = w_qkv.shape[1]
    seq = segment_ids.shape[1]
    rows = seq // 8
    outer = lax.axis_size("do") > 1
    ids = jnp.concatenate(
        [jnp.stack([c, g, z, d]).astype(jnp.int32), jnp.asarray(run_table(width, cols))]
    )
    vectors = jnp.stack(
        [norm1_gain, norm1_shift, norm2_gain, norm2_shift, out_bias, down_bias, q_bias, v_bias]
    ).astype(F32)

    def row(vector):
        return vector.reshape(1, -1)

    def over_outer(value):
        return lax.psum(value, "do") if outer else value

    block = ((2, quarter, rows), BF)
    own_bf, own_f32 = ((rows, width), BF), ((rows, width), F32)
    held_tokens = ((4, quarter, rows), BF)

    def peers(blocks):
        return [blocks[0]] + [from_peer(blocks[k], k) for k in range(1, 4)]

    def gather_near(own):
        return [own] + [from_peer(own, k) for k in range(1, 4)]

    def gather_later(near, after):
        held = kernel(keep, [(a.shape, a.dtype) for a in near], [], ids, *near, us=0.8, after=after)
        return near + [swap_core(piece) for piece in held]

    def shifted(blocks):
        return [blocks[0]] + [from_below(blocks[s], s) for s in range(1, 4)]

    sent = kernel(
        send_tokens, [block] * 4, [], ids, hidden_in.transpose(0, 2, 1), cotangent.transpose(0, 2, 1), us=1.0
    )
    blocks = [lax.ppermute(sent[m], EVERY, MOVES[m]) for m in range(4)]
    window = ((WINDOW, quarter), BF)
    window_wide = ((WINDOW, width), BF)
    windows = peers(
        kernel(
            qkv_windows, [window] * 4, [((cols + WINDOW, quarter), F32)], ids, w_qkv, us=1.5, after=(sent[0],)
        )
    )
    lines = TALL + 3 * 16
    out_piece = kernel(
        out_half, [((lines, quarter), BF)], [((cols, quarter), F32)], ids, w_out, w_qkv, us=1.0, after=(sent[0],)
    )
    x_own, n1_own = kernel(take_normed, [own_bf, own_bf], [held_tokens], ids, *blocks, vectors, us=1.5)
    n1 = gather_plane(n1_own)
    piece = ((WINDOW + lines // 4, width), BF)
    joined = kernel(join_lanes, [piece], [((4, WINDOW, quarter), BF)], ids, *windows, out_piece, us=1.0)
    joined = shifted([joined] * 4)
    *mlp_sent, up_bias_own = kernel(
        mlp_blocks,
        [((2, part, quarter), BF)] * 4 + [((1, own_hidden), F32)],
        [((2, 8, part, quarter), F32)],
        ids,
        w_up,
        w_down.T,
        up_bias.astype(F32).reshape(4, 8, part),
        us=2.0,
        after=(joined[0], n1[1], n1[2], n1[3]),
    )
    mlp_got = peers(mlp_sent)
    g_own = kernel(
        take_tokens, [own_bf], [held_tokens], ids, *blocks, us=1.0, after=(n1[1], n1[2], n1[3])
    )
    g_near = gather_near(g_own)
    w_own, out_row = kernel(
        qkv_assemble,
        [((3 * PAIR, width), BF), ((TALL + 32, width), BF)],
        [((4, *piece[0]), BF), ((3 * PAIR + WINDOW, width), BF)],
        ids,
        *joined,
        us=1.0,
        after=(*g_near[1:], *mlp_got[1:]),
    )
    up_part, down_part = kernel(
        mlp_join,
        [((part, width), BF)] * 2,
        [((4, 2, part, quarter), BF)],
        ids,
        *mlp_got,
        us=1.0,
        after=(w_own,),
    )
    up_own = lax.all_gather(up_part, "gy", axis=0, tiled=False).reshape(own_hidden, width)
    down_own = lax.all_gather(down_part, "gy", axis=0, tiled=False).reshape(own_hidden, width)
    swapped_ids = swap_core(segment_ids)

    half_rows = ((4 * rows, width), BF)
    all_bf = ((8, rows, width), BF)
    heads_bf = ((8, rows, PAIR), BF)
    pair_seq = ((seq, PAIR), BF)
    n_abs, q, k, v, probs, att = kernel(
        attend,
        [all_bf, pair_seq, pair_seq, pair_seq, ((2, seq, seq), BF), heads_bf],
        [],
        ids,
        *n1,
        w_own,
        vectors,
        segment_ids,
        swapped_ids,
        us=11.0,
        far=True,
    )
    out_rows = gather_later(gather_near(out_row), (att,))
    att_got = lax.all_to_all(att, PLANE, split_axis=0, concat_axis=0, tiled=True)
    wo, w16 = kernel(
        out_whole,
        [((width, width), BF), ((3 * HEAD_DIM, width), BF)],
        [((4, 3, 2, 4, 8, quarter), F32)],
        ids,
        *out_rows,
        us=1.0,
        after=(att_got,),
    )
    kv, qs, probs_s, att_s = kernel(
        attend_shared,
        [pair_seq, ((rows, PAIR), BF), ((seq, rows), BF), ((rows, HEAD_DIM), BF)],
        [((1, seq), F32)],
        ids,
        n_abs,
        n1_own,
        w16,
        vectors,
        segment_ids,
        swapped_ids,
        us=2.0,
        work=6,
    )
    middle, n2_own = kernel(
        out_norm, [own_f32, own_bf], [], ids, att_got, att_s, wo, x_own, vectors, us=2.0, work=6
    )
    g_all = gather_later(g_near, (n2_own,))
    summed = [own_f32, own_bf, own_bf, own_bf]

    def scatter(near, far, after=()):
        return peers(
            kernel(add_far, summed, [], ids, near, *[swap_core(f) for f in far], us=1.2, after=after)
        )

    n2 = gather_plane(n2_own)

    g_rel, grad_act = kernel(
        grad_activated, [all_bf, ((seq, own_hidden), F32)], [], ids, *g_all, down_own, us=3.0, after=(n2_own, up_own)
    )
    n_rel, act, grad_pre, up_sum, *far, near = kernel(
        feed_forward,
        [
            all_bf,
            ((seq, own_hidden), BF),
            ((seq, own_hidden), BF),
            ((1, own_hidden), F32),
            *[own_bf] * 4,
            half_rows,
        ],
        [],
        ids,
        *n2,
        up_own,
        grad_act,
        up_bias_own,
        us=7.0,
        work=8,
    )
    parts = scatter(near, far)
    mlp_partial = kernel(
        mlp_grads,
        [((4, 2, part, width), BF)],
        [],
        ids,
        act,
        grad_pre,
        n_rel,
        g_rel,
        us=5.0,
        work=8,
        after=(parts[0],),
    )
    *feed_far, feed_near = kernel(
        feed_out, [own_bf] * 4 + [half_rows], [], ids, act, down_own, us=2.5, work=4, after=(mlp_partial,)
    )
    mlp_summed = over_outer(lax.psum_scatter(mlp_partial, "gy", scatter_dimension=0, tiled=False))
    grad_middle, gb_own, middle_sums, back, back_s = kernel(
        middle_back,
        [own_f32, own_bf, ((4, width), F32), heads_bf, ((rows, HEAD_DIM), BF)],
        [],
        ids,
        *parts,
        middle,
        g_own,
        wo,
        vectors,
        us=2.5,
        work=6,
        after=(mlp_partial,),
    )
    back = lax.all_to_all(back, PLANE, split_axis=0, concat_axis=0, tiled=True)
    gb = gather_plane(gb_own)

    feed_parts = scatter(feed_near, feed_far, (back,))

    grad_kv, grad_qs, qkv_sums, moments, near, *rest = kernel(
        attend_back,
        [pair_seq, ((rows, HEAD_DIM), BF), ((8, PAIR), F32), ((2, width), F32), half_rows]
        + [own_bf] * 4
        + [window_wide] * 4,
        [
            ((8, rows, 4 * PAIR), BF),
            ((8, rows, 4 * PAIR), BF),
            ((3 * PAIR + WINDOW, width), F32),
        ],
        ids,
        back,
        back_s,
        q,
        k,
        v,
        kv,
        qs,
        probs,
        probs_s,
        w_own,
        w16,
        n_abs,
        us=13.0,
        far=True,
        after=(feed_parts[0],),
    )
    far = rest[:4]
    windows = shifted(rest[4:])
    parts = scatter(near, far)
    out_sent, moments_s = kernel(
        out_grads,
        [((8, half, PAIR + 4 * HEAD_DIM), BF), ((2, width), F32)],
        [all_bf],
        ids,
        *gb,
        att,
        att_s,
        grad_kv,
        grad_qs,
        n_abs,
        n1_own,
        w16,
        us=3.5,
        work=10,
        after=tuple(parts[1:]),
    )
    out_got = lax.all_to_all(out_sent, PLANE, split_axis=0, concat_axis=0, tiled=True)
    mlp_parts = kernel(
        mlp_lanes,
        [((2, part, quarter), BF)] * 4,
        [((4, 2, part, quarter), BF)],
        ids,
        mlp_summed,
        us=1.0,
    )
    split_piece = ((half, quarter + HEAD_DIM), BF)
    out_split_parts = shifted(
        kernel(
            out_split,
            [split_piece] * 4,
            [((half, width), F32), ((4, half, quarter + HEAD_DIM), BF)],
            ids,
            out_got,
            us=1.0,
        )
    )
    done = kernel(
        finish,
        [block] * 4,
        [held_tokens],
        ids,
        *parts,
        *feed_parts,
        middle,
        grad_middle,
        x_own,
        vectors,
        us=2.5,
    )
    landed = [lax.ppermute(done[m], EVERY, BACK[m]) for m in range(4)]
    hidden_out, grad_in = kernel(land_tokens, [((2, quarter, 2 * rows), BF)] * 2, [], ids, *landed, us=1.0)

    smalls = kernel(
        join_sums, [((12, width), F32)], [], ids, moments, moments_s, qkv_sums, middle_sums, up_sum, us=0.7
    )
    smalls = smalls + swap_core(smalls)
    smalls = smalls + from_peer(smalls, 1)
    others = from_peer(smalls, 2)
    blocks = peers(mlp_parts)
    lanes = kernel(
        qkv_lanes, [window] * 4, [((4, WINDOW, quarter), BF)], ids, *windows, us=1.0, after=(*landed, *blocks[1:], out_split_parts[0], others)
    )
    near = peers(lanes)
    near = [*near, *[swap_core(piece) for piece in near]]
    total_up, total_down = kernel(
        mlp_land,
        [((quarter, hidden // 4), F32)] * 2,
        [((8, 2, part, quarter), F32)],
        ids,
        *blocks,
        *[swap_core(piece) for piece in blocks],
        us=2.0,
        after=(lanes[0],),
    )
    mine = kernel(sum_four, [split_piece], [], ids, *out_split_parts, us=0.6, after=(lanes[0],))
    theirs = swap_core(mine)
    total_out = kernel(
        out_land, [((quarter, quarter), F32)], [((2, half, quarter), F32)], ids, mine, theirs, us=0.7
    )
    total_out = over_outer(total_out)

    total_qkv = kernel(
        qkv_land,
        [((quarter, cols), F32)],
        [((cols + WINDOW, quarter), F32), ((2, half, HEAD_DIM), F32)],
        ids,
        *near,
        mine,
        theirs,
        us=2.0,
    )
    total_qkv = over_outer(total_qkv)
    smalls = kernel(add_two, [((12, width), F32)], [], ids, smalls, others, us=0.7, after=(lanes[0],))
    smalls = smalls + lax.ppermute(smalls, "gy", [(i, i ^ 1) for i in range(4)])
    others = lax.ppermute(smalls, "gy", [(i, i ^ 2) for i in range(4)])
    smalls, others = over_outer(smalls), over_outer(others)
    smalls = kernel(split_sums, [((12, width), F32)], [], ids, smalls, others, vectors, us=0.7)


    return (
        hidden_out.transpose(0, 2, 1),
        grad_in.transpose(0, 2, 1),
        smalls[0],
        smalls[1],
        total_qkv,
        smalls[2],
        smalls[3],
        total_out,
        smalls[4],
        smalls[5],
        smalls[6],
        total_up,
        smalls[8:12].reshape(hidden),
        total_down.T,
        smalls[7],
    )


def solution(mesh):
    devices = mesh.devices
    split = Mesh(
        devices.reshape(devices.shape[0] // 2, 2, devices.shape[1], devices.shape[2]), ("do", "c", "gx", "gy")
    )
    stream = P(None, ("do", "c", "gy"), "gx")
    flat = P()
    tall = P("gx", "gy")
    wide = P("gy", "gx")
    grads = (flat, flat, tall, flat, flat, wide, flat, flat, flat, tall, flat, wide, flat)
    return jax.shard_map(
        shards,
        mesh=split,
        in_specs=(stream, P(None, ("do", "c")), stream, *grads),
        out_specs=(stream, stream, *grads),
        check_vma=False,
    )
```

profile of v0, /device:TPU:0, one launch (start us, length us, event | category | flops | bytes accessed | tf_op | source)
XLA Modules:
  0.0 352.5 jit_solution(6304889689037315543)
XLA Ops:
  10.5 4.1 %collective-permute-start.1 = (bf16[2,272,128]{2,1,0:T(8,128)(2,1)S(1)}, bf16[2,272,128]{2,1,0:T(8,128)(2,1)S(1)}, u32[]{:S(2)}, u32[]{:S(2)}) collective-permute-start(bf16[2,272,128]{2,1,0:T(8,128)(2,1)S(1)} %get-tuple-element.125), channel_id=1, source_target_pairs={{0,2},{1,10},{2,18},{3,26},{4,0},{5,8},{6,16},{7,24},{8,6},{9,14},... | collective-permute-start | bytes 417800 | tf_op jit(solution)/shard_map/ppermute | solution.py:780
  14.6 2.9 collective-permute-start.3
  19.3 5.0 %collective-permute-start.11 = (bf16[128,272]{1,0:T(8,128)(2,1)S(1)}, bf16[128,272]{1,0:T(8,128)(2,1)S(1)}, u32[]{:S(2)}, u32[]{:S(2)}) collective-permute-start(bf16[128,272]{1,0:T(8,128)(2,1)S(1)} %get-tuple-element.130), channel_id=1, source_target_pairs={{0,4},{4,0},{8,12},{12,8},{1,5},{5,1},{9,13},{13,9},{2,6},{6,2},{1... | collective-permute-start | bytes 208904 | tf_op jit(solution)/shard_map/ppermute | solution.py:62
  25.6 2.6 collective-permute-start.12
  29.2 3.0 collective-permute-start.6
  32.8 5.3 %collective-permute-done.12.refs_3_ = bf16[128,272]{1,0:T(8,128)(2,1)S(1)} collective-permute-done((bf16[128,272]{1,0:T(8,128)(2,1)S(1)}, bf16[128,272]{1,0:T(8,128)(2,1)S(1)}, u32[]{:S(2)}, u32[]{:S(2)}) %collective-permute-start.12) | collective-permute-done | bytes 69664 | tf_op jit(solution)/shard_map/ppermute | solution.py:62
  39.0 2.7 collective-permute-start.15
  41.7 2.6 collective-permute-start.14
  44.3 3.0 collective-permute-done.5.refs_6_.refs_3_
  48.5 1.6 collective-permute-start.20
  50.9 1.6 collective-permute-start.19
  53.3 24.7 %collective-permute-done.15.refs_3_ = bf16[176,1088]{1,0:T(8,128)(2,1)S(1)} collective-permute-done((bf16[176,1088]{1,0:T(8,128)(2,1)S(1)}, bf16[176,1088]{1,0:T(8,128)(2,1)S(1)}, u32[]{:S(2)}, u32[]{:S(2)}) %collective-permute-start.15) | collective-permute-done | bytes 383008 | tf_op jit(solution)/shard_map/ppermute | solution.py:66
  78.0 3.0 collective-permute-start.21
  81.0 1.5 collective-permute-start.22
  82.5 3.9 %collective-permute-done.21.refs_9_.refs_3_ = bf16[2,136,272]{2,1,0:T(8,128)(2,1)S(1)} collective-permute-done((bf16[2,136,272]{2,1,0:T(8,128)(2,1)S(1)}, bf16[2,136,272]{2,1,0:T(8,128)(2,1)S(1)}, u32[]{:S(2)}, u32[]{:S(2)}) %collective-permute-start.21) | collective-permute-done | bytes 148000 | tf_op jit(solution)/shard_map/ppermute | solution.py:62
  86.4 7.5 %collective-permute-done.22.refs_10_.refs_4_ = bf16[2,136,272]{2,1,0:T(8,128)(2,1)S(1)} collective-permute-done((bf16[2,136,272]{2,1,0:T(8,128)(2,1)S(1)}, bf16[2,136,272]{2,1,0:T(8,128)(2,1)S(1)}, u32[]{:S(2)}, u32[]{:S(2)}) %collective-permute-start.22) | collective-permute-done | bytes 148000 | tf_op jit(solution)/shard_map/ppermute | solution.py:62
  96.2 1.7 mlp_join.1
  98.1 1.7 collective-permute-start.25
  99.8 1.7 collective-permute-start.24
  101.6 10.3 %attend.1 = (bf16[8,128,1088]{2,1,0:T(8,128)(2,1)}, bf16[1024,128]{1,0:T(8,128)(2,1)}, bf16[1024,128]{1,0:T(8,128)(2,1)}, bf16[1024,128]{1,0:T(8,128)(2,1)}, bf1...) custom-call(s32[100]{0:T(128)} %copy-done.3, bf16[128,1088]{1,0:T(8,128)(2,1)} %copy-done.14, ...), custom_call_target="tpu_custom_call" | custom-call | flops 54999998464 | bytes 1100000 | tf_op jit(solution)/shard_map/attend/pallas_call | solution.py:44
  111.8 6.4 %collective-permute-done.25.refs_3_ = bf16[176,1088]{1,0:T(8,128)(2,1)S(1)} collective-permute-done((bf16[176,1088]{1,0:T(8,128)(2,1)S(1)}, bf16[176,1088]{1,0:T(8,128)(2,1)S(1)}, u32[]{:S(2)}, u32[]{:S(2)}) %collective-permute-start.25) | collective-permute-done | bytes 383008 | tf_op jit(solution)/shard_map/ppermute | solution.py:62
  118.2 1.8 keep.2
  121.1 3.4 all-to-all-start
  125.3 5.7 %all-to-all-done.refs_9_.refs_1_ = bf16[8,128,128]{2,1,0:T(8,128)(2,1)S(1)} async-done(((bf16[8,128,128]{2,1,0:T(8,128)(2,1)}), bf16[8,128,128]{2,1,0:T(8,128)(2,1)S(1)}, u32[]{:S(2)}, u32[]{:S(2)}) %all-to-all-start) | async-done | bytes 262176 | tf_op jit(solution)/shard_map/all_to_all | solution.py:853
  131.0 1.8 out_whole.1
  132.9 2.2 attend_shared.1
  137.1 1.7 out_norm.1
  139.8 1.4 collective-permute-start.32
  143.6 6.1 %collective-permute-done.33.refs_4_ = bf16[128,1088]{1,0:T(8,128)(2,1)S(1)} collective-permute-done((bf16[128,1088]{1,0:T(8,128)(2,1)S(1)}, bf16[128,1088]{1,0:T(8,128)(2,1)S(1)}, u32[]{:S(2)}, u32[]{:S(2)}) %collective-permute-start.33) | collective-permute-done | bytes 278560 | tf_op jit(solution)/shard_map/ppermute | solution.py:62
  149.7 4.9 %collective-permute-done.32.refs_3_ = bf16[128,1088]{1,0:T(8,128)(2,1)S(1)} collective-permute-done((bf16[128,1088]{1,0:T(8,128)(2,1)S(1)}, bf16[128,1088]{1,0:T(8,128)(2,1)S(1)}, u32[]{:S(2)}, u32[]{:S(2)}) %collective-permute-start.32) | collective-permute-done | bytes 278560 | tf_op jit(solution)/shard_map/ppermute | solution.py:62
  163.7 2.8 grad_activated.1
  166.6 6.5 %feed_forward.1 = (bf16[8,128,1088]{2,1,0:T(8,128)(2,1)S(1)}, bf16[1024,544]{1,0:T(8,128)(2,1)S(1)}, bf16[1024,544]{1,0:T(8,128)(2,1)S(1)}, f32[1,544]{1,0:T(1,1...) custom-call(s32[100]{0:T(128)S(1)} %copy-done.4, ...), custom_call_target="tpu_custom_call" | custom-call | flops 35000000512 | bytes 700000 | tf_op jit(solution)/shard_map/feed_forward/pallas_call | solution.py:44
  176.0 1.5 add_far.3
  177.5 1.5 collective-permute-start.46
  179.0 1.5 collective-permute-start.47
  181.0 16.4 %mlp_grads.1.refs_9_.refs_3_ = bf16[4,2,136,1088]{3,2,1,0:T(8,128)(2,1)} custom-call(s32[100]{0:T(128)S(1)} %copy-done.4, bf16[1024,544]{1,0:T(8,128)(2,1)S(1)} %get-tuple-element.168.refs_1_, bf16[1024,544]{1,0:T(8,128)(2,1)S(1)} %get-tuple-element.169.refs_2_, bf16[8,128,1088]{2,1,0:T(8,128)(2,1)S(1)} %get-tuple-element.170.refs_3_, ...), custom_call_target="tpu_custom_call" | custom-call | flops 24999999488 | bytes 500000 | tf_op jit(solution)/shard_map/mlp_grads/pallas_call | solution.py:44
  199.5 3.1 feed_out.1
  206.4 2.9 middle_back.1
  210.7 3.7 %all-to-all-start.1 = ((bf16[8,128,128]{2,1,0:T(8,128)(2,1)}), bf16[8,128,128]{2,1,0:T(8,128)(2,1)S(1)}, u32[]{:S(2)}, u32[]{:S(2)}) async-start(bf16[8,128,128]{2,1,0:T(8,128)(2,1)} %get-tuple-element.172), calls=%async_computation.1 | async-start | bytes 524288 | tf_op jit(solution)/shard_map/all_to_all | solution.py:944
  215.1 3.0 collective-permute-start.69
  226.2 13.9 %attend_back.1 = (bf16[1024,128]{1,0:T(8,128)(2,1)}, bf16[128,64]{1,0:T(8,128)(2,1)}, f32[8,128]{1,0:T(8,128)}, f32[2,1088]{1,0:T(2,128)}, bf16[512,1088]{1,0:T(...) custom-call(s32[100]{0:T(128)} %copy-done.3, ...), custom_call_target="tpu_custom_call" | custom-call | flops 65000001536 | bytes 1300000 | tf_op jit(solution)/shard_map/attend_back/pallas_call | solution.py:44
  252.0 4.0 %collective-permute-done.57.refs_2_.refs_16_ = bf16[128,1088]{1,0:T(8,128)(2,1)S(1)} collective-permute-done((bf16[128,1088]{1,0:T(8,128)(2,1)S(1)}, bf16[128,1088]{1,0:T(8,128)(2,1)S(1)}, u32[]{:S(2)}, u32[]{:S(2)}) %collective-permute-start.57) | collective-permute-done | bytes 278560 | tf_op jit(solution)/shard_map/ppermute | solution.py:62
  256.0 1.8 collective-permute-start.62
  257.8 5.6 %collective-permute-done.58.refs_3_.refs_17_ = bf16[128,1088]{1,0:T(8,128)(2,1)S(1)} collective-permute-done((bf16[128,1088]{1,0:T(8,128)(2,1)S(1)}, bf16[128,1088]{1,0:T(8,128)(2,1)S(1)}, u32[]{:S(2)}, u32[]{:S(2)}) %collective-permute-start.58) | collective-permute-done | bytes 278560 | tf_op jit(solution)/shard_map/ppermute | solution.py:62
  263.4 3.1 out_grads.1
  268.0 3.5 %all-to-all-start.2 = ((bf16[8,136,384]{2,1,0:T(8,128)(2,1)}), bf16[8,136,384]{2,1,0:T(8,128)(2,1)S(1)}, u32[]{:S(2)}, u32[]{:S(2)}) async-start(bf16[8,136,384]{2,1,0:T(8,128)(2,1)} %get-tuple-element.221), calls=%async_computation.3 | async-start | bytes 1671168 | tf_op jit(solution)/shard_map/all_to_all | solution.py:996
  272.8 2.6 collective-permute-start.79
  275.4 3.6 %collective-permute-start.75 = (f32[12,1088]{1,0:T(8,128)S(1)}, f32[12,1088]{1,0:T(8,128)S(1)}, u32[]{:S(2)}, u32[]{:S(2)}) collective-permute-start(f32[12,1088]{1,0:T(8,128)S(1)} %add.15), channel_id=1, source_target_pairs={{0,4},{4,0},{8,12},{12,8},{1,5},{5,1},{9,13},{13,9},{2,6},{6,2},{1... | collective-permute-start | bytes 156680 | tf_op jit(solution)/shard_map/ppermute | solution.py:62
  284.2 2.8 finish.1
  287.6 5.6 %collective-permute-start.64 = (bf16[2,272,128]{2,1,0:T(8,128)(2,1)}, bf16[2,272,128]{2,1,0:T(8,128)(2,1)S(1)}, u32[]{:S(2)}, u32[]{:S(2)}) collective-permute-start(bf16[2,272,128]{2,1,0:T(8,128)(2,1)} %get-tuple-element.201), channel_id=1, source_target_pairs={{2,0},{10,1},{18,2},{26,3},{0,4},{8,5},{16,6},{24,7},{6,8},{14,9},... | collective-permute-start | bytes 417800 | tf_op jit(solution)/shard_map/ppermute | solution.py:1029
  295.4 6.1 %collective-permute-start.66 = (bf16[2,272,128]{2,1,0:T(8,128)(2,1)}, bf16[2,272,128]{2,1,0:T(8,128)(2,1)}, u32[]{:S(2)}, u32[]{:S(2)}) collective-permute-start(bf16[2,272,128]{2,1,0:T(8,128)(2,1)} %get-tuple-element.203), channel_id=1, source_target_pairs={{6,0},{14,1},{22,2},{30,3},{4,4},{12,5},{20,6},{28,7},{2,8},{10,9}... | collective-permute-start | bytes 417800 | tf_op jit(solution)/shard_map/ppermute | solution.py:1029
  302.6 2.7 collective-permute-start.80
  305.9 2.0 collective-permute-start.81
  308.6 2.8 collective-permute-start.82
  312.9 6.2 %collective-permute-start.93 = (bf16[136,336]{1,0:T(8,128)(2,1)S(1)}, bf16[136,336]{1,0:T(8,128)(2,1)S(1)}, u32[]{:S(2)}, u32[]{:S(2)}) collective-permute-start(bf16[136,336]{1,0:T(8,128)(2,1)S(1)} %get-tuple-element.228), channel_id=1, source_target_pairs={{0,2},{1,3},{2,0},{3,1},{4,6},{5,7},{6,4},{7,5},{8,10},{9,11},{10,... | collective-permute-start | bytes 274184 | tf_op jit(solution)/shard_map/ppermute | solution.py:66
  320.5 2.1 collective-permute-start.83
  322.6 1.5 collective-permute-done.93.refs_3_
  325.9 1.8 land_tokens.1
  328.2 1.5 collective-permute-start.85
  330.3 1.4 collective-permute-start.87
  333.0 1.5 out_land.1
  334.6 1.8 collective-permute-done.86.refs_3_
  340.8 2.2 qkv_land.1
  343.0 2.8 mlp_land.1
  (396 shorter events, 85.9 us)
Async XLA Ops:
  7.2 150.7 %all-gather.5.cloned.1.call-start = ((), (), s32[]{:S(2)}) async-start(), calls=%async_computation.5 | async-start | bytes 1566720 | tf_op jit(solution)/shard_map/all_gather | solution.py:831
  10.5 15.0 %collective-permute-start.1 = (bf16[2,272,128]{2,1,0:T(8,128)(2,1)S(1)}, bf16[2,272,128]{2,1,0:T(8,128)(2,1)S(1)}, u32[]{:S(2)}, u32[]{:S(2)}) collective-permute-start(bf16[2,272,128]{2,1,0:T(8,128)(2,1)S(1)} %get-tuple-element.125), channel_id=1, source_target_pairs={{0,2},{1,10},{2,18},{3,26},{4,0},{5,8},{6,16},{7,24},{8,6},{9,14},... | collective-permute-start | bytes 417800 | tf_op jit(solution)/shard_map/ppermute | solution.py:780
  14.6 13.5 %collective-permute-start.2 = (bf16[2,272,128]{2,1,0:T(8,128)(2,1)S(1)}, bf16[2,272,128]{2,1,0:T(8,128)(2,1)S(1)}, u32[]{:S(2)}, u32[]{:S(2)}) collective-permute-start(bf16[2,272,128]{2,1,0:T(8,128)(2,1)S(1)} %get-tuple-element.126), channel_id=1, source_target_pairs={{0,4},{1,12},{2,20},{3,28},{4,6},{5,14},{6,22},{7,30},{8,0},{9,8},... | collective-permute-start | bytes 417800 | tf_op jit(solution)/shard_map/ppermute | solution.py:780
  14.6 13.5 %collective-permute-start.3 = (bf16[2,272,128]{2,1,0:T(8,128)(2,1)S(1)}, bf16[2,272,128]{2,1,0:T(8,128)(2,1)S(1)}, u32[]{:S(2)}, u32[]{:S(2)}) collective-permute-start(bf16[2,272,128]{2,1,0:T(8,128)(2,1)S(1)} %get-tuple-element.127), channel_id=1, source_target_pairs={{0,6},{1,14},{2,22},{3,30},{4,4},{5,12},{6,20},{7,28},{8,2},{9,10}... | collective-permute-start | bytes 417800 | tf_op jit(solution)/shard_map/ppermute | solution.py:780
  17.6 10.6 %collective-permute-start = (bf16[2,272,128]{2,1,0:T(8,128)(2,1)S(1)}, bf16[2,272,128]{2,1,0:T(8,128)(2,1)S(1)}, u32[]{:S(2)}, u32[]{:S(2)}) collective-permute-start(bf16[2,272,128]{2,1,0:T(8,128)(2,1)S(1)} %get-tuple-element.124.refs_2_.refs_3_), channel_id=1, source_target_pairs={{0,0},{1,8},{2,16},{3,24},{4,2},{5,10},{6,18},{7,26},{8,4},{9,12},... | collective-permute-start | bytes 417800 | tf_op jit(solution)/shard_map/ppermute | solution.py:780
  19.3 12.9 %collective-permute-start.11 = (bf16[128,272]{1,0:T(8,128)(2,1)S(1)}, bf16[128,272]{1,0:T(8,128)(2,1)S(1)}, u32[]{:S(2)}, u32[]{:S(2)}) collective-permute-start(bf16[128,272]{1,0:T(8,128)(2,1)S(1)} %get-tuple-element.130), channel_id=1, source_target_pairs={{0,4},{4,0},{8,12},{12,8},{1,5},{5,1},{9,13},{13,9},{2,6},{6,2},{1... | collective-permute-start | bytes 208904 | tf_op jit(solution)/shard_map/ppermute | solution.py:62
  25.6 12.5 %collective-permute-start.12 = (bf16[128,272]{1,0:T(8,128)(2,1)S(1)}, bf16[128,272]{1,0:T(8,128)(2,1)S(1)}, u32[]{:S(2)}, u32[]{:S(2)}) collective-permute-start(bf16[128,272]{1,0:T(8,128)(2,1)S(1)} %get-tuple-element.131), channel_id=1, source_target_pairs={{0,8},{4,12},{8,0},{12,4},{1,9},{5,13},{9,1},{13,5},{2,10},{6,14},... | collective-permute-start | bytes 208904 | tf_op jit(solution)/shard_map/ppermute | solution.py:62
  29.2 12.5 %collective-permute-start.6 = (bf16[128,1088]{1,0:T(8,128)(2,1)S(1)}, bf16[128,1088]{1,0:T(8,128)(2,1)S(1)}, u32[]{:S(2)}, u32[]{:S(2)}) collective-permute-start(bf16[128,1088]{1,0:T(8,128)(2,1)S(1)} %get-tuple-element.128.refs_1_.refs_2_.refs_14_), channel_id=1, source_target_pairs={{0,12},{4,8},{8,4},{12,0},{1,13},{5,9},{9,5},{13,1},{2,14},{6,10},... | collective-permute-start | bytes 835592 | tf_op jit(solution)/shard_map/ppermute | solution.py:62
  32.2 15.1 %collective-permute-start.5 = (bf16[128,1088]{1,0:T(8,128)(2,1)S(1)}, bf16[128,1088]{1,0:T(8,128)(2,1)S(1)}, u32[]{:S(2)}, u32[]{:S(2)}) collective-permute-start(bf16[128,1088]{1,0:T(8,128)(2,1)S(1)} %get-tuple-element.128.refs_1_.refs_2_.refs_14_), channel_id=1, source_target_pairs={{0,8},{4,12},{8,0},{12,4},{1,9},{5,13},{9,1},{13,5},{2,10},{6,14},... | collective-permute-start | bytes 835592 | tf_op jit(solution)/shard_map/ppermute | solution.py:62
  32.3 15.1 %collective-permute-start.4 = (bf16[128,1088]{1,0:T(8,128)(2,1)S(1)}, bf16[128,1088]{1,0:T(8,128)(2,1)S(1)}, u32[]{:S(2)}, u32[]{:S(2)}) collective-permute-start(bf16[128,1088]{1,0:T(8,128)(2,1)S(1)} %get-tuple-element.128.refs_1_.refs_2_.refs_14_), channel_id=1, source_target_pairs={{0,4},{4,0},{8,12},{12,8},{1,5},{5,1},{9,13},{13,9},{2,6},{6,2},{1... | collective-permute-start | bytes 835592 | tf_op jit(solution)/shard_map/ppermute | solution.py:62
  38.9 13.6 %collective-permute-start.16 = (bf16[176,1088]{1,0:T(8,128)(2,1)S(1)}, bf16[176,1088]{1,0:T(8,128)(2,1)S(1)}, u32[]{:S(2)}, u32[]{:S(2)}) collective-permute-start(bf16[176,1088]{1,0:T(8,128)(2,1)S(1)} %join_lanes.1.refs_4_.refs_1_), channel_id=1, source_target_pairs={{0,3},{1,0},{2,1},{3,2},{4,7},{5,4},{6,5},{7,6},{8,11},{9,8},{10,9... | collective-permute-start | bytes 1148936 | tf_op jit(solution)/shard_map/ppermute | solution.py:66
  39.0 38.9 %collective-permute-start.15 = (bf16[176,1088]{1,0:T(8,128)(2,1)S(1)}, bf16[176,1088]{1,0:T(8,128)(2,1)S(1)}, u32[]{:S(2)}, u32[]{:S(2)}) collective-permute-start(bf16[176,1088]{1,0:T(8,128)(2,1)S(1)} %join_lanes.1.refs_4_.refs_1_), channel_id=1, source_target_pairs={{0,2},{1,3},{2,0},{3,1},{4,6},{5,7},{6,4},{7,5},{8,10},{9,11},{10,... | collective-permute-start | bytes 1148936 | tf_op jit(solution)/shard_map/ppermute | solution.py:66
  41.7 36.3 %collective-permute-start.14 = (bf16[176,1088]{1,0:T(8,128)(2,1)S(1)}, bf16[176,1088]{1,0:T(8,128)(2,1)S(1)}, u32[]{:S(2)}, u32[]{:S(2)}) collective-permute-start(bf16[176,1088]{1,0:T(8,128)(2,1)S(1)} %join_lanes.1.refs_4_.refs_1_), channel_id=1, source_target_pairs={{0,1},{1,2},{2,3},{3,0},{4,5},{5,6},{6,7},{7,4},{8,9},{9,10},{10,1... | collective-permute-start | bytes 1148936 | tf_op jit(solution)/shard_map/ppermute | solution.py:66
  48.5 32.5 %collective-permute-start.20 = (bf16[2,136,272]{2,1,0:T(8,128)(2,1)S(1)}, bf16[2,136,272]{2,1,0:T(8,128)(2,1)S(1)}, u32[]{:S(2)}, u32[]{:S(2)}) collective-permute-start(bf16[2,136,272]{2,1,0:T(8,128)(2,1)S(1)} %get-tuple-element.133), channel_id=1, source_target_pairs={{0,4},{4,0},{8,12},{12,8},{1,5},{5,1},{9,13},{13,9},{2,6},{6,2},{1... | collective-permute-start | bytes 443912 | tf_op jit(solution)/shard_map/ppermute | solution.py:62
  50.9 43.0 %collective-permute-start.19 = (bf16[128,1088]{1,0:T(8,128)(2,1)S(1)}, bf16[128,1088]{1,0:T(8,128)(2,1)S(1)}, u32[]{:S(2)}, u32[]{:S(2)}) collective-permute-start(bf16[128,1088]{1,0:T(8,128)(2,1)S(1)} %take_tokens.1.refs_1_.refs_6_), channel_id=1, source_target_pairs={{0,12},{4,8},{8,4},{12,0},{1,13},{5,9},{9,5},{13,1},{2,14},{6,10},... | collective-permute-start | bytes 835592 | tf_op jit(solution)/shard_map/ppermute | solution.py:62
  52.5 41.9 %collective-permute-start.18 = (bf16[128,1088]{1,0:T(8,128)(2,1)S(1)}, bf16[128,1088]{1,0:T(8,128)(2,1)S(1)}, u32[]{:S(2)}, u32[]{:S(2)}) collective-permute-start(bf16[128,1088]{1,0:T(8,128)(2,1)S(1)} %take_tokens.1.refs_1_.refs_6_), channel_id=1, source_target_pairs={{0,8},{4,12},{8,0},{12,4},{1,9},{5,13},{9,1},{13,5},{2,10},{6,14},... | collective-permute-start | bytes 835592 | tf_op jit(solution)/shard_map/ppermute | solution.py:62
  78.0 16.6 %collective-permute-start.17 = (bf16[128,1088]{1,0:T(8,128)(2,1)S(1)}, bf16[128,1088]{1,0:T(8,128)(2,1)S(1)}, u32[]{:S(2)}, u32[]{:S(2)}) collective-permute-start(bf16[128,1088]{1,0:T(8,128)(2,1)S(1)} %take_tokens.1.refs_1_.refs_6_), channel_id=1, source_target_pairs={{0,4},{4,0},{8,12},{12,8},{1,5},{5,1},{9,13},{13,9},{2,6},{6,2},{1... | collective-permute-start | bytes 835592 | tf_op jit(solution)/shard_map/ppermute | solution.py:62
  81.0 12.9 %collective-permute-start.22 = (bf16[2,136,272]{2,1,0:T(8,128)(2,1)S(1)}, bf16[2,136,272]{2,1,0:T(8,128)(2,1)S(1)}, u32[]{:S(2)}, u32[]{:S(2)}) collective-permute-start(bf16[2,136,272]{2,1,0:T(8,128)(2,1)S(1)} %get-tuple-element.135), channel_id=1, source_target_pairs={{0,12},{4,8},{8,4},{12,0},{1,13},{5,9},{9,5},{13,1},{2,14},{6,10},... | collective-permute-start | bytes 443912 | tf_op jit(solution)/shard_map/ppermute | solution.py:62
  86.4 11.6 %collective-permute-start.23 = (s32[2,1024]{1,0:T(2,128)S(1)}, s32[2,1024]{1,0:T(2,128)S(1)}, u32[]{:S(2)}, u32[]{:S(2)}) collective-permute-start(s32[2,1024]{1,0:T(2,128)S(1)} %copy-done.47), channel_id=1, source_target_pairs={{0,16},{16,0},{1,17},{17,1},{2,18},{18,2},{3,19},{19,3},{4,20},{20... | collective-permute-start | bytes 24584 | tf_op jit(solution)/shard_map/ppermute | solution.py:58
  98.0 13.8 %collective-permute-start.26 = (bf16[176,1088]{1,0:T(8,128)(2,1)S(1)}, bf16[176,1088]{1,0:T(8,128)(2,1)S(1)}, u32[]{:S(2)}, u32[]{:S(2)}) collective-permute-start(bf16[176,1088]{1,0:T(8,128)(2,1)S(1)} %get-tuple-element.139.refs_1_), channel_id=1, source_target_pairs={{0,12},{4,8},{8,4},{12,0},{1,13},{5,9},{9,5},{13,1},{2,14},{6,10},... | collective-permute-start | bytes 1148936 | tf_op jit(solution)/shard_map/ppermute | solution.py:62
  98.1 20.1 %collective-permute-start.25 = (bf16[176,1088]{1,0:T(8,128)(2,1)S(1)}, bf16[176,1088]{1,0:T(8,128)(2,1)S(1)}, u32[]{:S(2)}, u32[]{:S(2)}) collective-permute-start(bf16[176,1088]{1,0:T(8,128)(2,1)S(1)} %get-tuple-element.139.refs_1_), channel_id=1, source_target_pairs={{0,8},{4,12},{8,0},{12,4},{1,9},{5,13},{9,1},{13,5},{2,10},{6,14},... | collective-permute-start | bytes 1148936 | tf_op jit(solution)/shard_map/ppermute | solution.py:62
  99.8 18.4 %collective-permute-start.24 = (bf16[176,1088]{1,0:T(8,128)(2,1)S(1)}, bf16[176,1088]{1,0:T(8,128)(2,1)S(1)}, u32[]{:S(2)}, u32[]{:S(2)}) collective-permute-start(bf16[176,1088]{1,0:T(8,128)(2,1)S(1)} %get-tuple-element.139.refs_1_), channel_id=1, source_target_pairs={{0,4},{4,0},{8,12},{12,8},{1,5},{5,1},{9,13},{13,9},{2,6},{6,2},{1... | collective-permute-start | bytes 1148936 | tf_op jit(solution)/shard_map/ppermute | solution.py:62
  120.0 10.9 %collective-permute-start.27 = (bf16[176,1088]{1,0:T(8,128)(2,1)}, bf16[176,1088]{1,0:T(8,128)(2,1)S(1)}, u32[]{:S(2)}, u32[]{:S(2)}) collective-permute-start(bf16[176,1088]{1,0:T(8,128)(2,1)} %get-tuple-element.140), channel_id=1, source_target_pairs={{0,16},{16,0},{1,17},{17,1},{2,18},{18,2},{3,19},{19,3},{4,20},{20... | collective-permute-start | bytes 1148936 | tf_op jit(solution)/shard_map/ppermute | solution.py:58
  120.0 10.9 %collective-permute-start.28 = (bf16[176,1088]{1,0:T(8,128)(2,1)}, bf16[176,1088]{1,0:T(8,128)(2,1)S(1)}, u32[]{:S(2)}, u32[]{:S(2)}) collective-permute-start(bf16[176,1088]{1,0:T(8,128)(2,1)} %get-tuple-element.141), channel_id=1, source_target_pairs={{0,16},{16,0},{1,17},{17,1},{2,18},{18,2},{3,19},{19,3},{4,20},{20... | collective-permute-start | bytes 1148936 | tf_op jit(solution)/shard_map/ppermute | solution.py:58
  124.5 33.8 %all-gather.7.cloned.1.call-start = ((), (), s32[]{:S(2)}) async-start(), calls=%async_computation.6 | async-start | bytes 1566720 | tf_op jit(solution)/shard_map/all_gather | solution.py:832
  138.8 10.9 %collective-permute-start.33 = (bf16[128,1088]{1,0:T(8,128)(2,1)S(1)}, bf16[128,1088]{1,0:T(8,128)(2,1)S(1)}, u32[]{:S(2)}, u32[]{:S(2)}) collective-permute-start(bf16[128,1088]{1,0:T(8,128)(2,1)S(1)} %get-tuple-element.148.refs_5_.refs_10_.refs_1_), channel_id=1, source_target_pairs={{0,12},{4,8},{8,4},{12,0},{1,13},{5,9},{9,5},{13,1},{2,14},{6,10},... | collective-permute-start | bytes 835592 | tf_op jit(solution)/shard_map/ppermute | solution.py:62
  139.8 14.8 %collective-permute-start.32 = (bf16[128,1088]{1,0:T(8,128)(2,1)S(1)}, bf16[128,1088]{1,0:T(8,128)(2,1)S(1)}, u32[]{:S(2)}, u32[]{:S(2)}) collective-permute-start(bf16[128,1088]{1,0:T(8,128)(2,1)S(1)} %get-tuple-element.148.refs_5_.refs_10_.refs_1_), channel_id=1, source_target_pairs={{0,8},{4,12},{8,0},{12,4},{1,9},{5,13},{9,1},{13,5},{2,10},{6,14},... | collective-permute-start | bytes 835592 | tf_op jit(solution)/shard_map/ppermute | solution.py:62
  141.2 13.4 %collective-permute-start.31 = (bf16[128,1088]{1,0:T(8,128)(2,1)S(1)}, bf16[128,1088]{1,0:T(8,128)(2,1)S(1)}, u32[]{:S(2)}, u32[]{:S(2)}) collective-permute-start(bf16[128,1088]{1,0:T(8,128)(2,1)S(1)} %get-tuple-element.148.refs_5_.refs_10_.refs_1_), channel_id=1, source_target_pairs={{0,4},{4,0},{8,12},{12,8},{1,5},{5,1},{9,13},{13,9},{2,6},{6,2},{1... | collective-permute-start | bytes 835592 | tf_op jit(solution)/shard_map/ppermute | solution.py:62
  143.1 12.1 %collective-permute-start.38 = (bf16[128,1088]{1,0:T(8,128)(2,1)S(1)}, bf16[128,1088]{1,0:T(8,128)(2,1)S(1)}, u32[]{:S(2)}, u32[]{:S(2)}) collective-permute-start(bf16[128,1088]{1,0:T(8,128)(2,1)S(1)} %get-tuple-element.151), channel_id=1, source_target_pairs={{0,16},{16,0},{1,17},{17,1},{2,18},{18,2},{3,19},{19,3},{4,20},{20... | collective-permute-start | bytes 835592 | tf_op jit(solution)/shard_map/ppermute | solution.py:58
  143.1 12.1 %collective-permute-start.39 = (bf16[128,1088]{1,0:T(8,128)(2,1)S(1)}, bf16[128,1088]{1,0:T(8,128)(2,1)S(1)}, u32[]{:S(2)}, u32[]{:S(2)}) collective-permute-start(bf16[128,1088]{1,0:T(8,128)(2,1)S(1)} %get-tuple-element.152), channel_id=1, source_target_pairs={{0,16},{16,0},{1,17},{17,1},{2,18},{18,2},{3,19},{19,3},{4,20},{20... | collective-permute-start | bytes 835592 | tf_op jit(solution)/shard_map/ppermute | solution.py:58
  154.6 11.9 %collective-permute-start.34 = (bf16[128,1088]{1,0:T(8,128)(2,1)S(1)}, bf16[128,1088]{1,0:T(8,128)(2,1)S(1)}, u32[]{:S(2)}, u32[]{:S(2)}) collective-permute-start(bf16[128,1088]{1,0:T(8,128)(2,1)S(1)} %get-tuple-element.148.refs_5_.refs_10_.refs_1_), channel_id=1, source_target_pairs={{0,16},{16,0},{1,17},{17,1},{2,18},{18,2},{3,19},{19,3},{4,20},{20... | collective-permute-start | bytes 835592 | tf_op jit(solution)/shard_map/ppermute | solution.py:58
  155.1 11.4 %collective-permute-start.37 = (bf16[128,1088]{1,0:T(8,128)(2,1)S(1)}, bf16[128,1088]{1,0:T(8,128)(2,1)}, u32[]{:S(2)}, u32[]{:S(2)}) collective-permute-start(bf16[128,1088]{1,0:T(8,128)(2,1)S(1)} %collective-permute-done.33.refs_4_), channel_id=1, source_target_pairs={{0,16},{16,0},{1,17},{17,1},{2,18},{18,2},{3,19},{19,3},{4,20},{20... | collective-permute-start | bytes 835592 | tf_op jit(solution)/shard_map/ppermute | solution.py:58
  155.9 10.6 %collective-permute-start.36 = (bf16[128,1088]{1,0:T(8,128)(2,1)S(1)}, bf16[128,1088]{1,0:T(8,128)(2,1)}, u32[]{:S(2)}, u32[]{:S(2)}) collective-permute-start(bf16[128,1088]{1,0:T(8,128)(2,1)S(1)} %collective-permute-done.32.refs_3_), channel_id=1, source_target_pairs={{0,16},{16,0},{1,17},{17,1},{2,18},{18,2},{3,19},{19,3},{4,20},{20... | collective-permute-start | bytes 835592 | tf_op jit(solution)/shard_map/ppermute | solution.py:58
  177.5 26.7 %collective-permute-start.46 = (bf16[128,1088]{1,0:T(8,128)(2,1)}, bf16[128,1088]{1,0:T(8,128)(2,1)S(1)}, u32[]{:S(2)}, u32[]{:S(2)}) collective-permute-start(bf16[128,1088]{1,0:T(8,128)(2,1)} %get-tuple-element.164), channel_id=1, source_target_pairs={{0,4},{4,0},{8,12},{12,8},{1,5},{5,1},{9,13},{13,9},{2,6},{6,2},{1... | collective-permute-start | bytes 835592 | tf_op jit(solution)/shard_map/ppermute | solution.py:62
  179.0 25.9 %collective-permute-start.47 = (bf16[128,1088]{1,0:T(8,128)(2,1)}, bf16[128,1088]{1,0:T(8,128)(2,1)}, u32[]{:S(2)}, u32[]{:S(2)}) collective-permute-start(bf16[128,1088]{1,0:T(8,128)(2,1)} %get-tuple-element.165), channel_id=1, source_target_pairs={{0,8},{4,12},{8,0},{12,4},{1,9},{5,13},{9,1},{13,5},{2,10},{6,14},... | collective-permute-start | bytes 835592 | tf_op jit(solution)/shard_map/ppermute | solution.py:62
  180.5 25.0 %collective-permute-start.48 = (bf16[128,1088]{1,0:T(8,128)(2,1)}, bf16[128,1088]{1,0:T(8,128)(2,1)}, u32[]{:S(2)}, u32[]{:S(2)}) collective-permute-start(bf16[128,1088]{1,0:T(8,128)(2,1)} %get-tuple-element.166), channel_id=1, source_target_pairs={{0,12},{4,8},{8,4},{12,0},{1,13},{5,9},{9,5},{13,1},{2,14},{6,10},... | collective-permute-start | bytes 835592 | tf_op jit(solution)/shard_map/ppermute | solution.py:62
  203.7 14.4 %collective-permute-start.49 = (bf16[128,1088]{1,0:T(8,128)(2,1)}, bf16[128,1088]{1,0:T(8,128)(2,1)S(1)}, u32[]{:S(2)}, u32[]{:S(2)}) collective-permute-start(bf16[128,1088]{1,0:T(8,128)(2,1)} %get-tuple-element.182), channel_id=1, source_target_pairs={{0,16},{16,0},{1,17},{17,1},{2,18},{18,2},{3,19},{19,3},{4,20},{20... | collective-permute-start | bytes 835592 | tf_op jit(solution)/shard_map/ppermute | solution.py:58
  203.7 15.0 %collective-permute-start.50 = (bf16[128,1088]{1,0:T(8,128)(2,1)}, bf16[128,1088]{1,0:T(8,128)(2,1)S(1)}, u32[]{:S(2)}, u32[]{:S(2)}) collective-permute-start(bf16[128,1088]{1,0:T(8,128)(2,1)} %get-tuple-element.183), channel_id=1, source_target_pairs={{0,16},{16,0},{1,17},{17,1},{2,18},{18,2},{3,19},{19,3},{4,20},{20... | collective-permute-start | bytes 835592 | tf_op jit(solution)/shard_map/ppermute | solution.py:58
  204.9 13.8 %collective-permute-start.51 = (bf16[128,1088]{1,0:T(8,128)(2,1)}, bf16[128,1088]{1,0:T(8,128)(2,1)S(1)}, u32[]{:S(2)}, u32[]{:S(2)}) collective-permute-start(bf16[128,1088]{1,0:T(8,128)(2,1)} %get-tuple-element.184), channel_id=1, source_target_pairs={{0,16},{16,0},{1,17},{17,1},{2,18},{18,2},{3,19},{19,3},{4,20},{20... | collective-permute-start | bytes 835592 | tf_op jit(solution)/shard_map/ppermute | solution.py:58
  204.9 14.6 %collective-permute-start.52 = (bf16[128,1088]{1,0:T(8,128)(2,1)S(1)}, bf16[128,1088]{1,0:T(8,128)(2,1)S(1)}, u32[]{:S(2)}, u32[]{:S(2)}) collective-permute-start(bf16[128,1088]{1,0:T(8,128)(2,1)S(1)} %get-tuple-element.185), channel_id=1, source_target_pairs={{0,16},{16,0},{1,17},{17,1},{2,18},{18,2},{3,19},{19,3},{4,20},{20... | collective-permute-start | bytes 835592 | tf_op jit(solution)/shard_map/ppermute | solution.py:58
  214.4 79.0 %reduce-scatter.2.cloned.1.call-start = ((), (), s32[]{:S(2)}) async-start(), calls=%async_computation.4 | async-start | bytes 3133440 | tf_op jit(solution)/shard_map/reduce_scatter | solution.py:929
  215.1 25.7 %collective-permute-start.69 = (bf16[128,1088]{1,0:T(8,128)(2,1)S(1)}, bf16[128,1088]{1,0:T(8,128)(2,1)S(1)}, u32[]{:S(2)}, u32[]{:S(2)}) collective-permute-start(bf16[128,1088]{1,0:T(8,128)(2,1)S(1)} %get-tuple-element.207.refs_1_), channel_id=1, source_target_pairs={{0,12},{4,8},{8,4},{12,0},{1,13},{5,9},{9,5},{13,1},{2,14},{6,10},... | collective-permute-start | bytes 835592 | tf_op jit(solution)/shard_map/ppermute | solution.py:62
  218.1 23.2 %collective-permute-start.68 = (bf16[128,1088]{1,0:T(8,128)(2,1)S(1)}, bf16[128,1088]{1,0:T(8,128)(2,1)S(1)}, u32[]{:S(2)}, u32[]{:S(2)}) collective-permute-start(bf16[128,1088]{1,0:T(8,128)(2,1)S(1)} %get-tuple-element.207.refs_1_), channel_id=1, source_target_pairs={{0,8},{4,12},{8,0},{12,4},{1,9},{5,13},{9,1},{13,5},{2,10},{6,14},... | collective-permute-start | bytes 835592 | tf_op jit(solution)/shard_map/ppermute | solution.py:62
  218.7 22.7 %collective-permute-start.67 = (bf16[128,1088]{1,0:T(8,128)(2,1)S(1)}, bf16[128,1088]{1,0:T(8,128)(2,1)S(1)}, u32[]{:S(2)}, u32[]{:S(2)}) collective-permute-start(bf16[128,1088]{1,0:T(8,128)(2,1)S(1)} %get-tuple-element.207.refs_1_), channel_id=1, source_target_pairs={{0,4},{4,0},{8,12},{12,8},{1,5},{5,1},{9,13},{13,9},{2,6},{6,2},{1... | collective-permute-start | bytes 835592 | tf_op jit(solution)/shard_map/ppermute | solution.py:62
  247.2 16.2 %collective-permute-start.58 = (bf16[128,1088]{1,0:T(8,128)(2,1)S(1)}, bf16[128,1088]{1,0:T(8,128)(2,1)S(1)}, u32[]{:S(2)}, u32[]{:S(2)}) collective-permute-start(bf16[128,1088]{1,0:T(8,128)(2,1)S(1)} %get-tuple-element.194), channel_id=1, source_target_pairs={{0,8},{4,12},{8,0},{12,4},{1,9},{5,13},{9,1},{13,5},{2,10},{6,14},... | collective-permute-start | bytes 835592 | tf_op jit(solution)/shard_map/ppermute | solution.py:62
  248.5 14.9 %collective-permute-start.59 = (bf16[128,1088]{1,0:T(8,128)(2,1)S(1)}, bf16[128,1088]{1,0:T(8,128)(2,1)S(1)}, u32[]{:S(2)}, u32[]{:S(2)}) collective-permute-start(bf16[128,1088]{1,0:T(8,128)(2,1)S(1)} %get-tuple-element.195), channel_id=1, source_target_pairs={{0,12},{4,8},{8,4},{12,0},{1,13},{5,9},{9,5},{13,1},{2,14},{6,10},... | collective-permute-start | bytes 835592 | tf_op jit(solution)/shard_map/ppermute | solution.py:62
  249.6 23.1 %collective-permute-start.60 = (bf16[128,1088]{1,0:T(8,128)(2,1)S(1)}, bf16[128,1088]{1,0:T(8,128)(2,1)}, u32[]{:S(2)}, u32[]{:S(2)}) collective-permute-start(bf16[128,1088]{1,0:T(8,128)(2,1)S(1)} %get-tuple-element.196), channel_id=1, source_target_pairs={{0,4},{4,0},{8,12},{12,8},{1,5},{5,1},{9,13},{13,9},{2,6},{6,2},{1... | collective-permute-start | bytes 835592 | tf_op jit(solution)/shard_map/ppermute | solution.py:62
  250.7 24.7 %collective-permute-start.61 = (bf16[128,1088]{1,0:T(8,128)(2,1)S(1)}, bf16[128,1088]{1,0:T(8,128)(2,1)}, u32[]{:S(2)}, u32[]{:S(2)}) collective-permute-start(bf16[128,1088]{1,0:T(8,128)(2,1)S(1)} %get-tuple-element.197), channel_id=1, source_target_pairs={{0,8},{4,12},{8,0},{12,4},{1,9},{5,13},{9,1},{13,5},{2,10},{6,14},... | collective-permute-start | bytes 835592 | tf_op jit(solution)/shard_map/ppermute | solution.py:62
  256.0 23.0 %collective-permute-start.62 = (bf16[128,1088]{1,0:T(8,128)(2,1)S(1)}, bf16[128,1088]{1,0:T(8,128)(2,1)}, u32[]{:S(2)}, u32[]{:S(2)}) collective-permute-start(bf16[128,1088]{1,0:T(8,128)(2,1)S(1)} %get-tuple-element.198), channel_id=1, source_target_pairs={{0,12},{4,8},{8,4},{12,0},{1,13},{5,9},{9,5},{13,1},{2,14},{6,10},... | collective-permute-start | bytes 835592 | tf_op jit(solution)/shard_map/ppermute | solution.py:62
  267.3 26.0 %collective-permute-start.77 = (bf16[128,1088]{1,0:T(8,128)(2,1)}, bf16[128,1088]{1,0:T(8,128)(2,1)S(1)}, u32[]{:S(2)}, u32[]{:S(2)}) collective-permute-start(bf16[128,1088]{1,0:T(8,128)(2,1)} %get-tuple-element.215), channel_id=1, source_target_pairs={{0,1},{1,2},{2,3},{3,0},{4,5},{5,6},{6,7},{7,4},{8,9},{9,10},{10,1... | collective-permute-start | bytes 835592 | tf_op jit(solution)/shard_map/ppermute | solution.py:66
  268.0 43.4 %all-to-all-start.2 = ((bf16[8,136,384]{2,1,0:T(8,128)(2,1)}), bf16[8,136,384]{2,1,0:T(8,128)(2,1)S(1)}, u32[]{:S(2)}, u32[]{:S(2)}) async-start(bf16[8,136,384]{2,1,0:T(8,128)(2,1)} %get-tuple-element.221), calls=%async_computation.3 | async-start | bytes 1671168 | tf_op jit(solution)/shard_map/all_to_all | solution.py:996
  271.6 23.8 %collective-permute-start.78 = (bf16[128,1088]{1,0:T(8,128)(2,1)}, bf16[128,1088]{1,0:T(8,128)(2,1)S(1)}, u32[]{:S(2)}, u32[]{:S(2)}) collective-permute-start(bf16[128,1088]{1,0:T(8,128)(2,1)} %get-tuple-element.216), channel_id=1, source_target_pairs={{0,2},{1,3},{2,0},{3,1},{4,6},{5,7},{6,4},{7,5},{8,10},{9,11},{10,... | collective-permute-start | bytes 835592 | tf_op jit(solution)/shard_map/ppermute | solution.py:66
  272.8 28.7 %collective-permute-start.79 = (bf16[128,1088]{1,0:T(8,128)(2,1)}, bf16[128,1088]{1,0:T(8,128)(2,1)S(1)}, u32[]{:S(2)}, u32[]{:S(2)}) collective-permute-start(bf16[128,1088]{1,0:T(8,128)(2,1)} %get-tuple-element.217), channel_id=1, source_target_pairs={{0,3},{1,0},{2,1},{3,2},{4,7},{5,4},{6,5},{7,6},{8,11},{9,8},{10,9... | collective-permute-start | bytes 835592 | tf_op jit(solution)/shard_map/ppermute | solution.py:66
  275.4 12.2 %collective-permute-start.75 = (f32[12,1088]{1,0:T(8,128)S(1)}, f32[12,1088]{1,0:T(8,128)S(1)}, u32[]{:S(2)}, u32[]{:S(2)}) collective-permute-start(f32[12,1088]{1,0:T(8,128)S(1)} %add.15), channel_id=1, source_target_pairs={{0,4},{4,0},{8,12},{12,8},{1,5},{5,1},{9,13},{13,9},{2,6},{6,2},{1... | collective-permute-start | bytes 156680 | tf_op jit(solution)/shard_map/ppermute | solution.py:62
  286.9 15.6 %collective-permute-start.63 = (bf16[2,272,128]{2,1,0:T(8,128)(2,1)S(1)}, bf16[2,272,128]{2,1,0:T(8,128)(2,1)S(1)}, u32[]{:S(2)}, u32[]{:S(2)}) collective-permute-start(bf16[2,272,128]{2,1,0:T(8,128)(2,1)S(1)} %get-tuple-element.200), channel_id=1, source_target_pairs={{0,0},{8,1},{16,2},{24,3},{2,4},{10,5},{18,6},{26,7},{4,8},{12,9},... | collective-permute-start | bytes 417800 | tf_op jit(solution)/shard_map/ppermute | solution.py:1029
  287.6 17.6 %collective-permute-start.64 = (bf16[2,272,128]{2,1,0:T(8,128)(2,1)}, bf16[2,272,128]{2,1,0:T(8,128)(2,1)S(1)}, u32[]{:S(2)}, u32[]{:S(2)}) collective-permute-start(bf16[2,272,128]{2,1,0:T(8,128)(2,1)} %get-tuple-element.201), channel_id=1, source_target_pairs={{2,0},{10,1},{18,2},{26,3},{0,4},{8,5},{16,6},{24,7},{6,8},{14,9},... | collective-permute-start | bytes 417800 | tf_op jit(solution)/shard_map/ppermute | solution.py:1029
  293.3 14.6 %collective-permute-start.65 = (bf16[2,272,128]{2,1,0:T(8,128)(2,1)}, bf16[2,272,128]{2,1,0:T(8,128)(2,1)S(1)}, u32[]{:S(2)}, u32[]{:S(2)}) collective-permute-start(bf16[2,272,128]{2,1,0:T(8,128)(2,1)} %get-tuple-element.202), channel_id=1, source_target_pairs={{4,0},{12,1},{20,2},{28,3},{6,4},{14,5},{22,6},{30,7},{0,8},{8,9},... | collective-permute-start | bytes 417800 | tf_op jit(solution)/shard_map/ppermute | solution.py:1029
  295.4 16.9 %collective-permute-start.66 = (bf16[2,272,128]{2,1,0:T(8,128)(2,1)}, bf16[2,272,128]{2,1,0:T(8,128)(2,1)}, u32[]{:S(2)}, u32[]{:S(2)}) collective-permute-start(bf16[2,272,128]{2,1,0:T(8,128)(2,1)} %get-tuple-element.203), channel_id=1, source_target_pairs={{6,0},{14,1},{22,2},{30,3},{4,4},{12,5},{20,6},{28,7},{2,8},{10,9}... | collective-permute-start | bytes 417800 | tf_op jit(solution)/shard_map/ppermute | solution.py:1029
  301.5 11.4 %collective-permute-start.76 = (f32[12,1088]{1,0:T(8,128)S(1)}, f32[12,1088]{1,0:T(8,128)S(1)}, u32[]{:S(2)}, u32[]{:S(2)}) collective-permute-start(f32[12,1088]{1,0:T(8,128)S(1)} %add.16.refs_1_), channel_id=1, source_target_pairs={{0,8},{4,12},{8,0},{12,4},{1,9},{5,13},{9,1},{13,5},{2,10},{6,14},... | collective-permute-start | bytes 156680 | tf_op jit(solution)/shard_map/ppermute | solution.py:62
  302.6 16.5 %collective-permute-start.80 = (bf16[2,136,272]{2,1,0:T(8,128)(2,1)S(1)}, bf16[2,136,272]{2,1,0:T(8,128)(2,1)S(1)}, u32[]{:S(2)}, u32[]{:S(2)}) collective-permute-start(bf16[2,136,272]{2,1,0:T(8,128)(2,1)S(1)} %get-tuple-element.218), channel_id=1, source_target_pairs={{0,4},{4,0},{8,12},{12,8},{1,5},{5,1},{9,13},{13,9},{2,6},{6,2},{1... | collective-permute-start | bytes 443912 | tf_op jit(solution)/shard_map/ppermute | solution.py:62
  305.9 13.2 %collective-permute-start.81 = (bf16[2,136,272]{2,1,0:T(8,128)(2,1)S(1)}, bf16[2,136,272]{2,1,0:T(8,128)(2,1)S(1)}, u32[]{:S(2)}, u32[]{:S(2)}) collective-permute-start(bf16[2,136,272]{2,1,0:T(8,128)(2,1)S(1)} %get-tuple-element.219), channel_id=1, source_target_pairs={{0,8},{4,12},{8,0},{12,4},{1,9},{5,13},{9,1},{13,5},{2,10},{6,14},... | collective-permute-start | bytes 443912 | tf_op jit(solution)/shard_map/ppermute | solution.py:62
  308.6 10.5 %collective-permute-start.82 = (bf16[2,136,272]{2,1,0:T(8,128)(2,1)S(1)}, bf16[2,136,272]{2,1,0:T(8,128)(2,1)S(1)}, u32[]{:S(2)}, u32[]{:S(2)}) collective-permute-start(bf16[2,136,272]{2,1,0:T(8,128)(2,1)S(1)} %get-tuple-element.220), channel_id=1, source_target_pairs={{0,12},{4,8},{8,4},{12,0},{1,13},{5,9},{9,5},{13,1},{2,14},{6,10},... | collective-permute-start | bytes 443912 | tf_op jit(solution)/shard_map/ppermute | solution.py:62
  312.9 11.2 %collective-permute-start.93 = (bf16[136,336]{1,0:T(8,128)(2,1)S(1)}, bf16[136,336]{1,0:T(8,128)(2,1)S(1)}, u32[]{:S(2)}, u32[]{:S(2)}) collective-permute-start(bf16[136,336]{1,0:T(8,128)(2,1)S(1)} %get-tuple-element.228), channel_id=1, source_target_pairs={{0,2},{1,3},{2,0},{3,1},{4,6},{5,7},{6,4},{7,5},{8,10},{9,11},{10,... | collective-permute-start | bytes 274184 | tf_op jit(solution)/shard_map/ppermute | solution.py:66
  327.7 15.3 %collective-permute-start.96 = (bf16[2,136,272]{2,1,0:T(8,128)(2,1)S(1)}, bf16[2,136,272]{2,1,0:T(8,128)(2,1)S(1)}, u32[]{:S(2)}, u32[]{:S(2)}) collective-permute-start(bf16[2,136,272]{2,1,0:T(8,128)(2,1)S(1)} %get-tuple-element.230.refs_1_), channel_id=1, source_target_pairs={{0,16},{16,0},{1,17},{17,1},{2,18},{18,2},{3,19},{19,3},{4,20},{20... | collective-permute-start | bytes 443912 | tf_op jit(solution)/shard_map/ppermute | solution.py:58
  (137 other events, 1060.2 us)
Sparse Core Ops, SparseCore 0:
  98.1 27.7 all-gather.4
  127.4 30.7 all-gather.6
  217.5 50.0 reduce-scatter.1
where the time goes:
time: 357 us; the launch traced here: 353 us
  starting transfers between devices  120 us (34%)
  Pallas kernels  95 us (27%)
  waiting for transfers between devices  87.8 us (25%)
  local copies, waits for them, and re-layouts  34.9 us (10%)
  between operations  15.3 us (4%)
    pallas_call x37, Pallas kernels, kernel(): pl.pallas_call(run, name=body.__name__, out_shape=tuple((jax.ShapeDtypeSt...  95 us
    ppermute x38, starting transfers between devices, from_peer(): return lax.ppermute(value, 'gx', [(i, i ^ step) for i in range(4)])  57.3 us
    ppermute x38, waiting for transfers between devices, from_peer(): return lax.ppermute(value, 'gx', [(i, i ^ step) for i in range(4)])  48.4 us
    unnamed x190, local copies, waits for them, and re-layouts  32.5 us
    ppermute x9, waiting for transfers between devices, from_below(): return lax.ppermute(value, 'gy', [(i, (i + step) % 4) for i in range(4)])  27.3 us
    ppermute x9, starting transfers between devices, from_below(): return lax.ppermute(value, 'gy', [(i, (i + step) % 4) for i in range(4)])  16.7 us
    ppermute x4, starting transfers between devices, shards(): landed = [lax.ppermute(done[m], EVERY, BACK[m]) for m in range(4)]  12.5 us
    ppermute x43, starting transfers between devices, swap_core(): return lax.ppermute(value, 'c', [(0, 1), (1, 0)])  11 us
  transfers between devices with their start and end apart: 106, of which 23 were waited for; matrix products, arithmetic and copies ran while one was open for 0% of the time, Pallas kernels for 24%

commit v1 on v0

--- a/solution.py
+++ b/solution.py
@@ -233,14 +233,17 @@
     own_bias[...] = jnp.concatenate([bias[i, pl.ds(d, 1)] for i in range(4)], 1)
 
 
-def mlp_join(ids, b0, b1, b2, b3, up, down, held):
+def mlp_join(ids, b0, b1, b2, b3, out, held):
     g = ids[1]
     for k, block in enumerate((b0, b1, b2, b3)):
         held[g ^ k] = block[...]
     part = held.shape[3]
     for i in range(4):
-        up[:, i * part : (i + 1) * part] = held[i, 0]
-        down[:, i * part : (i + 1) * part] = held[i, 1]
+        out[:, :, i * part : (i + 1) * part] = held[i]
+
+
+def rows_of(both, which):
+    return both[:, which].astype(F32).reshape(-1, both.shape[3]).astype(BF)
 
 
 def out_half(ids, w, wq, out, tall):
@@ -374,7 +377,7 @@
 
 def attend_back(ids, g_in, gs_in, q_in, k_in, v_in, kv_in, qs_in, probs, probs_s, w, w16, n_abs, *refs):
     grad_kv, grad_qs, sums, moments, near = refs[:5]
-    far, windows, grads, grads_rel, tall = refs[5:9], refs[9:13], *refs[13:]
+    far, windows, grads, grads_rel, tall = refs[5:9], *refs[9:]
     d = ids[3]
     rows = g_in.shape[1]
     seq = 8 * rows
@@ -453,12 +456,11 @@
     pairs = dot(grads[:, :, : 3 * PAIR].reshape(seq, 3 * PAIR), tokens, ((0,), (0,)))
     tall[: 3 * PAIR] = pairs
     tall[3 * PAIR :] = jnp.zeros((WINDOW, width), F32)
-    z = ids[2]
     line = lax.broadcasted_iota(jnp.int32, (WINDOW, width), 0)
-    for s, ref in enumerate(windows):
-        _, length, filled = run_of(ids, d, (z + s) & 3)
+    for i in range(4):
+        _, length, filled = run_of(ids, d, i)
         window = tall[pl.ds(aligned(filled, 16), WINDOW)]
-        ref[...] = jnp.where(line < length, window, 0.0).astype(BF)
+        windows[i] = jnp.where(line < length, window, 0.0).astype(BF)
     pair_sums = jnp.concatenate([qsum, ksum, vsum], 1)
     moments[...] = jnp.concatenate(
         [column_sum(pairs * w[...].astype(F32)), weighted(jnp.broadcast_to(pair_sums, (8, 3 * PAIR)), w[...])[:1]], 0
@@ -548,18 +550,20 @@
 
 
 def grad_activated(ids, *refs):
-    g, down, g_rel, out = refs[:8], refs[8], refs[9], refs[10]
-    rows = g_rel.shape[1]
+    g, both, out, held = refs[:8], *refs[8:]
+    rows = held.shape[1]
+    down = rows_of(both, 1)
     for r in range(8):
-        g_rel[r] = g[r][...]
+        held[r] = g[r][...]
     for b in range(4):
-        block = g_rel[2 * b : 2 * b + 2].reshape(2 * rows, g_rel.shape[2])
-        out[b * 2 * rows : (b + 1) * 2 * rows] = dot(block, down[...], ((1,), (1,)))
+        block = held[2 * b : 2 * b + 2].reshape(2 * rows, held.shape[2])
+        out[b * 2 * rows : (b + 1) * 2 * rows] = dot(block, down, ((1,), (1,)))
 
 
 def feed_forward(ids, *refs):
     n, refs = refs[:8], refs[8:]
-    up, grad_act, bias, n_rel, act, grad_pre, bias_sum = refs[:7]
+    both, grad_act, bias, n_rel, act, grad_pre, bias_sum = refs[:7]
+    up = rows_of(both, 0)
     far, near = refs[7:11], refs[11]
     rows = n_rel.shape[1]
     for r in range(8):
@@ -568,7 +572,7 @@
     for b in (2, 3, 0, 1):
         at = slice(b * 2 * rows, (b + 1) * 2 * rows)
         block = n_rel[2 * b : 2 * b + 2].reshape(2 * rows, n_rel.shape[2])
-        pre = dot(block, up[...], ((1,), (1,))) + bias[...]
+        pre = dot(block, up, ((1,), (1,))) + bias[...]
         square = pre * pre
         bent = jnp.tanh(ROOT * pre * (1.0 + 0.044715 * square))
         half = 0.5 * (1.0 + bent)
@@ -577,7 +581,7 @@
         low = (grad_act[at] * slope).astype(BF)
         grad_pre[at] = low
         total = total + column_sum(low.astype(F32))
-        out = dot(low, up[...], ((1,), (0,))).astype(BF)
+        out = dot(low, up, ((1,), (0,))).astype(BF)
         if b >= 2:
             far[2 * b - 4][...] = out[:rows]
             far[2 * b - 3][...] = out[rows:]
@@ -586,23 +590,27 @@
     bias_sum[...] = total
 
 
-def feed_out(ids, act, down, *refs):
+def feed_out(ids, act, both, *refs):
     far, near = refs[:4], refs[4]
+    down = rows_of(both, 1)
     half = near.shape[0]
-    out = dot(act[half:], down[...], ((1,), (0,))).astype(BF)
+    out = dot(act[half:], down, ((1,), (0,))).astype(BF)
     rows = half // 4
     for k, ref in enumerate(far):
         ref[...] = out[k * rows : (k + 1) * rows]
-    near[...] = dot(act[:half], down[...], ((1,), (0,))).astype(BF)
-
-
-def mlp_grads(ids, act, grad_pre, n_rel, g_rel, out):
+    near[...] = dot(act[:half], down, ((1,), (0,))).astype(BF)
+
+
+def mlp_grads(ids, act, grad_pre, n_rel, *refs):
+    g, out, held = refs[:8], refs[8], refs[9]
     rows, width = n_rel.shape[1], n_rel.shape[2]
     part = out.shape[2]
+    for r in range(8):
+        held[r] = g[r][...]
     up = dot(grad_pre[...], n_rel[...].reshape(8 * rows, width), ((0,), (0,)))
     for i in range(4):
         out[i, 0] = up[i * part : (i + 1) * part].astype(BF)
-    down = dot(act[...], g_rel[...].reshape(8 * rows, width), ((0,), (0,)))
+    down = dot(act[...], held[...].reshape(8 * rows, width), ((0,), (0,)))
     for i in range(4):
         out[i, 1] = down[i * part : (i + 1) * part].astype(BF)
 
@@ -625,12 +633,11 @@
     down[...] = held[:, 1].reshape(-1, held.shape[3]).T
 
 
-def qkv_lanes(ids, b0, b1, b2, b3, o0, o1, o2, o3, held):
+def qkv_lanes(ids, window, o0, o1, o2, o3, held):
     g = ids[1]
     part = held.shape[2]
-    window = sum(ref[...].astype(F32) for ref in (b0, b1, b2, b3))
     for i in range(4):
-        held[i] = window[:, i * part : (i + 1) * part].astype(BF)
+        held[i] = window[:, i * part : (i + 1) * part]
     for k, ref in enumerate((o0, o1, o2, o3)):
         ref[...] = held[g ^ k]
 
@@ -774,23 +781,19 @@
     def shifted(blocks):
         return [blocks[0]] + [from_below(blocks[s], s) for s in range(1, 4)]
 
-    sent = kernel(
-        send_tokens, [block] * 4, [], ids, hidden_in.transpose(0, 2, 1), cotangent.transpose(0, 2, 1), us=1.0
-    )
-    blocks = [lax.ppermute(sent[m], EVERY, MOVES[m]) for m in range(4)]
     window = ((WINDOW, quarter), BF)
     window_wide = ((WINDOW, width), BF)
-    windows = peers(
-        kernel(
-            qkv_windows, [window] * 4, [((cols + WINDOW, quarter), F32)], ids, w_qkv, us=1.5, after=(sent[0],)
-        )
-    )
+    windows = kernel(qkv_windows, [window] * 4, [((cols + WINDOW, quarter), F32)], ids, w_qkv, us=1.5)
+    first = windows[0]
+    windows = peers(windows)
+    sent = kernel(
+        send_tokens, [block] * 4, [], ids, hidden_in.transpose(0, 2, 1), cotangent.transpose(0, 2, 1), us=1.0, after=(first,)
+    )
+    blocks = [lax.ppermute(sent[m], EVERY, MOVES[m]) for m in range(4)]
     lines = TALL + 3 * 16
     out_piece = kernel(
         out_half, [((lines, quarter), BF)], [((cols, quarter), F32)], ids, w_out, w_qkv, us=1.0, after=(sent[0],)
     )
-    x_own, n1_own = kernel(take_normed, [own_bf, own_bf], [held_tokens], ids, *blocks, vectors, us=1.5)
-    n1 = gather_plane(n1_own)
     piece = ((WINDOW + lines // 4, width), BF)
     joined = kernel(join_lanes, [piece], [((4, WINDOW, quarter), BF)], ids, *windows, out_piece, us=1.0)
     joined = shifted([joined] * 4)
@@ -803,11 +806,15 @@
         w_down.T,
         up_bias.astype(F32).reshape(4, 8, part),
         us=2.0,
-        after=(joined[0], n1[1], n1[2], n1[3]),
+        after=(joined[0],),
     )
     mlp_got = peers(mlp_sent)
+    x_own, n1_own = kernel(
+        take_normed, [own_bf, own_bf], [held_tokens], ids, *blocks, vectors, us=1.5, after=(joined[1], joined[3], *mlp_got[1:])
+    )
+    n1 = gather_plane(n1_own)
     g_own = kernel(
-        take_tokens, [own_bf], [held_tokens], ids, *blocks, us=1.0, after=(n1[1], n1[2], n1[3])
+        take_tokens, [own_bf], [held_tokens], ids, *blocks, us=1.0, after=(n1_own,)
     )
     g_near = gather_near(g_own)
     w_own, out_row = kernel(
@@ -817,19 +824,18 @@
         ids,
         *joined,
         us=1.0,
-        after=(*g_near[1:], *mlp_got[1:]),
-    )
-    up_part, down_part = kernel(
+        after=(g_own,),
+    )
+    mlp_part = kernel(
         mlp_join,
-        [((part, width), BF)] * 2,
+        [((2, part, width), BF)],
         [((4, 2, part, quarter), BF)],
         ids,
         *mlp_got,
         us=1.0,
         after=(w_own,),
     )
-    up_own = lax.all_gather(up_part, "gy", axis=0, tiled=False).reshape(own_hidden, width)
-    down_own = lax.all_gather(down_part, "gy", axis=0, tiled=False).reshape(own_hidden, width)
+    mlp_own = lax.all_gather(mlp_part, "gy", axis=0, tiled=False)
     swapped_ids = swap_core(segment_ids)
 
     half_rows = ((4 * rows, width), BF)
@@ -846,11 +852,12 @@
         vectors,
         segment_ids,
         swapped_ids,
-        us=11.0,
+        us=3.0,
         far=True,
-    )
-    out_rows = gather_later(gather_near(out_row), (att,))
+        after=(mlp_part,),
+    )
     att_got = lax.all_to_all(att, PLANE, split_axis=0, concat_axis=0, tiled=True)
+    out_rows = gather_later(gather_near(out_row), (att_got,))
     wo, w16 = kernel(
         out_whole,
         [((width, width), BF), ((3 * HEAD_DIM, width), BF)],
@@ -858,7 +865,6 @@
         ids,
         *out_rows,
         us=1.0,
-        after=(att_got,),
     )
     kv, qs, probs_s, att_s = kernel(
         attend_shared,
@@ -871,11 +877,11 @@
         vectors,
         segment_ids,
         swapped_ids,
-        us=2.0,
+        us=0.5,
         work=6,
     )
     middle, n2_own = kernel(
-        out_norm, [own_f32, own_bf], [], ids, att_got, att_s, wo, x_own, vectors, us=2.0, work=6
+        out_norm, [own_f32, own_bf], [], ids, att_got, att_s, wo, x_own, vectors, us=0.5, work=6
     )
     g_all = gather_later(g_near, (n2_own,))
     summed = [own_f32, own_bf, own_bf, own_bf]
@@ -887,8 +893,16 @@
 
     n2 = gather_plane(n2_own)
 
-    g_rel, grad_act = kernel(
-        grad_activated, [all_bf, ((seq, own_hidden), F32)], [], ids, *g_all, down_own, us=3.0, after=(n2_own, up_own)
+    grad_act = kernel(
+        grad_activated,
+        [((seq, own_hidden), F32)],
+        [all_bf],
+        ids,
+        *g_all,
+        mlp_own,
+        us=3.0,
+        far=True,
+        after=(n2_own,),
     )
     n_rel, act, grad_pre, up_sum, *far, near = kernel(
         feed_forward,
@@ -903,28 +917,28 @@
         [],
         ids,
         *n2,
-        up_own,
+        mlp_own,
         grad_act,
         up_bias_own,
         us=7.0,
-        work=8,
+        work=14,
     )
     parts = scatter(near, far)
     mlp_partial = kernel(
         mlp_grads,
         [((4, 2, part, width), BF)],
-        [],
+        [all_bf],
         ids,
         act,
         grad_pre,
         n_rel,
-        g_rel,
+        *g_all,
         us=5.0,
-        work=8,
+        far=True,
         after=(parts[0],),
     )
     *feed_far, feed_near = kernel(
-        feed_out, [own_bf] * 4 + [half_rows], [], ids, act, down_own, us=2.5, work=4, after=(mlp_partial,)
+        feed_out, [own_bf] * 4 + [half_rows], [], ids, act, mlp_own, us=2.5, work=8, after=(mlp_partial,)
     )
     mlp_summed = over_outer(lax.psum_scatter(mlp_partial, "gy", scatter_dimension=0, tiled=False))
     grad_middle, gb_own, middle_sums, back, back_s = kernel(
@@ -950,7 +964,7 @@
         attend_back,
         [pair_seq, ((rows, HEAD_DIM), BF), ((8, PAIR), F32), ((2, width), F32), half_rows]
         + [own_bf] * 4
-        + [window_wide] * 4,
+        + [((4, WINDOW, width), BF)],
         [
             ((8, rows, 4 * PAIR), BF),
             ((8, rows, 4 * PAIR), BF),
@@ -969,12 +983,12 @@
         w_own,
         w16,
         n_abs,
-        us=13.0,
+        us=3.0,
         far=True,
         after=(feed_parts[0],),
     )
     far = rest[:4]
-    windows = shifted(rest[4:])
+    window_sum = lax.psum_scatter(rest[4], "gy", scatter_dimension=0, tiled=False)
     parts = scatter(near, far)
     out_sent, moments_s = kernel(
         out_grads,
@@ -1037,7 +1051,7 @@
     others = from_peer(smalls, 2)
     blocks = peers(mlp_parts)
     lanes = kernel(
-        qkv_lanes, [window] * 4, [((4, WINDOW, quarter), BF)], ids, *windows, us=1.0, after=(*landed, *blocks[1:], out_split_parts[0], others)
+        qkv_lanes, [window] * 4, [((4, WINDOW, quarter), BF)], ids, window_sum, us=1.0, after=(*landed, *blocks[1:], out_split_parts[0], others)
     )
     near = peers(lanes)
     near = [*near, *[swap_core(piece) for piece in near]]

time: 357 us -> 339 us (0.950)
  starting transfers between devices: 120 us -> 109 us
  waiting for transfers between devices: 87.8 us -> 77.4 us
  Pallas kernels: 95 us -> 101 us
    ppermute x38, starting transfers between devices: 57.3 us -> 45.6 us  [from_peer(): return lax.ppermute(value, 'gx', [(i, i ^ step) for i in range(4)])]
    ppermute x9 -> x6, waiting for transfers between devices: 27.3 us -> 16.8 us  [from_below(): return lax.ppermute(value, 'gy', [(i, (i + step) % 4) for i in range(4)])]
    pallas_call x37, Pallas kernels: 95 us -> 101 us  [kernel(): pl.pallas_call(run, name=body.__name__, out_shape=tuple((jax.ShapeDtypeSt...]
    unnamed x190 -> x176, local copies, waits for them, and re-layouts: 32.5 us -> 30.8 us
    ppermute x9 -> x6, starting transfers between devices: 16.7 us -> 16.2 us  [from_below(): return lax.ppermute(value, 'gy', [(i, (i + step) % 4) for i in range(4)])]
  transfers between devices with their start and end apart: 106 -> 103, of which waited for: 23 -> 25; matrix products, arithmetic and copies ran while one was open for 0% -> 0% of each run, Pallas kernels for 24% -> 21%
where the time goes in v1:
time: 339 us; the launch traced here: 336 us
  starting transfers between devices  109 us (32%)
  Pallas kernels  101 us (30%)
  waiting for transfers between devices  77.4 us (23%)
  local copies, waits for them, and re-layouts  33.2 us (10%)
  between operations  15.1 us (4%)
    pallas_call x37, Pallas kernels, kernel(): pl.pallas_call(run, name=body.__name__, out_shape=tuple((jax.ShapeDtypeSt...  101 us
    ppermute x38, waiting for transfers between devices, from_peer(): return lax.ppermute(value, 'gx', [(i, i ^ step) for i in range(4)])  48.8 us
    ppermute x38, starting transfers between devices, from_peer(): return lax.ppermute(value, 'gx', [(i, i ^ step) for i in range(4)])  45.6 us
    unnamed x176, local copies, waits for them, and re-layouts  30.8 us
    ppermute x6, waiting for transfers between devices, from_below(): return lax.ppermute(value, 'gy', [(i, (i + step) % 4) for i in range(4)])  16.8 us
    ppermute x6, starting transfers between devices, from_below(): return lax.ppermute(value, 'gy', [(i, (i + step) % 4) for i in range(4)])  16.2 us
    ppermute x4, starting transfers between devices, shards(): landed = [lax.ppermute(done[m], EVERY, BACK[m]) for m in range(4)]  11.6 us
    ppermute x43, starting transfers between devices, swap_core(): return lax.ppermute(value, 'c', [(0, 1), (1, 0)])  9.94 us
  transfers between devices with their start and end apart: 103, of which 25 were waited for; matrix products, arithmetic and copies ran while one was open for 0% of the time, Pallas kernels for 21%

profile of v1, /device:TPU:0, one launch (start us, length us, event | category | flops | bytes accessed | tf_op | source)
XLA Modules:
  0.0 335.5 jit_solution(10660131579358203444)
XLA Ops:
  9.8 3.0 collective-permute-start.4
  12.8 1.5 collective-permute-start.5
  15.1 3.1 collective-permute-start.1
  20.0 2.7 collective-permute-start.2
  22.7 3.1 collective-permute-start.3
  26.6 6.4 %collective-permute-start.8 = (bf16[176,1088]{1,0:T(8,128)(2,1)S(1)}, bf16[176,1088]{1,0:T(8,128)(2,1)S(1)}, u32[]{:S(2)}, u32[]{:S(2)}) collective-permute-start(bf16[176,1088]{1,0:T(8,128)(2,1)S(1)} %join_lanes.1.refs_4_.refs_1_), channel_id=1, source_target_pairs={{0,3},{1,0},{2,1},{3,2},{4,7},{5,4},{6,5},{7,6},{8,11},{9,8},{10,9... | collective-permute-start | bytes 1148936 | tf_op jit(solution)/shard_map/ppermute | solution.py:66
  35.0 3.5 %collective-permute-start.9 = (bf16[2,136,272]{2,1,0:T(8,128)(2,1)S(1)}, bf16[2,136,272]{2,1,0:T(8,128)(2,1)S(1)}, u32[]{:S(2)}, u32[]{:S(2)}) collective-permute-start(bf16[2,136,272]{2,1,0:T(8,128)(2,1)S(1)} %get-tuple-element.125), channel_id=1, source_target_pairs={{0,4},{4,0},{8,12},{12,8},{1,5},{5,1},{9,13},{13,9},{2,6},{6,2},{1... | collective-permute-start | bytes 443912 | tf_op jit(solution)/shard_map/ppermute | solution.py:62
  38.5 1.5 collective-permute-start.11
  40.3 4.1 %collective-permute-done.9.refs_8_.refs_2_ = bf16[2,136,272]{2,1,0:T(8,128)(2,1)S(1)} collective-permute-done((bf16[2,136,272]{2,1,0:T(8,128)(2,1)S(1)}, bf16[2,136,272]{2,1,0:T(8,128)(2,1)S(1)}, u32[]{:S(2)}, u32[]{:S(2)}) %collective-permute-start.9) | collective-permute-done | bytes 148000 | tf_op jit(solution)/shard_map/ppermute | solution.py:62
  44.4 5.4 %collective-permute-done.10.refs_9_.refs_3_ = bf16[2,136,272]{2,1,0:T(8,128)(2,1)S(1)} collective-permute-done((bf16[2,136,272]{2,1,0:T(8,128)(2,1)S(1)}, bf16[2,136,272]{2,1,0:T(8,128)(2,1)S(1)}, u32[]{:S(2)}, u32[]{:S(2)}) %collective-permute-start.10) | collective-permute-done | bytes 148000 | tf_op jit(solution)/shard_map/ppermute | solution.py:62
  49.8 1.9 collective-permute-start.19
  54.1 2.7 collective-permute-start.14
  57.5 14.0 %collective-permute-done.19.refs_3_ = bf16[176,1088]{1,0:T(8,128)(2,1)S(1)} collective-permute-done((bf16[176,1088]{1,0:T(8,128)(2,1)S(1)}, bf16[176,1088]{1,0:T(8,128)(2,1)S(1)}, u32[]{:S(2)}, u32[]{:S(2)}) %collective-permute-start.19) | collective-permute-done | bytes 383008 | tf_op jit(solution)/shard_map/ppermute | solution.py:66
  73.7 6.5 %collective-permute-done.12.refs_2_ = bf16[128,1088]{1,0:T(8,128)(2,1)S(1)} collective-permute-done((bf16[128,1088]{1,0:T(8,128)(2,1)S(1)}, bf16[128,1088]{1,0:T(8,128)(2,1)S(1)}, u32[]{:S(2)}, u32[]{:S(2)}) %collective-permute-start.12) | collective-permute-done | bytes 278560 | tf_op jit(solution)/shard_map/ppermute | solution.py:62
  80.2 1.7 mlp_join.1.refs_13_
  84.9 1.6 collective-permute-start.21
  86.4 10.4 %attend.1 = (bf16[8,128,1088]{2,1,0:T(8,128)(2,1)}, bf16[1024,128]{1,0:T(8,128)(2,1)}, bf16[1024,128]{1,0:T(8,128)(2,1)}, bf16[1024,128]{1,0:T(8,128)(2,1)}, bf1...) custom-call(s32[100]{0:T(128)} %copy-done.5, bf16[128,1088]{1,0:T(8,128)(2,1)} %copy-done.17, ...), custom_call_target="tpu_custom_call" | custom-call | flops 15000000512 | bytes 300000 | tf_op jit(solution)/shard_map/attend/pallas_call | solution.py:44
  96.9 3.4 %all-to-all-start = ((bf16[8,128,128]{2,1,0:T(8,128)(2,1)}), bf16[8,128,128]{2,1,0:T(8,128)(2,1)S(1)}, u32[]{:S(2)}, u32[]{:S(2)}) async-start(bf16[8,128,128]{2,1,0:T(8,128)(2,1)} %get-tuple-element.131.refs_9_), calls=%async_computation | async-start | bytes 524288 | tf_op jit(solution)/shard_map/all_to_all | solution.py:859
  100.6 3.8 %collective-permute-done.22.refs_3_ = bf16[176,1088]{1,0:T(8,128)(2,1)S(1)} collective-permute-done((bf16[176,1088]{1,0:T(8,128)(2,1)S(1)}, bf16[176,1088]{1,0:T(8,128)(2,1)S(1)}, u32[]{:S(2)}, u32[]{:S(2)}) %collective-permute-start.22) | collective-permute-done | bytes 383008 | tf_op jit(solution)/shard_map/ppermute | solution.py:62
  104.4 2.4 all-to-all-done.refs_5_.refs_1_
  113.6 2.2 attend_shared.1
  117.2 2.4 out_norm.1
  123.1 2.8 collective-permute-done.36.refs_3_.refs_6_
  127.2 5.0 %collective-permute-done.30.refs_4_ = bf16[128,1088]{1,0:T(8,128)(2,1)S(1)} collective-permute-done((bf16[128,1088]{1,0:T(8,128)(2,1)}, bf16[128,1088]{1,0:T(8,128)(2,1)S(1)}, u32[]{:S(2)}, u32[]{:S(2)}) %collective-permute-start.30) | collective-permute-done | bytes 278560 | tf_op jit(solution)/shard_map/ppermute | solution.py:62
  132.2 5.6 %collective-permute-done.29.refs_3_ = bf16[128,1088]{1,0:T(8,128)(2,1)} collective-permute-done((bf16[128,1088]{1,0:T(8,128)(2,1)}, bf16[128,1088]{1,0:T(8,128)(2,1)}, u32[]{:S(2)}, u32[]{:S(2)}) %collective-permute-start.29) | collective-permute-done | bytes 278560 | tf_op jit(solution)/shard_map/ppermute | solution.py:62
  139.9 6.3 %grad_activated.1.refs_10_ = f32[1024,544]{1,0:T(8,128)} custom-call(s32[100]{0:T(128)} %copy-done.5, bf16[128,1088]{1,0:T(8,128)(2,1)} %copy-done.19, bf16[128,1088]{1,0:T(8,128)(2,1)} %copy-done.24, bf16[128,1088]{1,0:T(8,128)(2,1)} %copy-done.23, bf16[128,1088]{1,0:T(8,128)(2,1)} %copy-done.22, bf16[128,1088]{1,0:T(8,128)(2,1)} %copy-done.84, ...), custom_call_target="tpu_custom_call" | custom-call | flops 15000000512 | bytes 300000 | tf_op jit(solution)/shard_map/grad_activated/pallas_call | solution.py:44
  146.2 1.7 copy-done.60
  148.0 6.5 %feed_forward.1 = (bf16[8,128,1088]{2,1,0:T(8,128)(2,1)S(1)}, bf16[1024,544]{1,0:T(8,128)(2,1)S(1)}, bf16[1024,544]{1,0:T(8,128)(2,1)S(1)}, f32[1,544]{1,0:T(1,1...) custom-call(s32[100]{0:T(128)S(1)} %copy-done.7, ...), custom_call_target="tpu_custom_call" | custom-call | flops 35000000512 | bytes 700000 | tf_op jit(solution)/shard_map/feed_forward/pallas_call | solution.py:44
  157.5 1.6 add_far.3
  159.9 19.3 %mlp_grads.1.refs_9_.refs_3_ = bf16[4,2,136,1088]{3,2,1,0:T(8,128)(2,1)} custom-call(s32[100]{0:T(128)} %copy-done.5, bf16[1024,544]{1,0:T(8,128)(2,1)} %copy-done.62, bf16[1024,544]{1,0:T(8,128)(2,1)} %copy-done.69, bf16[8,128,1088]{2,1,0:T(8,128)(2,1)} %copy-done.68, bf16[128,1088]{1,0:T(8,128)(2,1)} %copy-done.19, bf16[128,1088]{1,0:T(8,128)(2,1)} %copy-done.24, ...), custom_call_target="tpu_custom_call" | custom-call | flops 24999999488 | bytes 500000 | tf_op jit(solution)/shard_map/mlp_grads/pallas_call | solution.py:44
  180.7 2.0 collective-permute-start.48
  182.7 2.0 copy-done.11
  186.0 3.3 feed_out.1
  190.8 4.4 %collective-permute-done.47.refs_3_ = bf16[128,1088]{1,0:T(8,128)(2,1)S(1)} collective-permute-done((bf16[128,1088]{1,0:T(8,128)(2,1)}, bf16[128,1088]{1,0:T(8,128)(2,1)S(1)}, u32[]{:S(2)}, u32[]{:S(2)}) %collective-permute-start.47) | collective-permute-done | bytes 278560 | tf_op jit(solution)/shard_map/ppermute | solution.py:62
  195.2 2.4 middle_back.1
  199.0 3.4 %all-to-all-start.1 = ((bf16[8,128,128]{2,1,0:T(8,128)(2,1)}), bf16[8,128,128]{2,1,0:T(8,128)(2,1)S(1)}, u32[]{:S(2)}, u32[]{:S(2)}) async-start(bf16[8,128,128]{2,1,0:T(8,128)(2,1)} %get-tuple-element.161), calls=%async_computation.1 | async-start | bytes 524288 | tf_op jit(solution)/shard_map/all_to_all | solution.py:958
  202.5 2.8 collective-permute-start.69
  206.0 3.1 all-to-all-done.1.refs_6_.refs_1_
  209.2 1.4 copy-done.52
  210.5 1.5 add_far.4
  212.8 13.9 %attend_back.1 = (bf16[1024,128]{1,0:T(8,128)(2,1)}, bf16[128,64]{1,0:T(8,128)(2,1)}, f32[8,128]{1,0:T(8,128)}, f32[2,1088]{1,0:T(2,128)}, bf16[512,1088]{1,0:T(...) custom-call(s32[100]{0:T(128)} %copy-done.5, ...), custom_call_target="tpu_custom_call" | custom-call | flops 15000000512 | bytes 300000 | tf_op jit(solution)/shard_map/attend_back/pallas_call | solution.py:44
  231.7 1.5 add_far.5
  237.0 2.0 collective-permute-start.59
  240.6 3.4 %collective-permute-done.57.refs_2_.refs_16_ = bf16[128,1088]{1,0:T(8,128)(2,1)S(1)} collective-permute-done((bf16[128,1088]{1,0:T(8,128)(2,1)}, bf16[128,1088]{1,0:T(8,128)(2,1)S(1)}, u32[]{:S(2)}, u32[]{:S(2)}) %collective-permute-start.57) | collective-permute-done | bytes 278560 | tf_op jit(solution)/shard_map/ppermute | solution.py:62
  245.1 7.0 %collective-permute-done.58.refs_3_.refs_17_ = bf16[128,1088]{1,0:T(8,128)(2,1)S(1)} collective-permute-done((bf16[128,1088]{1,0:T(8,128)(2,1)}, bf16[128,1088]{1,0:T(8,128)(2,1)S(1)}, u32[]{:S(2)}, u32[]{:S(2)}) %collective-permute-start.58) | collective-permute-done | bytes 278560 | tf_op jit(solution)/shard_map/ppermute | solution.py:62
  254.0 1.7 copy-done.39
  257.6 3.2 out_grads.1
  261.6 3.9 %all-to-all-start.2 = ((bf16[8,136,384]{2,1,0:T(8,128)(2,1)}), bf16[8,136,384]{2,1,0:T(8,128)(2,1)S(1)}, u32[]{:S(2)}, u32[]{:S(2)}) async-start(bf16[8,136,384]{2,1,0:T(8,128)(2,1)} %get-tuple-element.207), calls=%async_computation.4 | async-start | bytes 1671168 | tf_op jit(solution)/shard_map/all_to_all | solution.py:1010
  265.6 2.0 collective-permute-start.75
  270.8 2.8 finish.1
  274.3 4.2 %collective-permute-start.64 = (bf16[2,272,128]{2,1,0:T(8,128)(2,1)S(1)}, bf16[2,272,128]{2,1,0:T(8,128)(2,1)S(1)}, u32[]{:S(2)}, u32[]{:S(2)}) collective-permute-start(bf16[2,272,128]{2,1,0:T(8,128)(2,1)S(1)} %get-tuple-element.190), channel_id=1, source_target_pairs={{2,0},{10,1},{18,2},{26,3},{0,4},{8,5},{16,6},{24,7},{6,8},{14,9},... | collective-permute-start | bytes 417800 | tf_op jit(solution)/shard_map/ppermute | solution.py:1043
  278.5 1.8 collective-permute-start.65
  280.4 4.8 %collective-permute-start.66 = (bf16[2,272,128]{2,1,0:T(8,128)(2,1)}, bf16[2,272,128]{2,1,0:T(8,128)(2,1)S(1)}, u32[]{:S(2)}, u32[]{:S(2)}) collective-permute-start(bf16[2,272,128]{2,1,0:T(8,128)(2,1)} %get-tuple-element.192), channel_id=1, source_target_pairs={{6,0},{14,1},{22,2},{30,3},{4,4},{12,5},{20,6},{28,7},{2,8},{10,9}... | collective-permute-start | bytes 417800 | tf_op jit(solution)/shard_map/ppermute | solution.py:1043
  289.4 1.4 collective-permute-start.79
  293.0 4.8 %collective-permute-start.89 = (bf16[136,336]{1,0:T(8,128)(2,1)S(1)}, bf16[136,336]{1,0:T(8,128)(2,1)S(1)}, u32[]{:S(2)}, u32[]{:S(2)}) collective-permute-start(bf16[136,336]{1,0:T(8,128)(2,1)S(1)} %get-tuple-element.213), channel_id=1, source_target_pairs={{0,1},{1,2},{2,3},{3,0},{4,5},{5,6},{6,7},{7,4},{8,9},{9,10},{10,1... | collective-permute-start | bytes 274184 | tf_op jit(solution)/shard_map/ppermute | solution.py:66
  297.8 3.1 collective-permute-start.90
  303.2 3.4 %collective-permute-start.80 = (f32[12,1088]{1,0:T(8,128)S(1)}, f32[12,1088]{1,0:T(8,128)S(1)}, u32[]{:S(2)}, u32[]{:S(2)}) collective-permute-start(f32[12,1088]{1,0:T(8,128)S(1)} %add_two.1), channel_id=1, source_target_pairs={{0,1},{1,0},{2,3},{3,2},{4,5},{5,4},{6,7},{7,6},{8,9},{9,8},{10,11... | collective-permute-start | bytes 156680 | tf_op jit(solution)/shard_map/ppermute | solution.py:1087
  306.6 2.1 collective-permute-done.90.refs_3_
  309.4 1.4 land_tokens.1
  313.2 1.6 collective-permute-start.84
  316.1 1.5 out_land.1
  319.0 1.8 collective-permute-done.81.refs_2_
  323.8 2.2 qkv_land.1
  326.0 2.8 mlp_land.1
  (376 shorter events, 79.8 us)
Async XLA Ops:
  7.2 132.7 %all-gather.3.cloned.1.call-start = ((), (), s32[]{:S(2)}) async-start(), calls=%async_computation.7 | async-start | bytes 3133440 | tf_op jit(solution)/shard_map/all_gather | solution.py:838
  9.8 10.1 %collective-permute-start.4 = (bf16[128,272]{1,0:T(8,128)(2,1)S(1)}, bf16[128,272]{1,0:T(8,128)(2,1)S(1)}, u32[]{:S(2)}, u32[]{:S(2)}) collective-permute-start(bf16[128,272]{1,0:T(8,128)(2,1)S(1)} %get-tuple-element.122), channel_id=1, source_target_pairs={{0,4},{4,0},{8,12},{12,8},{1,5},{5,1},{9,13},{13,9},{2,6},{6,2},{1... | collective-permute-start | bytes 208904 | tf_op jit(solution)/shard_map/ppermute | solution.py:62
  14.4 11.4 %collective-permute-start.6 = (bf16[128,272]{1,0:T(8,128)(2,1)S(1)}, bf16[128,272]{1,0:T(8,128)(2,1)S(1)}, u32[]{:S(2)}, u32[]{:S(2)}) collective-permute-start(bf16[128,272]{1,0:T(8,128)(2,1)S(1)} %get-tuple-element.124), channel_id=1, source_target_pairs={{0,12},{4,8},{8,4},{12,0},{1,13},{5,9},{9,5},{13,1},{2,14},{6,10},... | collective-permute-start | bytes 208904 | tf_op jit(solution)/shard_map/ppermute | solution.py:62
  15.1 17.9 %collective-permute-start.1 = (bf16[2,272,128]{2,1,0:T(8,128)(2,1)S(1)}, bf16[2,272,128]{2,1,0:T(8,128)(2,1)S(1)}, u32[]{:S(2)}, u32[]{:S(2)}) collective-permute-start(bf16[2,272,128]{2,1,0:T(8,128)(2,1)S(1)} %get-tuple-element.119), channel_id=1, source_target_pairs={{0,2},{1,10},{2,18},{3,26},{4,0},{5,8},{6,16},{7,24},{8,6},{9,14},... | collective-permute-start | bytes 417800 | tf_op jit(solution)/shard_map/ppermute | solution.py:792
  18.2 20.3 %collective-permute-start = (bf16[2,272,128]{2,1,0:T(8,128)(2,1)S(1)}, bf16[2,272,128]{2,1,0:T(8,128)(2,1)S(1)}, u32[]{:S(2)}, u32[]{:S(2)}) collective-permute-start(bf16[2,272,128]{2,1,0:T(8,128)(2,1)S(1)} %get-tuple-element.118.refs_3_), channel_id=1, source_target_pairs={{0,0},{1,8},{2,16},{3,24},{4,2},{5,10},{6,18},{7,26},{8,4},{9,12},... | collective-permute-start | bytes 417800 | tf_op jit(solution)/shard_map/ppermute | solution.py:792
  20.0 15.0 %collective-permute-start.2 = (bf16[2,272,128]{2,1,0:T(8,128)(2,1)S(1)}, bf16[2,272,128]{2,1,0:T(8,128)(2,1)S(1)}, u32[]{:S(2)}, u32[]{:S(2)}) collective-permute-start(bf16[2,272,128]{2,1,0:T(8,128)(2,1)S(1)} %get-tuple-element.120), channel_id=1, source_target_pairs={{0,4},{1,12},{2,20},{3,28},{4,6},{5,14},{6,22},{7,30},{8,0},{9,8},... | collective-permute-start | bytes 417800 | tf_op jit(solution)/shard_map/ppermute | solution.py:792
  22.7 15.8 %collective-permute-start.3 = (bf16[2,272,128]{2,1,0:T(8,128)(2,1)S(1)}, bf16[2,272,128]{2,1,0:T(8,128)(2,1)S(1)}, u32[]{:S(2)}, u32[]{:S(2)}) collective-permute-start(bf16[2,272,128]{2,1,0:T(8,128)(2,1)S(1)} %get-tuple-element.121), channel_id=1, source_target_pairs={{0,6},{1,14},{2,22},{3,30},{4,4},{5,12},{6,20},{7,28},{8,2},{9,10}... | collective-permute-start | bytes 417800 | tf_op jit(solution)/shard_map/ppermute | solution.py:792
  26.6 25.8 %collective-permute-start.8 = (bf16[176,1088]{1,0:T(8,128)(2,1)S(1)}, bf16[176,1088]{1,0:T(8,128)(2,1)S(1)}, u32[]{:S(2)}, u32[]{:S(2)}) collective-permute-start(bf16[176,1088]{1,0:T(8,128)(2,1)S(1)} %join_lanes.1.refs_4_.refs_1_), channel_id=1, source_target_pairs={{0,3},{1,0},{2,1},{3,2},{4,7},{5,4},{6,5},{7,6},{8,11},{9,8},{10,9... | collective-permute-start | bytes 1148936 | tf_op jit(solution)/shard_map/ppermute | solution.py:66
  33.0 19.4 %collective-permute-start.7 = (bf16[176,1088]{1,0:T(8,128)(2,1)S(1)}, bf16[176,1088]{1,0:T(8,128)(2,1)S(1)}, u32[]{:S(2)}, u32[]{:S(2)}) collective-permute-start(bf16[176,1088]{1,0:T(8,128)(2,1)S(1)} %join_lanes.1.refs_4_.refs_1_), channel_id=1, source_target_pairs={{0,1},{1,2},{2,3},{3,0},{4,5},{5,6},{6,7},{7,4},{8,9},{9,10},{10,1... | collective-permute-start | bytes 1148936 | tf_op jit(solution)/shard_map/ppermute | solution.py:66
  38.5 11.3 %collective-permute-start.10 = (bf16[2,136,272]{2,1,0:T(8,128)(2,1)S(1)}, bf16[2,136,272]{2,1,0:T(8,128)(2,1)S(1)}, u32[]{:S(2)}, u32[]{:S(2)}) collective-permute-start(bf16[2,136,272]{2,1,0:T(8,128)(2,1)S(1)} %get-tuple-element.126), channel_id=1, source_target_pairs={{0,8},{4,12},{8,0},{12,4},{1,9},{5,13},{9,1},{13,5},{2,10},{6,14},... | collective-permute-start | bytes 443912 | tf_op jit(solution)/shard_map/ppermute | solution.py:62
  38.5 13.2 %collective-permute-start.11 = (bf16[2,136,272]{2,1,0:T(8,128)(2,1)S(1)}, bf16[2,136,272]{2,1,0:T(8,128)(2,1)S(1)}, u32[]{:S(2)}, u32[]{:S(2)}) collective-permute-start(bf16[2,136,272]{2,1,0:T(8,128)(2,1)S(1)} %get-tuple-element.127), channel_id=1, source_target_pairs={{0,12},{4,8},{8,4},{12,0},{1,13},{5,9},{9,5},{13,1},{2,14},{6,10},... | collective-permute-start | bytes 443912 | tf_op jit(solution)/shard_map/ppermute | solution.py:62
  44.4 38.4 %collective-permute-start.20 = (s32[2,1024]{1,0:T(2,128)S(1)}, s32[2,1024]{1,0:T(2,128)S(1)}, u32[]{:S(2)}, u32[]{:S(2)}) collective-permute-start(s32[2,1024]{1,0:T(2,128)S(1)} %copy-done.32), channel_id=1, source_target_pairs={{0,16},{16,0},{1,17},{17,1},{2,18},{18,2},{3,19},{19,3},{4,20},{20... | collective-permute-start | bytes 24584 | tf_op jit(solution)/shard_map/ppermute | solution.py:58
  49.8 21.8 %collective-permute-start.19 = (bf16[176,1088]{1,0:T(8,128)(2,1)S(1)}, bf16[176,1088]{1,0:T(8,128)(2,1)S(1)}, u32[]{:S(2)}, u32[]{:S(2)}) collective-permute-start(bf16[176,1088]{1,0:T(8,128)(2,1)S(1)} %join_lanes.1.refs_4_.refs_1_), channel_id=1, source_target_pairs={{0,2},{1,3},{2,0},{3,1},{4,6},{5,7},{6,4},{7,5},{8,10},{9,11},{10,... | collective-permute-start | bytes 1148936 | tf_op jit(solution)/shard_map/ppermute | solution.py:66
  54.0 29.8 %collective-permute-start.15 = (bf16[128,1088]{1,0:T(8,128)(2,1)S(1)}, bf16[128,1088]{1,0:T(8,128)(2,1)}, u32[]{:S(2)}, u32[]{:S(2)}) collective-permute-start(bf16[128,1088]{1,0:T(8,128)(2,1)S(1)} %get-tuple-element.128.refs_5_.refs_1_.refs_2_.refs_14_), channel_id=1, source_target_pairs={{0,16},{16,0},{1,17},{17,1},{2,18},{18,2},{3,19},{19,3},{4,20},{20... | collective-permute-start | bytes 835592 | tf_op jit(solution)/shard_map/ppermute | solution.py:58
  54.1 19.0 %collective-permute-start.14 = (bf16[128,1088]{1,0:T(8,128)(2,1)S(1)}, bf16[128,1088]{1,0:T(8,128)(2,1)}, u32[]{:S(2)}, u32[]{:S(2)}) collective-permute-start(bf16[128,1088]{1,0:T(8,128)(2,1)S(1)} %get-tuple-element.128.refs_5_.refs_1_.refs_2_.refs_14_), channel_id=1, source_target_pairs={{0,12},{4,8},{8,4},{12,0},{1,13},{5,9},{9,5},{13,1},{2,14},{6,10},... | collective-permute-start | bytes 835592 | tf_op jit(solution)/shard_map/ppermute | solution.py:62
  56.7 16.4 %collective-permute-start.13 = (bf16[128,1088]{1,0:T(8,128)(2,1)S(1)}, bf16[128,1088]{1,0:T(8,128)(2,1)}, u32[]{:S(2)}, u32[]{:S(2)}) collective-permute-start(bf16[128,1088]{1,0:T(8,128)(2,1)S(1)} %get-tuple-element.128.refs_5_.refs_1_.refs_2_.refs_14_), channel_id=1, source_target_pairs={{0,8},{4,12},{8,0},{12,4},{1,9},{5,13},{9,1},{13,5},{2,10},{6,14},... | collective-permute-start | bytes 835592 | tf_op jit(solution)/shard_map/ppermute | solution.py:62
  73.1 11.8 %collective-permute-start.18 = (bf16[128,1088]{1,0:T(8,128)(2,1)}, bf16[128,1088]{1,0:T(8,128)(2,1)}, u32[]{:S(2)}, u32[]{:S(2)}) collective-permute-start(bf16[128,1088]{1,0:T(8,128)(2,1)} %collective-permute-done.14.refs_4_), channel_id=1, source_target_pairs={{0,16},{16,0},{1,17},{17,1},{2,18},{18,2},{3,19},{19,3},{4,20},{20... | collective-permute-start | bytes 835592 | tf_op jit(solution)/shard_map/ppermute | solution.py:58
  73.2 13.2 %collective-permute-start.17 = (bf16[128,1088]{1,0:T(8,128)(2,1)}, bf16[128,1088]{1,0:T(8,128)(2,1)}, u32[]{:S(2)}, u32[]{:S(2)}) collective-permute-start(bf16[128,1088]{1,0:T(8,128)(2,1)} %collective-permute-done.13.refs_3_), channel_id=1, source_target_pairs={{0,16},{16,0},{1,17},{17,1},{2,18},{18,2},{3,19},{19,3},{4,20},{20... | collective-permute-start | bytes 835592 | tf_op jit(solution)/shard_map/ppermute | solution.py:58
  82.9 17.7 %collective-permute-start.23 = (bf16[176,1088]{1,0:T(8,128)(2,1)S(1)}, bf16[176,1088]{1,0:T(8,128)(2,1)S(1)}, u32[]{:S(2)}, u32[]{:S(2)}) collective-permute-start(bf16[176,1088]{1,0:T(8,128)(2,1)S(1)} %get-tuple-element.133.refs_1_), channel_id=1, source_target_pairs={{0,12},{4,8},{8,4},{12,0},{1,13},{5,9},{9,5},{13,1},{2,14},{6,10},... | collective-permute-start | bytes 1148936 | tf_op jit(solution)/shard_map/ppermute | solution.py:62
  83.8 20.5 %collective-permute-start.22 = (bf16[176,1088]{1,0:T(8,128)(2,1)S(1)}, bf16[176,1088]{1,0:T(8,128)(2,1)S(1)}, u32[]{:S(2)}, u32[]{:S(2)}) collective-permute-start(bf16[176,1088]{1,0:T(8,128)(2,1)S(1)} %get-tuple-element.133.refs_1_), channel_id=1, source_target_pairs={{0,8},{4,12},{8,0},{12,4},{1,9},{5,13},{9,1},{13,5},{2,10},{6,14},... | collective-permute-start | bytes 1148936 | tf_op jit(solution)/shard_map/ppermute | solution.py:62
  84.9 19.5 %collective-permute-start.21 = (bf16[176,1088]{1,0:T(8,128)(2,1)S(1)}, bf16[176,1088]{1,0:T(8,128)(2,1)S(1)}, u32[]{:S(2)}, u32[]{:S(2)}) collective-permute-start(bf16[176,1088]{1,0:T(8,128)(2,1)S(1)} %get-tuple-element.133.refs_1_), channel_id=1, source_target_pairs={{0,4},{4,0},{8,12},{12,8},{1,5},{5,1},{9,13},{13,9},{2,6},{6,2},{1... | collective-permute-start | bytes 1148936 | tf_op jit(solution)/shard_map/ppermute | solution.py:62
  96.9 9.9 %all-to-all-start = ((bf16[8,128,128]{2,1,0:T(8,128)(2,1)}), bf16[8,128,128]{2,1,0:T(8,128)(2,1)S(1)}, u32[]{:S(2)}, u32[]{:S(2)}) async-start(bf16[8,128,128]{2,1,0:T(8,128)(2,1)} %get-tuple-element.131.refs_9_), calls=%async_computation | async-start | bytes 524288 | tf_op jit(solution)/shard_map/all_to_all | solution.py:859
  100.3 185.0 %reduce-scatter.5.cloned.1.call-start = ((), (), s32[]{:S(2)}) async-start(), calls=%async_computation.6 | async-start | bytes 3133440 | tf_op jit(solution)/shard_map/reduce_scatter | solution.py:943
  108.8 13.0 %collective-permute-start.37 = (bf16[128,1088]{1,0:T(8,128)(2,1)S(1)}, bf16[128,1088]{1,0:T(8,128)(2,1)S(1)}, u32[]{:S(2)}, u32[]{:S(2)}) collective-permute-start(bf16[128,1088]{1,0:T(8,128)(2,1)S(1)} %take_tokens.1.refs_5_.refs_1_.refs_4_.refs_6_), channel_id=1, source_target_pairs={{0,12},{4,8},{8,4},{12,0},{1,13},{5,9},{9,5},{13,1},{2,14},{6,10},... | collective-permute-start | bytes 835592 | tf_op jit(solution)/shard_map/ppermute | solution.py:62
  109.8 16.1 %collective-permute-start.36 = (bf16[128,1088]{1,0:T(8,128)(2,1)S(1)}, bf16[128,1088]{1,0:T(8,128)(2,1)S(1)}, u32[]{:S(2)}, u32[]{:S(2)}) collective-permute-start(bf16[128,1088]{1,0:T(8,128)(2,1)S(1)} %take_tokens.1.refs_5_.refs_1_.refs_4_.refs_6_), channel_id=1, source_target_pairs={{0,8},{4,12},{8,0},{12,4},{1,9},{5,13},{9,1},{13,5},{2,10},{6,14},... | collective-permute-start | bytes 835592 | tf_op jit(solution)/shard_map/ppermute | solution.py:62
  111.0 15.0 %collective-permute-start.35 = (bf16[128,1088]{1,0:T(8,128)(2,1)S(1)}, bf16[128,1088]{1,0:T(8,128)(2,1)S(1)}, u32[]{:S(2)}, u32[]{:S(2)}) collective-permute-start(bf16[128,1088]{1,0:T(8,128)(2,1)S(1)} %take_tokens.1.refs_5_.refs_1_.refs_4_.refs_6_), channel_id=1, source_target_pairs={{0,4},{4,0},{8,12},{12,8},{1,5},{5,1},{9,13},{13,9},{2,6},{6,2},{1... | collective-permute-start | bytes 835592 | tf_op jit(solution)/shard_map/ppermute | solution.py:62
  119.6 12.6 %collective-permute-start.30 = (bf16[128,1088]{1,0:T(8,128)(2,1)}, bf16[128,1088]{1,0:T(8,128)(2,1)S(1)}, u32[]{:S(2)}, u32[]{:S(2)}) collective-permute-start(bf16[128,1088]{1,0:T(8,128)(2,1)} %get-tuple-element.142.refs_5_.refs_10_.refs_1_), channel_id=1, source_target_pairs={{0,12},{4,8},{8,4},{12,0},{1,13},{5,9},{9,5},{13,1},{2,14},{6,10},... | collective-permute-start | bytes 835592 | tf_op jit(solution)/shard_map/ppermute | solution.py:62
  120.7 17.2 %collective-permute-start.29 = (bf16[128,1088]{1,0:T(8,128)(2,1)}, bf16[128,1088]{1,0:T(8,128)(2,1)}, u32[]{:S(2)}, u32[]{:S(2)}) collective-permute-start(bf16[128,1088]{1,0:T(8,128)(2,1)} %get-tuple-element.142.refs_5_.refs_10_.refs_1_), channel_id=1, source_target_pairs={{0,8},{4,12},{8,0},{12,4},{1,9},{5,13},{9,1},{13,5},{2,10},{6,14},... | collective-permute-start | bytes 835592 | tf_op jit(solution)/shard_map/ppermute | solution.py:62
  121.8 16.1 %collective-permute-start.28 = (bf16[128,1088]{1,0:T(8,128)(2,1)}, bf16[128,1088]{1,0:T(8,128)(2,1)}, u32[]{:S(2)}, u32[]{:S(2)}) collective-permute-start(bf16[128,1088]{1,0:T(8,128)(2,1)} %get-tuple-element.142.refs_5_.refs_10_.refs_1_), channel_id=1, source_target_pairs={{0,4},{4,0},{8,12},{12,8},{1,5},{5,1},{9,13},{13,9},{2,6},{6,2},{1... | collective-permute-start | bytes 835592 | tf_op jit(solution)/shard_map/ppermute | solution.py:62
  126.7 11.6 %collective-permute-start.38 = (bf16[128,1088]{1,0:T(8,128)(2,1)S(1)}, bf16[128,1088]{1,0:T(8,128)(2,1)S(1)}, u32[]{:S(2)}, u32[]{:S(2)}) collective-permute-start(bf16[128,1088]{1,0:T(8,128)(2,1)S(1)} %get-tuple-element.143), channel_id=1, source_target_pairs={{0,16},{16,0},{1,17},{17,1},{2,18},{18,2},{3,19},{19,3},{4,20},{20... | collective-permute-start | bytes 835592 | tf_op jit(solution)/shard_map/ppermute | solution.py:58
  126.7 11.7 %collective-permute-start.39 = (bf16[128,1088]{1,0:T(8,128)(2,1)S(1)}, bf16[128,1088]{1,0:T(8,128)(2,1)S(1)}, u32[]{:S(2)}, u32[]{:S(2)}) collective-permute-start(bf16[128,1088]{1,0:T(8,128)(2,1)S(1)} %get-tuple-element.144), channel_id=1, source_target_pairs={{0,16},{16,0},{1,17},{17,1},{2,18},{18,2},{3,19},{19,3},{4,20},{20... | collective-permute-start | bytes 835592 | tf_op jit(solution)/shard_map/ppermute | solution.py:58
  179.2 11.6 %collective-permute-start.46 = (bf16[128,1088]{1,0:T(8,128)(2,1)}, bf16[128,1088]{1,0:T(8,128)(2,1)S(1)}, u32[]{:S(2)}, u32[]{:S(2)}) collective-permute-start(bf16[128,1088]{1,0:T(8,128)(2,1)} %get-tuple-element.154), channel_id=1, source_target_pairs={{0,4},{4,0},{8,12},{12,8},{1,5},{5,1},{9,13},{13,9},{2,6},{6,2},{1... | collective-permute-start | bytes 835592 | tf_op jit(solution)/shard_map/ppermute | solution.py:62
  179.9 15.3 %collective-permute-start.47 = (bf16[128,1088]{1,0:T(8,128)(2,1)}, bf16[128,1088]{1,0:T(8,128)(2,1)S(1)}, u32[]{:S(2)}, u32[]{:S(2)}) collective-permute-start(bf16[128,1088]{1,0:T(8,128)(2,1)} %get-tuple-element.155), channel_id=1, source_target_pairs={{0,8},{4,12},{8,0},{12,4},{1,9},{5,13},{9,1},{13,5},{2,10},{6,14},... | collective-permute-start | bytes 835592 | tf_op jit(solution)/shard_map/ppermute | solution.py:62
  180.7 14.5 %collective-permute-start.48 = (bf16[128,1088]{1,0:T(8,128)(2,1)S(1)}, bf16[128,1088]{1,0:T(8,128)(2,1)S(1)}, u32[]{:S(2)}, u32[]{:S(2)}) collective-permute-start(bf16[128,1088]{1,0:T(8,128)(2,1)S(1)} %get-tuple-element.156), channel_id=1, source_target_pairs={{0,12},{4,8},{8,4},{12,0},{1,13},{5,9},{9,5},{13,1},{2,14},{6,10},... | collective-permute-start | bytes 835592 | tf_op jit(solution)/shard_map/ppermute | solution.py:62
  190.3 15.0 %collective-permute-start.49 = (bf16[128,1088]{1,0:T(8,128)(2,1)}, bf16[128,1088]{1,0:T(8,128)(2,1)S(1)}, u32[]{:S(2)}, u32[]{:S(2)}) collective-permute-start(bf16[128,1088]{1,0:T(8,128)(2,1)} %get-tuple-element.171), channel_id=1, source_target_pairs={{0,16},{16,0},{1,17},{17,1},{2,18},{18,2},{3,19},{19,3},{4,20},{20... | collective-permute-start | bytes 835592 | tf_op jit(solution)/shard_map/ppermute | solution.py:58
  190.3 15.5 %collective-permute-start.50 = (bf16[128,1088]{1,0:T(8,128)(2,1)}, bf16[128,1088]{1,0:T(8,128)(2,1)}, u32[]{:S(2)}, u32[]{:S(2)}) collective-permute-start(bf16[128,1088]{1,0:T(8,128)(2,1)} %get-tuple-element.172), channel_id=1, source_target_pairs={{0,16},{16,0},{1,17},{17,1},{2,18},{18,2},{3,19},{19,3},{4,20},{20... | collective-permute-start | bytes 835592 | tf_op jit(solution)/shard_map/ppermute | solution.py:58
  190.8 15.2 %collective-permute-start.51 = (bf16[128,1088]{1,0:T(8,128)(2,1)}, bf16[128,1088]{1,0:T(8,128)(2,1)}, u32[]{:S(2)}, u32[]{:S(2)}) collective-permute-start(bf16[128,1088]{1,0:T(8,128)(2,1)} %get-tuple-element.173), channel_id=1, source_target_pairs={{0,16},{16,0},{1,17},{17,1},{2,18},{18,2},{3,19},{19,3},{4,20},{20... | collective-permute-start | bytes 835592 | tf_op jit(solution)/shard_map/ppermute | solution.py:58
  195.2 10.9 %collective-permute-start.52 = (bf16[128,1088]{1,0:T(8,128)(2,1)}, bf16[128,1088]{1,0:T(8,128)(2,1)}, u32[]{:S(2)}, u32[]{:S(2)}) collective-permute-start(bf16[128,1088]{1,0:T(8,128)(2,1)} %get-tuple-element.174), channel_id=1, source_target_pairs={{0,16},{16,0},{1,17},{17,1},{2,18},{18,2},{3,19},{19,3},{4,20},{20... | collective-permute-start | bytes 835592 | tf_op jit(solution)/shard_map/ppermute | solution.py:58
  199.0 10.1 %all-to-all-start.1 = ((bf16[8,128,128]{2,1,0:T(8,128)(2,1)}), bf16[8,128,128]{2,1,0:T(8,128)(2,1)S(1)}, u32[]{:S(2)}, u32[]{:S(2)}) async-start(bf16[8,128,128]{2,1,0:T(8,128)(2,1)} %get-tuple-element.161), calls=%async_computation.1 | async-start | bytes 524288 | tf_op jit(solution)/shard_map/all_to_all | solution.py:958
  202.4 98.5 %reduce-scatter.3.cloned.1.call-start = ((), (), s32[]{:S(2)}) async-start(), calls=%async_computation.5 | async-start | bytes 1474560 | tf_op jit(solution)/shard_map/reduce_scatter | solution.py:991
  202.5 24.9 %collective-permute-start.69 = (bf16[128,1088]{1,0:T(8,128)(2,1)S(1)}, bf16[128,1088]{1,0:T(8,128)(2,1)S(1)}, u32[]{:S(2)}, u32[]{:S(2)}) collective-permute-start(bf16[128,1088]{1,0:T(8,128)(2,1)S(1)} %get-tuple-element.196.refs_1_), channel_id=1, source_target_pairs={{0,12},{4,8},{8,4},{12,0},{1,13},{5,9},{9,5},{13,1},{2,14},{6,10},... | collective-permute-start | bytes 835592 | tf_op jit(solution)/shard_map/ppermute | solution.py:62
  205.3 22.6 %collective-permute-start.68 = (bf16[128,1088]{1,0:T(8,128)(2,1)S(1)}, bf16[128,1088]{1,0:T(8,128)(2,1)S(1)}, u32[]{:S(2)}, u32[]{:S(2)}) collective-permute-start(bf16[128,1088]{1,0:T(8,128)(2,1)S(1)} %get-tuple-element.196.refs_1_), channel_id=1, source_target_pairs={{0,8},{4,12},{8,0},{12,4},{1,9},{5,13},{9,1},{13,5},{2,10},{6,14},... | collective-permute-start | bytes 835592 | tf_op jit(solution)/shard_map/ppermute | solution.py:62
  205.8 22.1 %collective-permute-start.67 = (bf16[128,1088]{1,0:T(8,128)(2,1)S(1)}, bf16[128,1088]{1,0:T(8,128)(2,1)S(1)}, u32[]{:S(2)}, u32[]{:S(2)}) collective-permute-start(bf16[128,1088]{1,0:T(8,128)(2,1)S(1)} %get-tuple-element.196.refs_1_), channel_id=1, source_target_pairs={{0,4},{4,0},{8,12},{12,8},{1,5},{5,1},{9,13},{13,9},{2,6},{6,2},{1... | collective-permute-start | bytes 835592 | tf_op jit(solution)/shard_map/ppermute | solution.py:62
  229.6 10.4 %collective-permute-start.71 = (bf16[128,1088]{1,0:T(8,128)(2,1)S(1)}, bf16[128,1088]{1,0:T(8,128)(2,1)}, u32[]{:S(2)}, u32[]{:S(2)}) collective-permute-start(bf16[128,1088]{1,0:T(8,128)(2,1)S(1)} %collective-permute-done.67.refs_2_), channel_id=1, source_target_pairs={{0,16},{16,0},{1,17},{17,1},{2,18},{18,2},{3,19},{19,3},{4,20},{20... | collective-permute-start | bytes 835592 | tf_op jit(solution)/shard_map/ppermute | solution.py:58
  234.0 10.1 %collective-permute-start.57 = (bf16[128,1088]{1,0:T(8,128)(2,1)}, bf16[128,1088]{1,0:T(8,128)(2,1)S(1)}, u32[]{:S(2)}, u32[]{:S(2)}) collective-permute-start(bf16[128,1088]{1,0:T(8,128)(2,1)} %get-tuple-element.182), channel_id=1, source_target_pairs={{0,4},{4,0},{8,12},{12,8},{1,5},{5,1},{9,13},{13,9},{2,6},{6,2},{1... | collective-permute-start | bytes 835592 | tf_op jit(solution)/shard_map/ppermute | solution.py:62
  235.6 16.4 %collective-permute-start.58 = (bf16[128,1088]{1,0:T(8,128)(2,1)}, bf16[128,1088]{1,0:T(8,128)(2,1)S(1)}, u32[]{:S(2)}, u32[]{:S(2)}) collective-permute-start(bf16[128,1088]{1,0:T(8,128)(2,1)} %get-tuple-element.183), channel_id=1, source_target_pairs={{0,8},{4,12},{8,0},{12,4},{1,9},{5,13},{9,1},{13,5},{2,10},{6,14},... | collective-permute-start | bytes 835592 | tf_op jit(solution)/shard_map/ppermute | solution.py:62
  237.0 15.0 %collective-permute-start.59 = (bf16[128,1088]{1,0:T(8,128)(2,1)}, bf16[128,1088]{1,0:T(8,128)(2,1)}, u32[]{:S(2)}, u32[]{:S(2)}) collective-permute-start(bf16[128,1088]{1,0:T(8,128)(2,1)} %get-tuple-element.184), channel_id=1, source_target_pairs={{0,12},{4,8},{8,4},{12,0},{1,13},{5,9},{9,5},{13,1},{2,14},{6,10},... | collective-permute-start | bytes 835592 | tf_op jit(solution)/shard_map/ppermute | solution.py:62
  239.1 28.5 %collective-permute-start.60 = (bf16[128,1088]{1,0:T(8,128)(2,1)S(1)}, bf16[128,1088]{1,0:T(8,128)(2,1)}, u32[]{:S(2)}, u32[]{:S(2)}) collective-permute-start(bf16[128,1088]{1,0:T(8,128)(2,1)S(1)} %get-tuple-element.185), channel_id=1, source_target_pairs={{0,4},{4,0},{8,12},{12,8},{1,5},{5,1},{9,13},{13,9},{2,6},{6,2},{1... | collective-permute-start | bytes 835592 | tf_op jit(solution)/shard_map/ppermute | solution.py:62
  240.0 27.6 %collective-permute-start.61 = (bf16[128,1088]{1,0:T(8,128)(2,1)S(1)}, bf16[128,1088]{1,0:T(8,128)(2,1)}, u32[]{:S(2)}, u32[]{:S(2)}) collective-permute-start(bf16[128,1088]{1,0:T(8,128)(2,1)S(1)} %get-tuple-element.186), channel_id=1, source_target_pairs={{0,8},{4,12},{8,0},{12,4},{1,9},{5,13},{9,1},{13,5},{2,10},{6,14},... | collective-permute-start | bytes 835592 | tf_op jit(solution)/shard_map/ppermute | solution.py:62
  244.1 23.5 %collective-permute-start.62 = (bf16[128,1088]{1,0:T(8,128)(2,1)S(1)}, bf16[128,1088]{1,0:T(8,128)(2,1)}, u32[]{:S(2)}, u32[]{:S(2)}) collective-permute-start(bf16[128,1088]{1,0:T(8,128)(2,1)S(1)} %get-tuple-element.187), channel_id=1, source_target_pairs={{0,12},{4,8},{8,4},{12,0},{1,13},{5,9},{9,5},{13,1},{2,14},{6,10},... | collective-permute-start | bytes 835592 | tf_op jit(solution)/shard_map/ppermute | solution.py:62
  261.6 29.3 %all-to-all-start.2 = ((bf16[8,136,384]{2,1,0:T(8,128)(2,1)}), bf16[8,136,384]{2,1,0:T(8,128)(2,1)S(1)}, u32[]{:S(2)}, u32[]{:S(2)}) async-start(bf16[8,136,384]{2,1,0:T(8,128)(2,1)} %get-tuple-element.207), calls=%async_computation.4 | async-start | bytes 1671168 | tf_op jit(solution)/shard_map/all_to_all | solution.py:1010
  265.6 19.6 %collective-permute-start.75 = (f32[12,1088]{1,0:T(8,128)S(1)}, f32[12,1088]{1,0:T(8,128)S(1)}, u32[]{:S(2)}, u32[]{:S(2)}) collective-permute-start(f32[12,1088]{1,0:T(8,128)S(1)} %add.17), channel_id=1, source_target_pairs={{0,4},{4,0},{8,12},{12,8},{1,5},{5,1},{9,13},{13,9},{2,6},{6,2},{1... | collective-permute-start | bytes 156680 | tf_op jit(solution)/shard_map/ppermute | solution.py:62
  273.6 13.7 %collective-permute-start.63 = (bf16[2,272,128]{2,1,0:T(8,128)(2,1)S(1)}, bf16[2,272,128]{2,1,0:T(8,128)(2,1)S(1)}, u32[]{:S(2)}, u32[]{:S(2)}) collective-permute-start(bf16[2,272,128]{2,1,0:T(8,128)(2,1)S(1)} %get-tuple-element.189), channel_id=1, source_target_pairs={{0,0},{8,1},{16,2},{24,3},{2,4},{10,5},{18,6},{26,7},{4,8},{12,9},... | collective-permute-start | bytes 417800 | tf_op jit(solution)/shard_map/ppermute | solution.py:1043
  274.3 13.9 %collective-permute-start.64 = (bf16[2,272,128]{2,1,0:T(8,128)(2,1)S(1)}, bf16[2,272,128]{2,1,0:T(8,128)(2,1)S(1)}, u32[]{:S(2)}, u32[]{:S(2)}) collective-permute-start(bf16[2,272,128]{2,1,0:T(8,128)(2,1)S(1)} %get-tuple-element.190), channel_id=1, source_target_pairs={{2,0},{10,1},{18,2},{26,3},{0,4},{8,5},{16,6},{24,7},{6,8},{14,9},... | collective-permute-start | bytes 417800 | tf_op jit(solution)/shard_map/ppermute | solution.py:1043
  278.5 10.9 %collective-permute-start.65 = (bf16[2,272,128]{2,1,0:T(8,128)(2,1)S(1)}, bf16[2,272,128]{2,1,0:T(8,128)(2,1)S(1)}, u32[]{:S(2)}, u32[]{:S(2)}) collective-permute-start(bf16[2,272,128]{2,1,0:T(8,128)(2,1)S(1)} %get-tuple-element.191), channel_id=1, source_target_pairs={{4,0},{12,1},{20,2},{28,3},{6,4},{14,5},{22,6},{30,7},{0,8},{8,9},... | collective-permute-start | bytes 417800 | tf_op jit(solution)/shard_map/ppermute | solution.py:1043
  280.4 12.6 %collective-permute-start.66 = (bf16[2,272,128]{2,1,0:T(8,128)(2,1)}, bf16[2,272,128]{2,1,0:T(8,128)(2,1)S(1)}, u32[]{:S(2)}, u32[]{:S(2)}) collective-permute-start(bf16[2,272,128]{2,1,0:T(8,128)(2,1)} %get-tuple-element.192), channel_id=1, source_target_pairs={{6,0},{14,1},{22,2},{30,3},{4,4},{12,5},{20,6},{28,7},{2,8},{10,9}... | collective-permute-start | bytes 417800 | tf_op jit(solution)/shard_map/ppermute | solution.py:1043
  285.2 12.6 %collective-permute-start.76 = (f32[12,1088]{1,0:T(8,128)S(1)}, f32[12,1088]{1,0:T(8,128)S(1)}, u32[]{:S(2)}, u32[]{:S(2)}) collective-permute-start(f32[12,1088]{1,0:T(8,128)S(1)} %add.18.refs_1_), channel_id=1, source_target_pairs={{0,8},{4,12},{8,0},{12,4},{1,9},{5,13},{9,1},{13,5},{2,10},{6,14},... | collective-permute-start | bytes 156680 | tf_op jit(solution)/shard_map/ppermute | solution.py:62
  287.3 13.6 %collective-permute-start.77 = (bf16[2,136,272]{2,1,0:T(8,128)(2,1)S(1)}, bf16[2,136,272]{2,1,0:T(8,128)(2,1)S(1)}, u32[]{:S(2)}, u32[]{:S(2)}) collective-permute-start(bf16[2,136,272]{2,1,0:T(8,128)(2,1)S(1)} %get-tuple-element.204), channel_id=1, source_target_pairs={{0,4},{4,0},{8,12},{12,8},{1,5},{5,1},{9,13},{13,9},{2,6},{6,2},{1... | collective-permute-start | bytes 443912 | tf_op jit(solution)/shard_map/ppermute | solution.py:62
  288.1 12.8 %collective-permute-start.78 = (bf16[2,136,272]{2,1,0:T(8,128)(2,1)S(1)}, bf16[2,136,272]{2,1,0:T(8,128)(2,1)S(1)}, u32[]{:S(2)}, u32[]{:S(2)}) collective-permute-start(bf16[2,136,272]{2,1,0:T(8,128)(2,1)S(1)} %get-tuple-element.205), channel_id=1, source_target_pairs={{0,8},{4,12},{8,0},{12,4},{1,9},{5,13},{9,1},{13,5},{2,10},{6,14},... | collective-permute-start | bytes 443912 | tf_op jit(solution)/shard_map/ppermute | solution.py:62
  289.4 11.5 %collective-permute-start.79 = (bf16[2,136,272]{2,1,0:T(8,128)(2,1)S(1)}, bf16[2,136,272]{2,1,0:T(8,128)(2,1)S(1)}, u32[]{:S(2)}, u32[]{:S(2)}) collective-permute-start(bf16[2,136,272]{2,1,0:T(8,128)(2,1)S(1)} %get-tuple-element.206), channel_id=1, source_target_pairs={{0,12},{4,8},{8,4},{12,0},{1,13},{5,9},{9,5},{13,1},{2,14},{6,10},... | collective-permute-start | bytes 443912 | tf_op jit(solution)/shard_map/ppermute | solution.py:62
  293.0 13.6 %collective-permute-start.89 = (bf16[136,336]{1,0:T(8,128)(2,1)S(1)}, bf16[136,336]{1,0:T(8,128)(2,1)S(1)}, u32[]{:S(2)}, u32[]{:S(2)}) collective-permute-start(bf16[136,336]{1,0:T(8,128)(2,1)S(1)} %get-tuple-element.213), channel_id=1, source_target_pairs={{0,1},{1,2},{2,3},{3,0},{4,5},{5,6},{6,7},{7,4},{8,9},{9,10},{10,1... | collective-permute-start | bytes 274184 | tf_op jit(solution)/shard_map/ppermute | solution.py:66
  297.8 10.9 %collective-permute-start.90 = (bf16[136,336]{1,0:T(8,128)(2,1)S(1)}, bf16[136,336]{1,0:T(8,128)(2,1)S(1)}, u32[]{:S(2)}, u32[]{:S(2)}) collective-permute-start(bf16[136,336]{1,0:T(8,128)(2,1)S(1)} %get-tuple-element.214), channel_id=1, source_target_pairs={{0,2},{1,3},{2,0},{3,1},{4,6},{5,7},{6,4},{7,5},{8,10},{9,11},{10,... | collective-permute-start | bytes 274184 | tf_op jit(solution)/shard_map/ppermute | solution.py:66
  303.2 10.0 %collective-permute-start.80 = (f32[12,1088]{1,0:T(8,128)S(1)}, f32[12,1088]{1,0:T(8,128)S(1)}, u32[]{:S(2)}, u32[]{:S(2)}) collective-permute-start(f32[12,1088]{1,0:T(8,128)S(1)} %add_two.1), channel_id=1, source_target_pairs={{0,1},{1,0},{2,3},{3,2},{4,5},{5,4},{6,7},{7,6},{8,9},{9,8},{10,11... | collective-permute-start | bytes 156680 | tf_op jit(solution)/shard_map/ppermute | solution.py:1087
  310.8 15.2 %collective-permute-start.93 = (bf16[2,136,272]{2,1,0:T(8,128)(2,1)S(1)}, bf16[2,136,272]{2,1,0:T(8,128)(2,1)S(1)}, u32[]{:S(2)}, u32[]{:S(2)}) collective-permute-start(bf16[2,136,272]{2,1,0:T(8,128)(2,1)S(1)} %get-tuple-element.216.refs_1_), channel_id=1, source_target_pairs={{0,16},{16,0},{1,17},{17,1},{2,18},{18,2},{3,19},{19,3},{4,20},{20... | collective-permute-start | bytes 443912 | tf_op jit(solution)/shard_map/ppermute | solution.py:58
  (127 other events, 758.9 us)
Sparse Core Ops, SparseCore 0:
  82.9 51.1 all-gather.2
  179.3 48.4 reduce-scatter.4
  239.2 27.3 reduce-scatter.2

commit v2 on v1

--- a/solution.py
+++ b/solution.py
@@ -33,7 +33,7 @@
     return math.prod(shape[:-2]) * lines * (-(-shape[-1] // 128) * 128) * size
 
 
-def kernel(body, outs, scratch, ids, *arrays, us=1.0, work=2, after=(), far=False):
+def kernel(body, outs, scratch, ids, *arrays, us=0.2, work=2, after=(), far=False):
     count, late = len(arrays), len(after)
 
     def run(*refs):
@@ -787,15 +787,15 @@
     first = windows[0]
     windows = peers(windows)
     sent = kernel(
-        send_tokens, [block] * 4, [], ids, hidden_in.transpose(0, 2, 1), cotangent.transpose(0, 2, 1), us=1.0, after=(first,)
+        send_tokens, [block] * 4, [], ids, hidden_in.transpose(0, 2, 1), cotangent.transpose(0, 2, 1), us=0.5, after=(first,)
     )
     blocks = [lax.ppermute(sent[m], EVERY, MOVES[m]) for m in range(4)]
     lines = TALL + 3 * 16
     out_piece = kernel(
-        out_half, [((lines, quarter), BF)], [((cols, quarter), F32)], ids, w_out, w_qkv, us=1.0, after=(sent[0],)
+        out_half, [((lines, quarter), BF)], [((cols, quarter), F32)], ids, w_out, w_qkv, us=0.2, after=(sent[0],)
     )
     piece = ((WINDOW + lines // 4, width), BF)
-    joined = kernel(join_lanes, [piece], [((4, WINDOW, quarter), BF)], ids, *windows, out_piece, us=1.0)
+    joined = kernel(join_lanes, [piece], [((4, WINDOW, quarter), BF)], ids, *windows, out_piece, us=1)
     joined = shifted([joined] * 4)
     *mlp_sent, up_bias_own = kernel(
         mlp_blocks,
@@ -805,7 +805,7 @@
         w_up,
         w_down.T,
         up_bias.astype(F32).reshape(4, 8, part),
-        us=2.0,
+        us=2,
         after=(joined[0],),
     )
     mlp_got = peers(mlp_sent)
@@ -814,7 +814,7 @@
     )
     n1 = gather_plane(n1_own)
     g_own = kernel(
-        take_tokens, [own_bf], [held_tokens], ids, *blocks, us=1.0, after=(n1_own,)
+        take_tokens, [own_bf], [held_tokens], ids, *blocks, us=1, after=(n1_own,)
     )
     g_near = gather_near(g_own)
     w_own, out_row = kernel(
@@ -823,7 +823,7 @@
         [((4, *piece[0]), BF), ((3 * PAIR + WINDOW, width), BF)],
         ids,
         *joined,
-        us=1.0,
+        us=1,
         after=(g_own,),
     )
     mlp_part = kernel(
@@ -832,7 +832,7 @@
         [((4, 2, part, quarter), BF)],
         ids,
         *mlp_got,
-        us=1.0,
+        us=0.2,
         after=(w_own,),
     )
     mlp_own = lax.all_gather(mlp_part, "gy", axis=0, tiled=False)
@@ -852,7 +852,7 @@
         vectors,
         segment_ids,
         swapped_ids,
-        us=3.0,
+        us=3,
         far=True,
         after=(mlp_part,),
     )
@@ -864,7 +864,7 @@
         [((4, 3, 2, 4, 8, quarter), F32)],
         ids,
         *out_rows,
-        us=1.0,
+        us=1,
     )
     kv, qs, probs_s, att_s = kernel(
         attend_shared,
@@ -881,7 +881,7 @@
         work=6,
     )
     middle, n2_own = kernel(
-        out_norm, [own_f32, own_bf], [], ids, att_got, att_s, wo, x_own, vectors, us=0.5, work=6
+        out_norm, [own_f32, own_bf], [], ids, att_got, att_s, wo, x_own, vectors, us=0.1, work=6
     )
     g_all = gather_later(g_near, (n2_own,))
     summed = [own_f32, own_bf, own_bf, own_bf]
@@ -900,7 +900,7 @@
         ids,
         *g_all,
         mlp_own,
-        us=3.0,
+        us=12,
         far=True,
         after=(n2_own,),
     )
@@ -920,7 +920,7 @@
         mlp_own,
         grad_act,
         up_bias_own,
-        us=7.0,
+        us=1.4,
         work=14,
     )
     parts = scatter(near, far)
@@ -933,7 +933,7 @@
         grad_pre,
         n_rel,
         *g_all,
-        us=5.0,
+        us=20,
         far=True,
         after=(parts[0],),
     )
@@ -983,7 +983,7 @@
         w_own,
         w16,
         n_abs,
-        us=3.0,
+        us=3,
         far=True,
         after=(feed_parts[0],),
     )
@@ -1014,7 +1014,7 @@
         [((4, 2, part, quarter), BF)],
         ids,
         mlp_summed,
-        us=1.0,
+        us=1,
     )
     split_piece = ((half, quarter + HEAD_DIM), BF)
     out_split_parts = shifted(
@@ -1024,7 +1024,7 @@
             [((half, width), F32), ((4, half, quarter + HEAD_DIM), BF)],
             ids,
             out_got,
-            us=1.0,
+            us=1,
         )
     )
     done = kernel(
@@ -1041,7 +1041,7 @@
         us=2.5,
     )
     landed = [lax.ppermute(done[m], EVERY, BACK[m]) for m in range(4)]
-    hidden_out, grad_in = kernel(land_tokens, [((2, quarter, 2 * rows), BF)] * 2, [], ids, *landed, us=1.0)
+    hidden_out, grad_in = kernel(land_tokens, [((2, quarter, 2 * rows), BF)] * 2, [], ids, *landed, us=1)
 
     smalls = kernel(
         join_sums, [((12, width), F32)], [], ids, moments, moments_s, qkv_sums, middle_sums, up_sum, us=0.7
@@ -1051,7 +1051,7 @@
     others = from_peer(smalls, 2)
     blocks = peers(mlp_parts)
     lanes = kernel(
-        qkv_lanes, [window] * 4, [((4, WINDOW, quarter), BF)], ids, window_sum, us=1.0, after=(*landed, *blocks[1:], out_split_parts[0], others)
+        qkv_lanes, [window] * 4, [((4, WINDOW, quarter), BF)], ids, window_sum, us=0.2, after=(*landed, *blocks[1:], out_split_parts[0], others)
     )
     near = peers(lanes)
     near = [*near, *[swap_core(piece) for piece in near]]
@@ -1062,7 +1062,7 @@
         ids,
         *blocks,
         *[swap_core(piece) for piece in blocks],
-        us=2.0,
+        us=2,
         after=(lanes[0],),
     )
     mine = kernel(sum_four, [split_piece], [], ids, *out_split_parts, us=0.6, after=(lanes[0],))
@@ -1080,10 +1080,10 @@
         *near,
         mine,
         theirs,
-        us=2.0,
+        us=2,
     )
     total_qkv = over_outer(total_qkv)
-    smalls = kernel(add_two, [((12, width), F32)], [], ids, smalls, others, us=0.7, after=(lanes[0],))
+    smalls = kernel(add_two, [((12, width), F32)], [], ids, smalls, others, us=2.8, after=(lanes[0],))
     smalls = smalls + lax.ppermute(smalls, "gy", [(i, i ^ 1) for i in range(4)])
     others = lax.ppermute(smalls, "gy", [(i, i ^ 2) for i in range(4)])
     smalls, others = over_outer(smalls), over_outer(others)

time: 339 us -> 336 us (level)
  waiting for transfers between devices: 77.4 us -> 71.8 us
    ppermute x4, starting transfers between devices: 11.6 us -> 16.3 us  [shards(): landed = [lax.ppermute(done[m], EVERY, BACK[m]) for m in range(4)]]
    ppermute x6, waiting for transfers between devices: 16.8 us -> 13.3 us  [from_below(): return lax.ppermute(value, 'gy', [(i, (i + step) % 4) for i in range(4)])]
    unnamed x176 -> x190, local copies, waits for them, and re-layouts: 30.8 us -> 32.4 us
  transfers between devices with their start and end apart: 103 -> 103, of which waited for: 25 -> 27; matrix products, arithmetic and copies ran while one was open for 0% -> 0% of each run, Pallas kernels for 21% -> 21%
where the time goes in v2:
time: 336 us; the launch traced here: 332 us
  starting transfers between devices  110 us (33%)
  Pallas kernels  100 us (30%)
  waiting for transfers between devices  71.8 us (21%)
  local copies, waits for them, and re-layouts  34.7 us (10%)
  between operations  15.2 us (5%)
    pallas_call x37, Pallas kernels, kernel(): pl.pallas_call(run, name=body.__name__, out_shape=tuple((jax.ShapeDtypeSt...  100 us
    ppermute x38, waiting for transfers between devices, from_peer(): return lax.ppermute(value, 'gx', [(i, i ^ step) for i in range(4)])  46.8 us
    ppermute x38, starting transfers between devices, from_peer(): return lax.ppermute(value, 'gx', [(i, i ^ step) for i in range(4)])  45.8 us
    unnamed x190, local copies, waits for them, and re-layouts  32.4 us
    ppermute x4, starting transfers between devices, shards(): landed = [lax.ppermute(done[m], EVERY, BACK[m]) for m in range(4)]  16.3 us
    ppermute x6, starting transfers between devices, from_below(): return lax.ppermute(value, 'gy', [(i, (i + step) % 4) for i in range(4)])  14.5 us
    ppermute x6, waiting for transfers between devices, from_below(): return lax.ppermute(value, 'gy', [(i, (i + step) % 4) for i in range(4)])  13.3 us
    ppermute x43, starting transfers between devices, swap_core(): return lax.ppermute(value, 'c', [(0, 1), (1, 0)])  10.3 us
  transfers between devices with their start and end apart: 103, of which 27 were waited for; matrix products, arithmetic and copies ran while one was open for 0% of the time, Pallas kernels for 21%

profile of v2, /device:TPU:0, one launch (start us, length us, event | category | flops | bytes accessed | tf_op | source)
XLA Modules:
  0.0 332.5 jit_solution(33929020243043271)
XLA Ops:
  9.8 3.0 collective-permute-start.4
  12.8 1.5 collective-permute-start.5
  15.1 3.1 collective-permute-start.1
  19.9 2.8 collective-permute-start.2
  22.7 3.0 collective-permute-start.3
  26.4 6.4 %collective-permute-start.8 = (bf16[176,1088]{1,0:T(8,128)(2,1)S(1)}, bf16[176,1088]{1,0:T(8,128)(2,1)S(1)}, u32[]{:S(2)}, u32[]{:S(2)}) collective-permute-start(bf16[176,1088]{1,0:T(8,128)(2,1)S(1)} %join_lanes.1.refs_4_.refs_1_), channel_id=1, source_target_pairs={{0,3},{1,0},{2,1},{3,2},{4,7},{5,4},{6,5},{7,6},{8,11},{9,8},{10,9... | collective-permute-start | bytes 1148936 | tf_op jit(solution)/shard_map/ppermute | solution.py:66
  34.9 3.5 %collective-permute-start.9 = (bf16[2,136,272]{2,1,0:T(8,128)(2,1)S(1)}, bf16[2,136,272]{2,1,0:T(8,128)(2,1)S(1)}, u32[]{:S(2)}, u32[]{:S(2)}) collective-permute-start(bf16[2,136,272]{2,1,0:T(8,128)(2,1)S(1)} %get-tuple-element.125), channel_id=1, source_target_pairs={{0,4},{4,0},{8,12},{12,8},{1,5},{5,1},{9,13},{13,9},{2,6},{6,2},{1... | collective-permute-start | bytes 443912 | tf_op jit(solution)/shard_map/ppermute | solution.py:62
  38.4 1.5 collective-permute-start.11
  40.2 4.1 %collective-permute-done.9.refs_8_.refs_2_ = bf16[2,136,272]{2,1,0:T(8,128)(2,1)S(1)} collective-permute-done((bf16[2,136,272]{2,1,0:T(8,128)(2,1)S(1)}, bf16[2,136,272]{2,1,0:T(8,128)(2,1)S(1)}, u32[]{:S(2)}, u32[]{:S(2)}) %collective-permute-start.9) | collective-permute-done | bytes 148000 | tf_op jit(solution)/shard_map/ppermute | solution.py:62
  44.3 5.4 %collective-permute-done.10.refs_9_.refs_3_ = bf16[2,136,272]{2,1,0:T(8,128)(2,1)S(1)} collective-permute-done((bf16[2,136,272]{2,1,0:T(8,128)(2,1)S(1)}, bf16[2,136,272]{2,1,0:T(8,128)(2,1)S(1)}, u32[]{:S(2)}, u32[]{:S(2)}) %collective-permute-start.10) | collective-permute-done | bytes 148000 | tf_op jit(solution)/shard_map/ppermute | solution.py:62
  49.7 1.8 collective-permute-start.19
  53.3 3.0 collective-permute-start.14
  59.5 12.0 %collective-permute-done.19.refs_3_ = bf16[176,1088]{1,0:T(8,128)(2,1)S(1)} collective-permute-done((bf16[176,1088]{1,0:T(8,128)(2,1)S(1)}, bf16[176,1088]{1,0:T(8,128)(2,1)S(1)}, u32[]{:S(2)}, u32[]{:S(2)}) %collective-permute-start.19) | collective-permute-done | bytes 383008 | tf_op jit(solution)/shard_map/ppermute | solution.py:66
  73.5 1.7 mlp_join.1.refs_13_
  76.8 1.5 collective-permute-start.22
  78.3 1.5 collective-permute-start.21
  79.8 10.2 %attend.1 = (bf16[8,128,1088]{2,1,0:T(8,128)(2,1)}, bf16[1024,128]{1,0:T(8,128)(2,1)}, bf16[1024,128]{1,0:T(8,128)(2,1)}, bf16[1024,128]{1,0:T(8,128)(2,1)}, bf1...) custom-call(s32[100]{0:T(128)} %copy-done.12, bf16[128,1088]{1,0:T(8,128)(2,1)} %copy-done.24, ...), custom_call_target="tpu_custom_call" | custom-call | flops 15000000512 | bytes 300000 | tf_op jit(solution)/shard_map/attend/pallas_call | solution.py:44
  90.0 3.4 %all-to-all-start = ((bf16[8,128,128]{2,1,0:T(8,128)(2,1)}), bf16[8,128,128]{2,1,0:T(8,128)(2,1)S(1)}, u32[]{:S(2)}, u32[]{:S(2)}) async-start(bf16[8,128,128]{2,1,0:T(8,128)(2,1)} %get-tuple-element.131.refs_9_), calls=%async_computation | async-start | bytes 524288 | tf_op jit(solution)/shard_map/all_to_all | solution.py:859
  93.7 2.9 collective-permute-done.22.refs_3_
  96.6 3.3 all-to-all-done.refs_5_.refs_1_
  102.6 1.4 collective-permute-start.36
  106.7 2.1 attend_shared.1
  108.9 2.4 out_norm.1
  112.2 1.4 collective-permute-start.29
  114.9 4.1 %collective-permute-done.36.refs_3_.refs_6_ = bf16[128,1088]{1,0:T(8,128)(2,1)S(1)} collective-permute-done((bf16[128,1088]{1,0:T(8,128)(2,1)S(1)}, bf16[128,1088]{1,0:T(8,128)(2,1)S(1)}, u32[]{:S(2)}, u32[]{:S(2)}) %collective-permute-start.36) | collective-permute-done | bytes 278560 | tf_op jit(solution)/shard_map/ppermute | solution.py:62
  120.3 5.0 %collective-permute-done.30.refs_4_ = bf16[128,1088]{1,0:T(8,128)(2,1)S(1)} collective-permute-done((bf16[128,1088]{1,0:T(8,128)(2,1)}, bf16[128,1088]{1,0:T(8,128)(2,1)S(1)}, u32[]{:S(2)}, u32[]{:S(2)}) %collective-permute-start.30) | collective-permute-done | bytes 278560 | tf_op jit(solution)/shard_map/ppermute | solution.py:62
  125.3 5.5 %collective-permute-done.29.refs_3_ = bf16[128,1088]{1,0:T(8,128)(2,1)S(1)} collective-permute-done((bf16[128,1088]{1,0:T(8,128)(2,1)}, bf16[128,1088]{1,0:T(8,128)(2,1)S(1)}, u32[]{:S(2)}, u32[]{:S(2)}) %collective-permute-start.29) | collective-permute-done | bytes 278560 | tf_op jit(solution)/shard_map/ppermute | solution.py:62
  133.9 6.3 %grad_activated.1.refs_10_ = f32[1024,544]{1,0:T(8,128)} custom-call(s32[100]{0:T(128)} %copy-done.12, bf16[128,1088]{1,0:T(8,128)(2,1)} %copy-done.27, bf16[128,1088]{1,0:T(8,128)(2,1)} %copy-done.32, bf16[128,1088]{1,0:T(8,128)(2,1)} %copy-done.31, bf16[128,1088]{1,0:T(8,128)(2,1)} %copy-done.30, bf16[128,1088]{1,0:T(8,128)(2,1)} %copy-done.92, ...), custom_call_target="tpu_custom_call" | custom-call | flops 60000002048 | bytes 1200000 | tf_op jit(solution)/shard_map/grad_activated/pallas_call | solution.py:44
  140.3 1.7 copy-done.59
  142.0 6.5 %feed_forward.1 = (bf16[8,128,1088]{2,1,0:T(8,128)(2,1)S(1)}, bf16[1024,544]{1,0:T(8,128)(2,1)S(1)}, bf16[1024,544]{1,0:T(8,128)(2,1)S(1)}, f32[1,544]{1,0:T(1,1...) custom-call(s32[100]{0:T(128)S(1)} %copy-done.14, ...), custom_call_target="tpu_custom_call" | custom-call | flops 7000000000 | bytes 140000 | tf_op jit(solution)/shard_map/feed_forward/pallas_call | solution.py:44
  154.6 19.2 %mlp_grads.1.refs_9_.refs_3_ = bf16[4,2,136,1088]{3,2,1,0:T(8,128)(2,1)} custom-call(s32[100]{0:T(128)} %copy-done.12, bf16[1024,544]{1,0:T(8,128)(2,1)} %copy-done.63, bf16[1024,544]{1,0:T(8,128)(2,1)} %copy-done.65, bf16[8,128,1088]{2,1,0:T(8,128)(2,1)} %copy-done.62, bf16[128,1088]{1,0:T(8,128)(2,1)} %copy-done.27, bf16[128,1088]{1,0:T(8,128)(2,1)} %copy-done.32, ...), custom_call_target="tpu_custom_call" | custom-call | flops 99999997952 | bytes 2000000 | tf_op jit(solution)/shard_map/mlp_grads/pallas_call | solution.py:44
  173.8 1.5 collective-permute-start.46
  175.4 1.5 collective-permute-start.47
  177.4 1.9 copy-done.18
  180.6 3.3 feed_out.1
  184.5 6.2 %collective-permute-done.47.refs_3_ = bf16[128,1088]{1,0:T(8,128)(2,1)S(1)} collective-permute-done((bf16[128,1088]{1,0:T(8,128)(2,1)}, bf16[128,1088]{1,0:T(8,128)(2,1)S(1)}, u32[]{:S(2)}, u32[]{:S(2)}) %collective-permute-start.47) | collective-permute-done | bytes 278560 | tf_op jit(solution)/shard_map/ppermute | solution.py:62
  190.7 2.4 middle_back.1
  194.5 3.4 %all-to-all-start.1 = ((bf16[8,128,128]{2,1,0:T(8,128)(2,1)}), bf16[8,128,128]{2,1,0:T(8,128)(2,1)S(1)}, u32[]{:S(2)}, u32[]{:S(2)}) async-start(bf16[8,128,128]{2,1,0:T(8,128)(2,1)} %get-tuple-element.161), calls=%async_computation.1 | async-start | bytes 524288 | tf_op jit(solution)/shard_map/all_to_all | solution.py:958
  198.0 2.8 collective-permute-start.69
  201.5 3.1 all-to-all-done.1.refs_6_.refs_1_
  206.0 1.5 add_far.4
  208.4 13.9 %attend_back.1 = (bf16[1024,128]{1,0:T(8,128)(2,1)}, bf16[128,64]{1,0:T(8,128)(2,1)}, f32[8,128]{1,0:T(8,128)}, f32[2,1088]{1,0:T(2,128)}, bf16[512,1088]{1,0:T(...) custom-call(s32[100]{0:T(128)} %copy-done.12, ...), custom_call_target="tpu_custom_call" | custom-call | flops 15000000512 | bytes 300000 | tf_op jit(solution)/shard_map/attend_back/pallas_call | solution.py:44
  227.6 1.5 add_far.5
  232.7 2.2 collective-permute-start.59
  236.2 3.9 %collective-permute-done.57.refs_2_.refs_16_ = bf16[128,1088]{1,0:T(8,128)(2,1)} collective-permute-done((bf16[128,1088]{1,0:T(8,128)(2,1)}, bf16[128,1088]{1,0:T(8,128)(2,1)}, u32[]{:S(2)}, u32[]{:S(2)}) %collective-permute-start.57) | collective-permute-done | bytes 278560 | tf_op jit(solution)/shard_map/ppermute | solution.py:62
  240.8 6.9 %collective-permute-done.58.refs_3_.refs_17_ = bf16[128,1088]{1,0:T(8,128)(2,1)} collective-permute-done((bf16[128,1088]{1,0:T(8,128)(2,1)}, bf16[128,1088]{1,0:T(8,128)(2,1)}, u32[]{:S(2)}, u32[]{:S(2)}) %collective-permute-start.58) | collective-permute-done | bytes 278560 | tf_op jit(solution)/shard_map/ppermute | solution.py:62
  249.7 1.7 copy-done.54
  253.4 3.2 out_grads.1
  257.4 3.8 %all-to-all-start.2 = ((bf16[8,136,384]{2,1,0:T(8,128)(2,1)}), bf16[8,136,384]{2,1,0:T(8,128)(2,1)S(1)}, u32[]{:S(2)}, u32[]{:S(2)}) async-start(bf16[8,136,384]{2,1,0:T(8,128)(2,1)} %get-tuple-element.207), calls=%async_computation.4 | async-start | bytes 1671168 | tf_op jit(solution)/shard_map/all_to_all | solution.py:1010
  261.2 2.0 collective-permute-start.75
  266.4 2.4 finish.1
  269.5 4.2 %collective-permute-start.64 = (bf16[2,272,128]{2,1,0:T(8,128)(2,1)S(1)}, bf16[2,272,128]{2,1,0:T(8,128)(2,1)S(1)}, u32[]{:S(2)}, u32[]{:S(2)}) collective-permute-start(bf16[2,272,128]{2,1,0:T(8,128)(2,1)S(1)} %get-tuple-element.190), channel_id=1, source_target_pairs={{2,0},{10,1},{18,2},{26,3},{0,4},{8,5},{16,6},{24,7},{6,8},{14,9},... | collective-permute-start | bytes 417800 | tf_op jit(solution)/shard_map/ppermute | solution.py:1043
  273.7 2.4 collective-permute-start.65
  276.1 9.0 %collective-permute-start.66 = (bf16[2,272,128]{2,1,0:T(8,128)(2,1)S(1)}, bf16[2,272,128]{2,1,0:T(8,128)(2,1)S(1)}, u32[]{:S(2)}, u32[]{:S(2)}) collective-permute-start(bf16[2,272,128]{2,1,0:T(8,128)(2,1)S(1)} %get-tuple-element.192), channel_id=1, source_target_pairs={{6,0},{14,1},{22,2},{30,3},{4,4},{12,5},{20,6},{28,7},{2,8},{10,9}... | collective-permute-start | bytes 417800 | tf_op jit(solution)/shard_map/ppermute | solution.py:1043
  287.9 1.5 collective-permute-start.78
  289.4 1.4 collective-permute-start.79
  290.9 1.5 out_split.1
  294.2 4.0 %collective-permute-start.90 = (bf16[136,336]{1,0:T(8,128)(2,1)S(1)}, bf16[136,336]{1,0:T(8,128)(2,1)S(1)}, u32[]{:S(2)}, u32[]{:S(2)}) collective-permute-start(bf16[136,336]{1,0:T(8,128)(2,1)S(1)} %get-tuple-element.214), channel_id=1, source_target_pairs={{0,2},{1,3},{2,0},{3,1},{4,6},{5,7},{6,4},{7,5},{8,10},{9,11},{10,... | collective-permute-start | bytes 274184 | tf_op jit(solution)/shard_map/ppermute | solution.py:66
  303.5 1.9 collective-permute-start.80
  306.7 1.4 land_tokens.1
  310.9 1.4 collective-permute-start.84
  313.3 1.5 out_land.1
  320.7 2.2 qkv_land.1
  322.9 2.8 mlp_land.1
  (390 shorter events, 81.5 us)
Async XLA Ops:
  7.2 126.7 %all-gather.3.cloned.1.call-start = ((), (), s32[]{:S(2)}) async-start(), calls=%async_computation.7 | async-start | bytes 3133440 | tf_op jit(solution)/shard_map/all_gather | solution.py:838
  9.8 10.0 %collective-permute-start.4 = (bf16[128,272]{1,0:T(8,128)(2,1)S(1)}, bf16[128,272]{1,0:T(8,128)(2,1)S(1)}, u32[]{:S(2)}, u32[]{:S(2)}) collective-permute-start(bf16[128,272]{1,0:T(8,128)(2,1)S(1)} %get-tuple-element.122), channel_id=1, source_target_pairs={{0,4},{4,0},{8,12},{12,8},{1,5},{5,1},{9,13},{13,9},{2,6},{6,2},{1... | collective-permute-start | bytes 208904 | tf_op jit(solution)/shard_map/ppermute | solution.py:62
  12.8 9.8 %collective-permute-start.5 = (bf16[128,272]{1,0:T(8,128)(2,1)S(1)}, bf16[128,272]{1,0:T(8,128)(2,1)S(1)}, u32[]{:S(2)}, u32[]{:S(2)}) collective-permute-start(bf16[128,272]{1,0:T(8,128)(2,1)S(1)} %get-tuple-element.123), channel_id=1, source_target_pairs={{0,8},{4,12},{8,0},{12,4},{1,9},{5,13},{9,1},{13,5},{2,10},{6,14},... | collective-permute-start | bytes 208904 | tf_op jit(solution)/shard_map/ppermute | solution.py:62
  14.4 11.3 %collective-permute-start.6 = (bf16[128,272]{1,0:T(8,128)(2,1)S(1)}, bf16[128,272]{1,0:T(8,128)(2,1)S(1)}, u32[]{:S(2)}, u32[]{:S(2)}) collective-permute-start(bf16[128,272]{1,0:T(8,128)(2,1)S(1)} %get-tuple-element.124), channel_id=1, source_target_pairs={{0,12},{4,8},{8,4},{12,0},{1,13},{5,9},{9,5},{13,1},{2,14},{6,10},... | collective-permute-start | bytes 208904 | tf_op jit(solution)/shard_map/ppermute | solution.py:62
  15.1 17.8 %collective-permute-start.1 = (bf16[2,272,128]{2,1,0:T(8,128)(2,1)S(1)}, bf16[2,272,128]{2,1,0:T(8,128)(2,1)S(1)}, u32[]{:S(2)}, u32[]{:S(2)}) collective-permute-start(bf16[2,272,128]{2,1,0:T(8,128)(2,1)S(1)} %get-tuple-element.119), channel_id=1, source_target_pairs={{0,2},{1,10},{2,18},{3,26},{4,0},{5,8},{6,16},{7,24},{8,6},{9,14},... | collective-permute-start | bytes 417800 | tf_op jit(solution)/shard_map/ppermute | solution.py:792
  18.2 20.2 %collective-permute-start = (bf16[2,272,128]{2,1,0:T(8,128)(2,1)S(1)}, bf16[2,272,128]{2,1,0:T(8,128)(2,1)S(1)}, u32[]{:S(2)}, u32[]{:S(2)}) collective-permute-start(bf16[2,272,128]{2,1,0:T(8,128)(2,1)S(1)} %get-tuple-element.118.refs_3_), channel_id=1, source_target_pairs={{0,0},{1,8},{2,16},{3,24},{4,2},{5,10},{6,18},{7,26},{8,4},{9,12},... | collective-permute-start | bytes 417800 | tf_op jit(solution)/shard_map/ppermute | solution.py:792
  19.9 15.0 %collective-permute-start.2 = (bf16[2,272,128]{2,1,0:T(8,128)(2,1)S(1)}, bf16[2,272,128]{2,1,0:T(8,128)(2,1)S(1)}, u32[]{:S(2)}, u32[]{:S(2)}) collective-permute-start(bf16[2,272,128]{2,1,0:T(8,128)(2,1)S(1)} %get-tuple-element.120), channel_id=1, source_target_pairs={{0,4},{1,12},{2,20},{3,28},{4,6},{5,14},{6,22},{7,30},{8,0},{9,8},... | collective-permute-start | bytes 417800 | tf_op jit(solution)/shard_map/ppermute | solution.py:792
  22.7 15.7 %collective-permute-start.3 = (bf16[2,272,128]{2,1,0:T(8,128)(2,1)S(1)}, bf16[2,272,128]{2,1,0:T(8,128)(2,1)S(1)}, u32[]{:S(2)}, u32[]{:S(2)}) collective-permute-start(bf16[2,272,128]{2,1,0:T(8,128)(2,1)S(1)} %get-tuple-element.121), channel_id=1, source_target_pairs={{0,6},{1,14},{2,22},{3,30},{4,4},{5,12},{6,20},{7,28},{8,2},{9,10}... | collective-permute-start | bytes 417800 | tf_op jit(solution)/shard_map/ppermute | solution.py:792
  26.4 25.8 %collective-permute-start.8 = (bf16[176,1088]{1,0:T(8,128)(2,1)S(1)}, bf16[176,1088]{1,0:T(8,128)(2,1)S(1)}, u32[]{:S(2)}, u32[]{:S(2)}) collective-permute-start(bf16[176,1088]{1,0:T(8,128)(2,1)S(1)} %join_lanes.1.refs_4_.refs_1_), channel_id=1, source_target_pairs={{0,3},{1,0},{2,1},{3,2},{4,7},{5,4},{6,5},{7,6},{8,11},{9,8},{10,9... | collective-permute-start | bytes 1148936 | tf_op jit(solution)/shard_map/ppermute | solution.py:66
  32.9 19.4 %collective-permute-start.7 = (bf16[176,1088]{1,0:T(8,128)(2,1)S(1)}, bf16[176,1088]{1,0:T(8,128)(2,1)S(1)}, u32[]{:S(2)}, u32[]{:S(2)}) collective-permute-start(bf16[176,1088]{1,0:T(8,128)(2,1)S(1)} %join_lanes.1.refs_4_.refs_1_), channel_id=1, source_target_pairs={{0,1},{1,2},{2,3},{3,0},{4,5},{5,6},{6,7},{7,4},{8,9},{9,10},{10,1... | collective-permute-start | bytes 1148936 | tf_op jit(solution)/shard_map/ppermute | solution.py:66
  34.9 9.4 %collective-permute-start.9 = (bf16[2,136,272]{2,1,0:T(8,128)(2,1)S(1)}, bf16[2,136,272]{2,1,0:T(8,128)(2,1)S(1)}, u32[]{:S(2)}, u32[]{:S(2)}) collective-permute-start(bf16[2,136,272]{2,1,0:T(8,128)(2,1)S(1)} %get-tuple-element.125), channel_id=1, source_target_pairs={{0,4},{4,0},{8,12},{12,8},{1,5},{5,1},{9,13},{13,9},{2,6},{6,2},{1... | collective-permute-start | bytes 443912 | tf_op jit(solution)/shard_map/ppermute | solution.py:62
  38.3 11.3 %collective-permute-start.10 = (bf16[2,136,272]{2,1,0:T(8,128)(2,1)S(1)}, bf16[2,136,272]{2,1,0:T(8,128)(2,1)S(1)}, u32[]{:S(2)}, u32[]{:S(2)}) collective-permute-start(bf16[2,136,272]{2,1,0:T(8,128)(2,1)S(1)} %get-tuple-element.126), channel_id=1, source_target_pairs={{0,8},{4,12},{8,0},{12,4},{1,9},{5,13},{9,1},{13,5},{2,10},{6,14},... | collective-permute-start | bytes 443912 | tf_op jit(solution)/shard_map/ppermute | solution.py:62
  38.4 13.1 %collective-permute-start.11 = (bf16[2,136,272]{2,1,0:T(8,128)(2,1)S(1)}, bf16[2,136,272]{2,1,0:T(8,128)(2,1)S(1)}, u32[]{:S(2)}, u32[]{:S(2)}) collective-permute-start(bf16[2,136,272]{2,1,0:T(8,128)(2,1)S(1)} %get-tuple-element.127), channel_id=1, source_target_pairs={{0,12},{4,8},{8,4},{12,0},{1,13},{5,9},{9,5},{13,1},{2,14},{6,10},... | collective-permute-start | bytes 443912 | tf_op jit(solution)/shard_map/ppermute | solution.py:62
  44.3 31.9 %collective-permute-start.20 = (s32[2,1024]{1,0:T(2,128)S(1)}, s32[2,1024]{1,0:T(2,128)S(1)}, u32[]{:S(2)}, u32[]{:S(2)}) collective-permute-start(s32[2,1024]{1,0:T(2,128)S(1)} %copy-done.46), channel_id=1, source_target_pairs={{0,16},{16,0},{1,17},{17,1},{2,18},{18,2},{3,19},{19,3},{4,20},{20... | collective-permute-start | bytes 24584 | tf_op jit(solution)/shard_map/ppermute | solution.py:58
  49.7 21.8 %collective-permute-start.19 = (bf16[176,1088]{1,0:T(8,128)(2,1)S(1)}, bf16[176,1088]{1,0:T(8,128)(2,1)S(1)}, u32[]{:S(2)}, u32[]{:S(2)}) collective-permute-start(bf16[176,1088]{1,0:T(8,128)(2,1)S(1)} %join_lanes.1.refs_4_.refs_1_), channel_id=1, source_target_pairs={{0,2},{1,3},{2,0},{3,1},{4,6},{5,7},{6,4},{7,5},{8,10},{9,11},{10,... | collective-permute-start | bytes 1148936 | tf_op jit(solution)/shard_map/ppermute | solution.py:66
  53.3 18.2 %collective-permute-start.14 = (bf16[128,1088]{1,0:T(8,128)(2,1)S(1)}, bf16[128,1088]{1,0:T(8,128)(2,1)}, u32[]{:S(2)}, u32[]{:S(2)}) collective-permute-start(bf16[128,1088]{1,0:T(8,128)(2,1)S(1)} %get-tuple-element.128.refs_5_.refs_1_.refs_2_.refs_14_), channel_id=1, source_target_pairs={{0,12},{4,8},{8,4},{12,0},{1,13},{5,9},{9,5},{13,1},{2,14},{6,10},... | collective-permute-start | bytes 835592 | tf_op jit(solution)/shard_map/ppermute | solution.py:62
  56.3 15.7 %collective-permute-start.13 = (bf16[128,1088]{1,0:T(8,128)(2,1)S(1)}, bf16[128,1088]{1,0:T(8,128)(2,1)}, u32[]{:S(2)}, u32[]{:S(2)}) collective-permute-start(bf16[128,1088]{1,0:T(8,128)(2,1)S(1)} %get-tuple-element.128.refs_5_.refs_1_.refs_2_.refs_14_), channel_id=1, source_target_pairs={{0,8},{4,12},{8,0},{12,4},{1,9},{5,13},{9,1},{13,5},{2,10},{6,14},... | collective-permute-start | bytes 835592 | tf_op jit(solution)/shard_map/ppermute | solution.py:62
  56.3 15.8 %collective-permute-start.12 = (bf16[128,1088]{1,0:T(8,128)(2,1)S(1)}, bf16[128,1088]{1,0:T(8,128)(2,1)}, u32[]{:S(2)}, u32[]{:S(2)}) collective-permute-start(bf16[128,1088]{1,0:T(8,128)(2,1)S(1)} %get-tuple-element.128.refs_5_.refs_1_.refs_2_.refs_14_), channel_id=1, source_target_pairs={{0,4},{4,0},{8,12},{12,8},{1,5},{5,1},{9,13},{13,9},{2,6},{6,2},{1... | collective-permute-start | bytes 835592 | tf_op jit(solution)/shard_map/ppermute | solution.py:62
  76.2 17.5 %collective-permute-start.23 = (bf16[176,1088]{1,0:T(8,128)(2,1)S(1)}, bf16[176,1088]{1,0:T(8,128)(2,1)S(1)}, u32[]{:S(2)}, u32[]{:S(2)}) collective-permute-start(bf16[176,1088]{1,0:T(8,128)(2,1)S(1)} %get-tuple-element.133.refs_1_), channel_id=1, source_target_pairs={{0,12},{4,8},{8,4},{12,0},{1,13},{5,9},{9,5},{13,1},{2,14},{6,10},... | collective-permute-start | bytes 1148936 | tf_op jit(solution)/shard_map/ppermute | solution.py:62
  76.8 19.8 %collective-permute-start.22 = (bf16[176,1088]{1,0:T(8,128)(2,1)S(1)}, bf16[176,1088]{1,0:T(8,128)(2,1)S(1)}, u32[]{:S(2)}, u32[]{:S(2)}) collective-permute-start(bf16[176,1088]{1,0:T(8,128)(2,1)S(1)} %get-tuple-element.133.refs_1_), channel_id=1, source_target_pairs={{0,8},{4,12},{8,0},{12,4},{1,9},{5,13},{9,1},{13,5},{2,10},{6,14},... | collective-permute-start | bytes 1148936 | tf_op jit(solution)/shard_map/ppermute | solution.py:62
  78.3 18.3 %collective-permute-start.21 = (bf16[176,1088]{1,0:T(8,128)(2,1)S(1)}, bf16[176,1088]{1,0:T(8,128)(2,1)S(1)}, u32[]{:S(2)}, u32[]{:S(2)}) collective-permute-start(bf16[176,1088]{1,0:T(8,128)(2,1)S(1)} %get-tuple-element.133.refs_1_), channel_id=1, source_target_pairs={{0,4},{4,0},{8,12},{12,8},{1,5},{5,1},{9,13},{13,9},{2,6},{6,2},{1... | collective-permute-start | bytes 1148936 | tf_op jit(solution)/shard_map/ppermute | solution.py:62
  90.0 9.9 %all-to-all-start = ((bf16[8,128,128]{2,1,0:T(8,128)(2,1)}), bf16[8,128,128]{2,1,0:T(8,128)(2,1)S(1)}, u32[]{:S(2)}, u32[]{:S(2)}) async-start(bf16[8,128,128]{2,1,0:T(8,128)(2,1)} %get-tuple-element.131.refs_9_), calls=%async_computation | async-start | bytes 524288 | tf_op jit(solution)/shard_map/all_to_all | solution.py:859
  93.4 191.9 %reduce-scatter.5.cloned.1.call-start = ((), (), s32[]{:S(2)}) async-start(), calls=%async_computation.6 | async-start | bytes 3133440 | tf_op jit(solution)/shard_map/reduce_scatter | solution.py:943
  101.9 11.7 %collective-permute-start.37 = (bf16[128,1088]{1,0:T(8,128)(2,1)S(1)}, bf16[128,1088]{1,0:T(8,128)(2,1)S(1)}, u32[]{:S(2)}, u32[]{:S(2)}) collective-permute-start(bf16[128,1088]{1,0:T(8,128)(2,1)S(1)} %take_tokens.1.refs_5_.refs_1_.refs_4_.refs_6_), channel_id=1, source_target_pairs={{0,12},{4,8},{8,4},{12,0},{1,13},{5,9},{9,5},{13,1},{2,14},{6,10},... | collective-permute-start | bytes 835592 | tf_op jit(solution)/shard_map/ppermute | solution.py:62
  102.6 16.3 %collective-permute-start.36 = (bf16[128,1088]{1,0:T(8,128)(2,1)S(1)}, bf16[128,1088]{1,0:T(8,128)(2,1)S(1)}, u32[]{:S(2)}, u32[]{:S(2)}) collective-permute-start(bf16[128,1088]{1,0:T(8,128)(2,1)S(1)} %take_tokens.1.refs_5_.refs_1_.refs_4_.refs_6_), channel_id=1, source_target_pairs={{0,8},{4,12},{8,0},{12,4},{1,9},{5,13},{9,1},{13,5},{2,10},{6,14},... | collective-permute-start | bytes 835592 | tf_op jit(solution)/shard_map/ppermute | solution.py:62
  104.1 14.9 %collective-permute-start.35 = (bf16[128,1088]{1,0:T(8,128)(2,1)S(1)}, bf16[128,1088]{1,0:T(8,128)(2,1)S(1)}, u32[]{:S(2)}, u32[]{:S(2)}) collective-permute-start(bf16[128,1088]{1,0:T(8,128)(2,1)S(1)} %take_tokens.1.refs_5_.refs_1_.refs_4_.refs_6_), channel_id=1, source_target_pairs={{0,4},{4,0},{8,12},{12,8},{1,5},{5,1},{9,13},{13,9},{2,6},{6,2},{1... | collective-permute-start | bytes 835592 | tf_op jit(solution)/shard_map/ppermute | solution.py:62
  111.3 14.0 %collective-permute-start.30 = (bf16[128,1088]{1,0:T(8,128)(2,1)}, bf16[128,1088]{1,0:T(8,128)(2,1)S(1)}, u32[]{:S(2)}, u32[]{:S(2)}) collective-permute-start(bf16[128,1088]{1,0:T(8,128)(2,1)} %get-tuple-element.142.refs_5_.refs_10_.refs_1_), channel_id=1, source_target_pairs={{0,12},{4,8},{8,4},{12,0},{1,13},{5,9},{9,5},{13,1},{2,14},{6,10},... | collective-permute-start | bytes 835592 | tf_op jit(solution)/shard_map/ppermute | solution.py:62
  112.2 18.6 %collective-permute-start.29 = (bf16[128,1088]{1,0:T(8,128)(2,1)}, bf16[128,1088]{1,0:T(8,128)(2,1)S(1)}, u32[]{:S(2)}, u32[]{:S(2)}) collective-permute-start(bf16[128,1088]{1,0:T(8,128)(2,1)} %get-tuple-element.142.refs_5_.refs_10_.refs_1_), channel_id=1, source_target_pairs={{0,8},{4,12},{8,0},{12,4},{1,9},{5,13},{9,1},{13,5},{2,10},{6,14},... | collective-permute-start | bytes 835592 | tf_op jit(solution)/shard_map/ppermute | solution.py:62
  113.6 17.2 %collective-permute-start.28 = (bf16[128,1088]{1,0:T(8,128)(2,1)}, bf16[128,1088]{1,0:T(8,128)(2,1)}, u32[]{:S(2)}, u32[]{:S(2)}) collective-permute-start(bf16[128,1088]{1,0:T(8,128)(2,1)} %get-tuple-element.142.refs_5_.refs_10_.refs_1_), channel_id=1, source_target_pairs={{0,4},{4,0},{8,12},{12,8},{1,5},{5,1},{9,13},{13,9},{2,6},{6,2},{1... | collective-permute-start | bytes 835592 | tf_op jit(solution)/shard_map/ppermute | solution.py:62
  119.8 11.6 %collective-permute-start.38 = (bf16[128,1088]{1,0:T(8,128)(2,1)S(1)}, bf16[128,1088]{1,0:T(8,128)(2,1)S(1)}, u32[]{:S(2)}, u32[]{:S(2)}) collective-permute-start(bf16[128,1088]{1,0:T(8,128)(2,1)S(1)} %get-tuple-element.143), channel_id=1, source_target_pairs={{0,16},{16,0},{1,17},{17,1},{2,18},{18,2},{3,19},{19,3},{4,20},{20... | collective-permute-start | bytes 835592 | tf_op jit(solution)/shard_map/ppermute | solution.py:58
  119.8 11.6 %collective-permute-start.39 = (bf16[128,1088]{1,0:T(8,128)(2,1)S(1)}, bf16[128,1088]{1,0:T(8,128)(2,1)S(1)}, u32[]{:S(2)}, u32[]{:S(2)}) collective-permute-start(bf16[128,1088]{1,0:T(8,128)(2,1)S(1)} %get-tuple-element.144), channel_id=1, source_target_pairs={{0,16},{16,0},{1,17},{17,1},{2,18},{18,2},{3,19},{19,3},{4,20},{20... | collective-permute-start | bytes 835592 | tf_op jit(solution)/shard_map/ppermute | solution.py:58
  130.8 9.4 %collective-permute-start.31 = (bf16[128,1088]{1,0:T(8,128)(2,1)}, bf16[128,1088]{1,0:T(8,128)(2,1)S(1)}, u32[]{:S(2)}, u32[]{:S(2)}) collective-permute-start(bf16[128,1088]{1,0:T(8,128)(2,1)} %get-tuple-element.142.refs_5_.refs_10_.refs_1_), channel_id=1, source_target_pairs={{0,16},{16,0},{1,17},{17,1},{2,18},{18,2},{3,19},{19,3},{4,20},{20... | collective-permute-start | bytes 835592 | tf_op jit(solution)/shard_map/ppermute | solution.py:58
  173.8 10.6 %collective-permute-start.46 = (bf16[128,1088]{1,0:T(8,128)(2,1)}, bf16[128,1088]{1,0:T(8,128)(2,1)S(1)}, u32[]{:S(2)}, u32[]{:S(2)}) collective-permute-start(bf16[128,1088]{1,0:T(8,128)(2,1)} %copy-done.38), channel_id=1, source_target_pairs={{0,4},{4,0},{8,12},{12,8},{1,5},{5,1},{9,13},{13,9},{2,6},{6,2},{1... | collective-permute-start | bytes 835592 | tf_op jit(solution)/shard_map/ppermute | solution.py:62
  175.4 15.3 %collective-permute-start.47 = (bf16[128,1088]{1,0:T(8,128)(2,1)}, bf16[128,1088]{1,0:T(8,128)(2,1)S(1)}, u32[]{:S(2)}, u32[]{:S(2)}) collective-permute-start(bf16[128,1088]{1,0:T(8,128)(2,1)} %copy-done.37), channel_id=1, source_target_pairs={{0,8},{4,12},{8,0},{12,4},{1,9},{5,13},{9,1},{13,5},{2,10},{6,14},... | collective-permute-start | bytes 835592 | tf_op jit(solution)/shard_map/ppermute | solution.py:62
  176.9 13.8 %collective-permute-start.48 = (bf16[128,1088]{1,0:T(8,128)(2,1)S(1)}, bf16[128,1088]{1,0:T(8,128)(2,1)S(1)}, u32[]{:S(2)}, u32[]{:S(2)}) collective-permute-start(bf16[128,1088]{1,0:T(8,128)(2,1)S(1)} %get-tuple-element.156), channel_id=1, source_target_pairs={{0,12},{4,8},{8,4},{12,0},{1,13},{5,9},{9,5},{13,1},{2,14},{6,10},... | collective-permute-start | bytes 835592 | tf_op jit(solution)/shard_map/ppermute | solution.py:62
  183.9 16.8 %collective-permute-start.49 = (bf16[128,1088]{1,0:T(8,128)(2,1)}, bf16[128,1088]{1,0:T(8,128)(2,1)}, u32[]{:S(2)}, u32[]{:S(2)}) collective-permute-start(bf16[128,1088]{1,0:T(8,128)(2,1)} %get-tuple-element.171), channel_id=1, source_target_pairs={{0,16},{16,0},{1,17},{17,1},{2,18},{18,2},{3,19},{19,3},{4,20},{20... | collective-permute-start | bytes 835592 | tf_op jit(solution)/shard_map/ppermute | solution.py:58
  183.9 17.4 %collective-permute-start.50 = (bf16[128,1088]{1,0:T(8,128)(2,1)}, bf16[128,1088]{1,0:T(8,128)(2,1)}, u32[]{:S(2)}, u32[]{:S(2)}) collective-permute-start(bf16[128,1088]{1,0:T(8,128)(2,1)} %get-tuple-element.172), channel_id=1, source_target_pairs={{0,16},{16,0},{1,17},{17,1},{2,18},{18,2},{3,19},{19,3},{4,20},{20... | collective-permute-start | bytes 835592 | tf_op jit(solution)/shard_map/ppermute | solution.py:58
  184.4 17.1 %collective-permute-start.51 = (bf16[128,1088]{1,0:T(8,128)(2,1)}, bf16[128,1088]{1,0:T(8,128)(2,1)}, u32[]{:S(2)}, u32[]{:S(2)}) collective-permute-start(bf16[128,1088]{1,0:T(8,128)(2,1)} %get-tuple-element.173), channel_id=1, source_target_pairs={{0,16},{16,0},{1,17},{17,1},{2,18},{18,2},{3,19},{19,3},{4,20},{20... | collective-permute-start | bytes 835592 | tf_op jit(solution)/shard_map/ppermute | solution.py:58
  190.7 10.8 %collective-permute-start.52 = (bf16[128,1088]{1,0:T(8,128)(2,1)}, bf16[128,1088]{1,0:T(8,128)(2,1)}, u32[]{:S(2)}, u32[]{:S(2)}) collective-permute-start(bf16[128,1088]{1,0:T(8,128)(2,1)} %get-tuple-element.174), channel_id=1, source_target_pairs={{0,16},{16,0},{1,17},{17,1},{2,18},{18,2},{3,19},{19,3},{4,20},{20... | collective-permute-start | bytes 835592 | tf_op jit(solution)/shard_map/ppermute | solution.py:58
  194.5 10.1 %all-to-all-start.1 = ((bf16[8,128,128]{2,1,0:T(8,128)(2,1)}), bf16[8,128,128]{2,1,0:T(8,128)(2,1)S(1)}, u32[]{:S(2)}, u32[]{:S(2)}) async-start(bf16[8,128,128]{2,1,0:T(8,128)(2,1)} %get-tuple-element.161), calls=%async_computation.1 | async-start | bytes 524288 | tf_op jit(solution)/shard_map/all_to_all | solution.py:958
  197.9 101.4 %reduce-scatter.3.cloned.1.call-start = ((), (), s32[]{:S(2)}) async-start(), calls=%async_computation.5 | async-start | bytes 1474560 | tf_op jit(solution)/shard_map/reduce_scatter | solution.py:991
  198.0 25.4 %collective-permute-start.69 = (bf16[128,1088]{1,0:T(8,128)(2,1)S(1)}, bf16[128,1088]{1,0:T(8,128)(2,1)S(1)}, u32[]{:S(2)}, u32[]{:S(2)}) collective-permute-start(bf16[128,1088]{1,0:T(8,128)(2,1)S(1)} %get-tuple-element.196.refs_1_), channel_id=1, source_target_pairs={{0,12},{4,8},{8,4},{12,0},{1,13},{5,9},{9,5},{13,1},{2,14},{6,10},... | collective-permute-start | bytes 835592 | tf_op jit(solution)/shard_map/ppermute | solution.py:62
  200.8 23.0 %collective-permute-start.68 = (bf16[128,1088]{1,0:T(8,128)(2,1)S(1)}, bf16[128,1088]{1,0:T(8,128)(2,1)S(1)}, u32[]{:S(2)}, u32[]{:S(2)}) collective-permute-start(bf16[128,1088]{1,0:T(8,128)(2,1)S(1)} %get-tuple-element.196.refs_1_), channel_id=1, source_target_pairs={{0,8},{4,12},{8,0},{12,4},{1,9},{5,13},{9,1},{13,5},{2,10},{6,14},... | collective-permute-start | bytes 835592 | tf_op jit(solution)/shard_map/ppermute | solution.py:62
  201.3 22.5 %collective-permute-start.67 = (bf16[128,1088]{1,0:T(8,128)(2,1)S(1)}, bf16[128,1088]{1,0:T(8,128)(2,1)S(1)}, u32[]{:S(2)}, u32[]{:S(2)}) collective-permute-start(bf16[128,1088]{1,0:T(8,128)(2,1)S(1)} %get-tuple-element.196.refs_1_), channel_id=1, source_target_pairs={{0,4},{4,0},{8,12},{12,8},{1,5},{5,1},{9,13},{13,9},{2,6},{6,2},{1... | collective-permute-start | bytes 835592 | tf_op jit(solution)/shard_map/ppermute | solution.py:62
  225.1 9.8 %collective-permute-start.72 = (bf16[128,1088]{1,0:T(8,128)(2,1)S(1)}, bf16[128,1088]{1,0:T(8,128)(2,1)}, u32[]{:S(2)}, u32[]{:S(2)}) collective-permute-start(bf16[128,1088]{1,0:T(8,128)(2,1)S(1)} %collective-permute-done.68.refs_3_), channel_id=1, source_target_pairs={{0,16},{16,0},{1,17},{17,1},{2,18},{18,2},{3,19},{19,3},{4,20},{20... | collective-permute-start | bytes 835592 | tf_op jit(solution)/shard_map/ppermute | solution.py:58
  225.5 10.1 %collective-permute-start.71 = (bf16[128,1088]{1,0:T(8,128)(2,1)S(1)}, bf16[128,1088]{1,0:T(8,128)(2,1)}, u32[]{:S(2)}, u32[]{:S(2)}) collective-permute-start(bf16[128,1088]{1,0:T(8,128)(2,1)S(1)} %collective-permute-done.67.refs_2_), channel_id=1, source_target_pairs={{0,16},{16,0},{1,17},{17,1},{2,18},{18,2},{3,19},{19,3},{4,20},{20... | collective-permute-start | bytes 835592 | tf_op jit(solution)/shard_map/ppermute | solution.py:58
  230.0 10.1 %collective-permute-start.57 = (bf16[128,1088]{1,0:T(8,128)(2,1)}, bf16[128,1088]{1,0:T(8,128)(2,1)}, u32[]{:S(2)}, u32[]{:S(2)}) collective-permute-start(bf16[128,1088]{1,0:T(8,128)(2,1)} %get-tuple-element.182), channel_id=1, source_target_pairs={{0,4},{4,0},{8,12},{12,8},{1,5},{5,1},{9,13},{13,9},{2,6},{6,2},{1... | collective-permute-start | bytes 835592 | tf_op jit(solution)/shard_map/ppermute | solution.py:62
  231.3 16.5 %collective-permute-start.58 = (bf16[128,1088]{1,0:T(8,128)(2,1)}, bf16[128,1088]{1,0:T(8,128)(2,1)}, u32[]{:S(2)}, u32[]{:S(2)}) collective-permute-start(bf16[128,1088]{1,0:T(8,128)(2,1)} %get-tuple-element.183), channel_id=1, source_target_pairs={{0,8},{4,12},{8,0},{12,4},{1,9},{5,13},{9,1},{13,5},{2,10},{6,14},... | collective-permute-start | bytes 835592 | tf_op jit(solution)/shard_map/ppermute | solution.py:62
  232.7 15.1 %collective-permute-start.59 = (bf16[128,1088]{1,0:T(8,128)(2,1)}, bf16[128,1088]{1,0:T(8,128)(2,1)}, u32[]{:S(2)}, u32[]{:S(2)}) collective-permute-start(bf16[128,1088]{1,0:T(8,128)(2,1)} %get-tuple-element.184), channel_id=1, source_target_pairs={{0,12},{4,8},{8,4},{12,0},{1,13},{5,9},{9,5},{13,1},{2,14},{6,10},... | collective-permute-start | bytes 835592 | tf_op jit(solution)/shard_map/ppermute | solution.py:62
  234.9 28.3 %collective-permute-start.60 = (bf16[128,1088]{1,0:T(8,128)(2,1)S(1)}, bf16[128,1088]{1,0:T(8,128)(2,1)}, u32[]{:S(2)}, u32[]{:S(2)}) collective-permute-start(bf16[128,1088]{1,0:T(8,128)(2,1)S(1)} %get-tuple-element.185), channel_id=1, source_target_pairs={{0,4},{4,0},{8,12},{12,8},{1,5},{5,1},{9,13},{13,9},{2,6},{6,2},{1... | collective-permute-start | bytes 835592 | tf_op jit(solution)/shard_map/ppermute | solution.py:62
  235.6 27.6 %collective-permute-start.61 = (bf16[128,1088]{1,0:T(8,128)(2,1)S(1)}, bf16[128,1088]{1,0:T(8,128)(2,1)}, u32[]{:S(2)}, u32[]{:S(2)}) collective-permute-start(bf16[128,1088]{1,0:T(8,128)(2,1)S(1)} %get-tuple-element.186), channel_id=1, source_target_pairs={{0,8},{4,12},{8,0},{12,4},{1,9},{5,13},{9,1},{13,5},{2,10},{6,14},... | collective-permute-start | bytes 835592 | tf_op jit(solution)/shard_map/ppermute | solution.py:62
  240.1 23.1 %collective-permute-start.62 = (bf16[128,1088]{1,0:T(8,128)(2,1)S(1)}, bf16[128,1088]{1,0:T(8,128)(2,1)}, u32[]{:S(2)}, u32[]{:S(2)}) collective-permute-start(bf16[128,1088]{1,0:T(8,128)(2,1)S(1)} %get-tuple-element.187), channel_id=1, source_target_pairs={{0,12},{4,8},{8,4},{12,0},{1,13},{5,9},{9,5},{13,1},{2,14},{6,10},... | collective-permute-start | bytes 835592 | tf_op jit(solution)/shard_map/ppermute | solution.py:62
  257.4 33.5 %all-to-all-start.2 = ((bf16[8,136,384]{2,1,0:T(8,128)(2,1)}), bf16[8,136,384]{2,1,0:T(8,128)(2,1)S(1)}, u32[]{:S(2)}, u32[]{:S(2)}) async-start(bf16[8,136,384]{2,1,0:T(8,128)(2,1)} %get-tuple-element.207), calls=%async_computation.4 | async-start | bytes 1671168 | tf_op jit(solution)/shard_map/all_to_all | solution.py:1010
  261.2 24.0 %collective-permute-start.75 = (f32[12,1088]{1,0:T(8,128)S(1)}, f32[12,1088]{1,0:T(8,128)S(1)}, u32[]{:S(2)}, u32[]{:S(2)}) collective-permute-start(f32[12,1088]{1,0:T(8,128)S(1)} %add.17), channel_id=1, source_target_pairs={{0,4},{4,0},{8,12},{12,8},{1,5},{5,1},{9,13},{13,9},{2,6},{6,2},{1... | collective-permute-start | bytes 156680 | tf_op jit(solution)/shard_map/ppermute | solution.py:62
  268.8 18.5 %collective-permute-start.63 = (bf16[2,272,128]{2,1,0:T(8,128)(2,1)S(1)}, bf16[2,272,128]{2,1,0:T(8,128)(2,1)S(1)}, u32[]{:S(2)}, u32[]{:S(2)}) collective-permute-start(bf16[2,272,128]{2,1,0:T(8,128)(2,1)S(1)} %get-tuple-element.189), channel_id=1, source_target_pairs={{0,0},{8,1},{16,2},{24,3},{2,4},{10,5},{18,6},{26,7},{4,8},{12,9},... | collective-permute-start | bytes 417800 | tf_op jit(solution)/shard_map/ppermute | solution.py:1043
  269.5 18.4 %collective-permute-start.64 = (bf16[2,272,128]{2,1,0:T(8,128)(2,1)S(1)}, bf16[2,272,128]{2,1,0:T(8,128)(2,1)S(1)}, u32[]{:S(2)}, u32[]{:S(2)}) collective-permute-start(bf16[2,272,128]{2,1,0:T(8,128)(2,1)S(1)} %get-tuple-element.190), channel_id=1, source_target_pairs={{2,0},{10,1},{18,2},{26,3},{0,4},{8,5},{16,6},{24,7},{6,8},{14,9},... | collective-permute-start | bytes 417800 | tf_op jit(solution)/shard_map/ppermute | solution.py:1043
  273.7 15.7 %collective-permute-start.65 = (bf16[2,272,128]{2,1,0:T(8,128)(2,1)S(1)}, bf16[2,272,128]{2,1,0:T(8,128)(2,1)S(1)}, u32[]{:S(2)}, u32[]{:S(2)}) collective-permute-start(bf16[2,272,128]{2,1,0:T(8,128)(2,1)S(1)} %get-tuple-element.191), channel_id=1, source_target_pairs={{4,0},{12,1},{20,2},{28,3},{6,4},{14,5},{22,6},{30,7},{0,8},{8,9},... | collective-permute-start | bytes 417800 | tf_op jit(solution)/shard_map/ppermute | solution.py:1043
  276.1 16.8 %collective-permute-start.66 = (bf16[2,272,128]{2,1,0:T(8,128)(2,1)S(1)}, bf16[2,272,128]{2,1,0:T(8,128)(2,1)S(1)}, u32[]{:S(2)}, u32[]{:S(2)}) collective-permute-start(bf16[2,272,128]{2,1,0:T(8,128)(2,1)S(1)} %get-tuple-element.192), channel_id=1, source_target_pairs={{6,0},{14,1},{22,2},{30,3},{4,4},{12,5},{20,6},{28,7},{2,8},{10,9}... | collective-permute-start | bytes 417800 | tf_op jit(solution)/shard_map/ppermute | solution.py:1043
  287.3 11.0 %collective-permute-start.77 = (bf16[2,136,272]{2,1,0:T(8,128)(2,1)S(1)}, bf16[2,136,272]{2,1,0:T(8,128)(2,1)S(1)}, u32[]{:S(2)}, u32[]{:S(2)}) collective-permute-start(bf16[2,136,272]{2,1,0:T(8,128)(2,1)S(1)} %get-tuple-element.204), channel_id=1, source_target_pairs={{0,4},{4,0},{8,12},{12,8},{1,5},{5,1},{9,13},{13,9},{2,6},{6,2},{1... | collective-permute-start | bytes 443912 | tf_op jit(solution)/shard_map/ppermute | solution.py:62
  287.9 12.5 %collective-permute-start.78 = (bf16[2,136,272]{2,1,0:T(8,128)(2,1)S(1)}, bf16[2,136,272]{2,1,0:T(8,128)(2,1)S(1)}, u32[]{:S(2)}, u32[]{:S(2)}) collective-permute-start(bf16[2,136,272]{2,1,0:T(8,128)(2,1)S(1)} %get-tuple-element.205), channel_id=1, source_target_pairs={{0,8},{4,12},{8,0},{12,4},{1,9},{5,13},{9,1},{13,5},{2,10},{6,14},... | collective-permute-start | bytes 443912 | tf_op jit(solution)/shard_map/ppermute | solution.py:62
  289.4 11.0 %collective-permute-start.79 = (bf16[2,136,272]{2,1,0:T(8,128)(2,1)S(1)}, bf16[2,136,272]{2,1,0:T(8,128)(2,1)S(1)}, u32[]{:S(2)}, u32[]{:S(2)}) collective-permute-start(bf16[2,136,272]{2,1,0:T(8,128)(2,1)S(1)} %get-tuple-element.206), channel_id=1, source_target_pairs={{0,12},{4,8},{8,4},{12,0},{1,13},{5,9},{9,5},{13,1},{2,14},{6,10},... | collective-permute-start | bytes 443912 | tf_op jit(solution)/shard_map/ppermute | solution.py:62
  293.0 12.5 %collective-permute-start.89 = (bf16[136,336]{1,0:T(8,128)(2,1)}, bf16[136,336]{1,0:T(8,128)(2,1)S(1)}, u32[]{:S(2)}, u32[]{:S(2)}) collective-permute-start(bf16[136,336]{1,0:T(8,128)(2,1)} %get-tuple-element.213), channel_id=1, source_target_pairs={{0,1},{1,2},{2,3},{3,0},{4,5},{5,6},{6,7},{7,4},{8,9},{9,10},{10,1... | collective-permute-start | bytes 274184 | tf_op jit(solution)/shard_map/ppermute | solution.py:66
  294.2 11.8 %collective-permute-start.90 = (bf16[136,336]{1,0:T(8,128)(2,1)S(1)}, bf16[136,336]{1,0:T(8,128)(2,1)S(1)}, u32[]{:S(2)}, u32[]{:S(2)}) collective-permute-start(bf16[136,336]{1,0:T(8,128)(2,1)S(1)} %get-tuple-element.214), channel_id=1, source_target_pairs={{0,2},{1,3},{2,0},{3,1},{4,6},{5,7},{6,4},{7,5},{8,10},{9,11},{10,... | collective-permute-start | bytes 274184 | tf_op jit(solution)/shard_map/ppermute | solution.py:66
  308.2 14.7 %collective-permute-start.93 = (bf16[2,136,272]{2,1,0:T(8,128)(2,1)S(1)}, bf16[2,136,272]{2,1,0:T(8,128)(2,1)S(1)}, u32[]{:S(2)}, u32[]{:S(2)}) collective-permute-start(bf16[2,136,272]{2,1,0:T(8,128)(2,1)S(1)} %get-tuple-element.216.refs_1_), channel_id=1, source_target_pairs={{0,16},{16,0},{1,17},{17,1},{2,18},{18,2},{3,19},{19,3},{4,20},{20... | collective-permute-start | bytes 443912 | tf_op jit(solution)/shard_map/ppermute | solution.py:58
  (134 other events, 867.4 us)
Sparse Core Ops, SparseCore 0:
  76.3 57.5 all-gather.2
  174.0 54.0 reduce-scatter.4
  235.0 31.6 reduce-scatter.2

commit v3 on v2

--- a/solution.py
+++ b/solution.py
@@ -1004,6 +1004,7 @@
         n1_own,
         w16,
         us=3.5,
+        far=True,
         work=10,
         after=tuple(parts[1:]),
     )
@@ -1039,6 +1040,7 @@
         x_own,
         vectors,
         us=2.5,
+        far=True,
     )
     landed = [lax.ppermute(done[m], EVERY, BACK[m]) for m in range(4)]
     hidden_out, grad_in = kernel(land_tokens, [((2, quarter, 2 * rows), BF)] * 2, [], ids, *landed, us=1)

time: 336 us -> 329 us (0.979)
  local copies, waits for them, and re-layouts: 34.7 us -> 25.1 us
  starting transfers between devices: 110 us -> 115 us
  waiting for transfers between devices: 71.8 us -> 68 us
    unnamed x190 -> x180, local copies, waits for them, and re-layouts: 32.4 us -> 22.8 us
    ppermute x38, waiting for transfers between devices: 46.8 us -> 43 us  [from_peer(): return lax.ppermute(value, 'gx', [(i, i ^ step) for i in range(4)])]
  transfers between devices with their start and end apart: 103 -> 103, of which waited for: 27 -> 23; matrix products, arithmetic and copies ran while one was open for 0% -> 1% of each run, Pallas kernels for 21% -> 22%
where the time goes in v3:
time: 329 us; the launch traced here: 326 us
  starting transfers between devices  115 us (35%)
  Pallas kernels  102 us (31%)
  waiting for transfers between devices  68 us (21%)
  local copies, waits for them, and re-layouts  25.1 us (8%)
  between operations  15.2 us (5%)
    pallas_call x37, Pallas kernels, kernel(): pl.pallas_call(run, name=body.__name__, out_shape=tuple((jax.ShapeDtypeSt...  102 us
    ppermute x38, starting transfers between devices, from_peer(): return lax.ppermute(value, 'gx', [(i, i ^ step) for i in range(4)])  45.7 us
    ppermute x38, waiting for transfers between devices, from_peer(): return lax.ppermute(value, 'gx', [(i, i ^ step) for i in range(4)])  43 us
    unnamed x180, local copies, waits for them, and re-layouts  22.8 us
    ppermute x6, starting transfers between devices, from_below(): return lax.ppermute(value, 'gy', [(i, (i + step) % 4) for i in range(4)])  17.2 us
    ppermute x4, starting transfers between devices, shards(): landed = [lax.ppermute(done[m], EVERY, BACK[m]) for m in range(4)]  16.3 us
    ppermute x6, waiting for transfers between devices, from_below(): return lax.ppermute(value, 'gy', [(i, (i + step) % 4) for i in range(4)])  12.8 us
    ppermute x43, starting transfers between devices, swap_core(): return lax.ppermute(value, 'c', [(0, 1), (1, 0)])  10.8 us
  transfers between devices with their start and end apart: 103, of which 23 were waited for; matrix products, arithmetic and copies ran while one was open for 1% of the time, Pallas kernels for 22%

profile of v3, /device:TPU:0, one launch (start us, length us, event | category | flops | bytes accessed | tf_op | source)
XLA Modules:
  0.0 325.6 jit_solution(2623664075252315540)
XLA Ops:
  9.8 3.0 collective-permute-start.4
  12.8 1.5 collective-permute-start.5
  15.1 3.1 collective-permute-start.1
  19.9 2.8 collective-permute-start.2
  22.7 3.0 collective-permute-start.3
  26.4 6.4 %collective-permute-start.8 = (bf16[176,1088]{1,0:T(8,128)(2,1)S(1)}, bf16[176,1088]{1,0:T(8,128)(2,1)S(1)}, u32[]{:S(2)}, u32[]{:S(2)}) collective-permute-start(bf16[176,1088]{1,0:T(8,128)(2,1)S(1)} %join_lanes.1.refs_4_.refs_1_), channel_id=1, source_target_pairs={{0,3},{1,0},{2,1},{3,2},{4,7},{5,4},{6,5},{7,6},{8,11},{9,8},{10,9... | collective-permute-start | bytes 1148936 | tf_op jit(solution)/shard_map/ppermute | solution.py:66
  34.9 3.5 %collective-permute-start.9 = (bf16[2,136,272]{2,1,0:T(8,128)(2,1)S(1)}, bf16[2,136,272]{2,1,0:T(8,128)(2,1)S(1)}, u32[]{:S(2)}, u32[]{:S(2)}) collective-permute-start(bf16[2,136,272]{2,1,0:T(8,128)(2,1)S(1)} %get-tuple-element.125), channel_id=1, source_target_pairs={{0,4},{4,0},{8,12},{12,8},{1,5},{5,1},{9,13},{13,9},{2,6},{6,2},{1... | collective-permute-start | bytes 443912 | tf_op jit(solution)/shard_map/ppermute | solution.py:62
  38.4 1.5 collective-permute-start.11
  40.2 4.1 %collective-permute-done.9.refs_8_.refs_2_ = bf16[2,136,272]{2,1,0:T(8,128)(2,1)S(1)} collective-permute-done((bf16[2,136,272]{2,1,0:T(8,128)(2,1)S(1)}, bf16[2,136,272]{2,1,0:T(8,128)(2,1)S(1)}, u32[]{:S(2)}, u32[]{:S(2)}) %collective-permute-start.9) | collective-permute-done | bytes 148000 | tf_op jit(solution)/shard_map/ppermute | solution.py:62
  44.3 5.4 %collective-permute-done.10.refs_9_.refs_3_ = bf16[2,136,272]{2,1,0:T(8,128)(2,1)S(1)} collective-permute-done((bf16[2,136,272]{2,1,0:T(8,128)(2,1)S(1)}, bf16[2,136,272]{2,1,0:T(8,128)(2,1)S(1)}, u32[]{:S(2)}, u32[]{:S(2)}) %collective-permute-start.10) | collective-permute-done | bytes 148000 | tf_op jit(solution)/shard_map/ppermute | solution.py:62
  49.7 1.8 collective-permute-start.19
  53.3 3.0 collective-permute-start.14
  59.5 12.0 %collective-permute-done.19.refs_3_ = bf16[176,1088]{1,0:T(8,128)(2,1)S(1)} collective-permute-done((bf16[176,1088]{1,0:T(8,128)(2,1)S(1)}, bf16[176,1088]{1,0:T(8,128)(2,1)S(1)}, u32[]{:S(2)}, u32[]{:S(2)}) %collective-permute-start.19) | collective-permute-done | bytes 383008 | tf_op jit(solution)/shard_map/ppermute | solution.py:66
  73.5 1.7 mlp_join.1.refs_13_
  76.8 1.5 collective-permute-start.22
  78.3 1.5 collective-permute-start.21
  79.8 10.2 %attend.1 = (bf16[8,128,1088]{2,1,0:T(8,128)(2,1)}, bf16[1024,128]{1,0:T(8,128)(2,1)}, bf16[1024,128]{1,0:T(8,128)(2,1)}, bf16[1024,128]{1,0:T(8,128)(2,1)}, bf1...) custom-call(s32[100]{0:T(128)} %copy-done.10, bf16[128,1088]{1,0:T(8,128)(2,1)} %copy-done.25, ...), custom_call_target="tpu_custom_call" | custom-call | flops 15000000512 | bytes 300000 | tf_op jit(solution)/shard_map/attend/pallas_call | solution.py:44
  90.1 3.4 %all-to-all-start = ((bf16[8,128,128]{2,1,0:T(8,128)(2,1)}), bf16[8,128,128]{2,1,0:T(8,128)(2,1)S(1)}, u32[]{:S(2)}, u32[]{:S(2)}) async-start(bf16[8,128,128]{2,1,0:T(8,128)(2,1)} %get-tuple-element.131.refs_9_), calls=%async_computation | async-start | bytes 524288 | tf_op jit(solution)/shard_map/all_to_all | solution.py:859
  93.8 2.8 collective-permute-done.22.refs_3_
  96.6 3.4 %all-to-all-done.refs_5_.refs_1_ = bf16[8,128,128]{2,1,0:T(8,128)(2,1)S(1)} async-done(((bf16[8,128,128]{2,1,0:T(8,128)(2,1)}), bf16[8,128,128]{2,1,0:T(8,128)(2,1)S(1)}, u32[]{:S(2)}, u32[]{:S(2)}) %all-to-all-start) | async-done | bytes 262176 | tf_op jit(solution)/shard_map/all_to_all | solution.py:859
  106.7 2.2 attend_shared.1
  110.3 2.4 out_norm.1
  116.3 2.8 collective-permute-done.36.refs_3_.refs_6_
  120.4 5.0 %collective-permute-done.30.refs_4_ = bf16[128,1088]{1,0:T(8,128)(2,1)S(1)} collective-permute-done((bf16[128,1088]{1,0:T(8,128)(2,1)}, bf16[128,1088]{1,0:T(8,128)(2,1)S(1)}, u32[]{:S(2)}, u32[]{:S(2)}) %collective-permute-start.30) | collective-permute-done | bytes 278560 | tf_op jit(solution)/shard_map/ppermute | solution.py:62
  125.4 5.5 %collective-permute-done.29.refs_3_ = bf16[128,1088]{1,0:T(8,128)(2,1)S(1)} collective-permute-done((bf16[128,1088]{1,0:T(8,128)(2,1)}, bf16[128,1088]{1,0:T(8,128)(2,1)S(1)}, u32[]{:S(2)}, u32[]{:S(2)}) %collective-permute-start.29) | collective-permute-done | bytes 278560 | tf_op jit(solution)/shard_map/ppermute | solution.py:62
  133.9 6.3 %grad_activated.1.refs_10_ = f32[1024,544]{1,0:T(8,128)} custom-call(s32[100]{0:T(128)} %copy-done.10, bf16[128,1088]{1,0:T(8,128)(2,1)} %copy-done.27, bf16[128,1088]{1,0:T(8,128)(2,1)} %copy-done.33, bf16[128,1088]{1,0:T(8,128)(2,1)} %copy-done.32, bf16[128,1088]{1,0:T(8,128)(2,1)} %copy-done.31, bf16[128,1088]{1,0:T(8,128)(2,1)} %copy-done.82, ...), custom_call_target="tpu_custom_call" | custom-call | flops 60000002048 | bytes 1200000 | tf_op jit(solution)/shard_map/grad_activated/pallas_call | solution.py:44
  140.3 1.7 copy-done.52
  142.0 6.5 %feed_forward.1 = (bf16[8,128,1088]{2,1,0:T(8,128)(2,1)S(1)}, bf16[1024,544]{1,0:T(8,128)(2,1)S(1)}, bf16[1024,544]{1,0:T(8,128)(2,1)S(1)}, f32[1,544]{1,0:T(1,1...) custom-call(s32[100]{0:T(128)S(1)} %copy-done.12, ...), custom_call_target="tpu_custom_call" | custom-call | flops 7000000000 | bytes 140000 | tf_op jit(solution)/shard_map/feed_forward/pallas_call | solution.py:44
  154.5 19.2 %mlp_grads.1.refs_9_.refs_3_ = bf16[4,2,136,1088]{3,2,1,0:T(8,128)(2,1)} custom-call(s32[100]{0:T(128)} %copy-done.10, bf16[1024,544]{1,0:T(8,128)(2,1)} %copy-done.56, bf16[1024,544]{1,0:T(8,128)(2,1)} %copy-done.58, bf16[8,128,1088]{2,1,0:T(8,128)(2,1)} %copy-done.55, bf16[128,1088]{1,0:T(8,128)(2,1)} %copy-done.27, bf16[128,1088]{1,0:T(8,128)(2,1)} %copy-done.33, ...), custom_call_target="tpu_custom_call" | custom-call | flops 99999997952 | bytes 2000000 | tf_op jit(solution)/shard_map/mlp_grads/pallas_call | solution.py:44
  173.8 1.5 collective-permute-start.46
  175.3 1.5 collective-permute-start.47
  177.4 1.9 copy-done.18
  180.6 3.3 %feed_out.1 = (bf16[128,1088]{1,0:T(8,128)(2,1)}, bf16[128,1088]{1,0:T(8,128)(2,1)}, bf16[128,1088]{1,0:T(8,128)(2,1)}, bf16[128,1088]{1,0:T(8,128)(2,1)}, bf16[512,1088]{1,0:T(8,128)(2,1)S(1)}) custom-call(s32[100]{0:T(128)S(1)} %copy-done.13, bf16[1024,544]{1,0:T(8,128)(2,1)S(1)} %copy-done.57, bf16[4,2,136,1088]{3,2,1,0:T(8,128)(2,1)S(1)} %bitcast.15, ...), custom_call_target="tpu_custom_call" | custom-call | flops 12499999744 | bytes 250000 | tf_op jit(solution)/shard_map/feed_out/pallas_call | solution.py:44
  184.5 6.1 %collective-permute-done.47.refs_3_ = bf16[128,1088]{1,0:T(8,128)(2,1)S(1)} collective-permute-done((bf16[128,1088]{1,0:T(8,128)(2,1)}, bf16[128,1088]{1,0:T(8,128)(2,1)S(1)}, u32[]{:S(2)}, u32[]{:S(2)}) %collective-permute-start.47) | collective-permute-done | bytes 278560 | tf_op jit(solution)/shard_map/ppermute | solution.py:62
  190.7 2.3 middle_back.1
  194.5 3.4 %all-to-all-start.1 = ((bf16[8,128,128]{2,1,0:T(8,128)(2,1)}), bf16[8,128,128]{2,1,0:T(8,128)(2,1)S(1)}, u32[]{:S(2)}, u32[]{:S(2)}) async-start(bf16[8,128,128]{2,1,0:T(8,128)(2,1)} %get-tuple-element.161), calls=%async_computation.1 | async-start | bytes 524288 | tf_op jit(solution)/shard_map/all_to_all | solution.py:958
  198.0 2.8 collective-permute-start.69
  201.5 3.1 all-to-all-done.1.refs_6_.refs_1_
  206.0 1.5 add_far.4
  208.4 13.9 %attend_back.1 = (bf16[1024,128]{1,0:T(8,128)(2,1)}, bf16[128,64]{1,0:T(8,128)(2,1)}, f32[8,128]{1,0:T(8,128)}, f32[2,1088]{1,0:T(2,128)}, bf16[512,1088]{1,0:T(...) custom-call(s32[100]{0:T(128)} %copy-done.10, ...), custom_call_target="tpu_custom_call" | custom-call | flops 15000000512 | bytes 300000 | tf_op jit(solution)/shard_map/attend_back/pallas_call | solution.py:44
  229.8 2.2 collective-permute-start.59
  233.4 4.9 %collective-permute-done.57.refs_2_.refs_16_ = bf16[128,1088]{1,0:T(8,128)(2,1)S(1)} collective-permute-done((bf16[128,1088]{1,0:T(8,128)(2,1)S(1)}, bf16[128,1088]{1,0:T(8,128)(2,1)S(1)}, u32[]{:S(2)}, u32[]{:S(2)}) %collective-permute-start.57) | collective-permute-done | bytes 278560 | tf_op jit(solution)/shard_map/ppermute | solution.py:62
  239.1 6.2 %collective-permute-done.58.refs_3_.refs_17_ = bf16[128,1088]{1,0:T(8,128)(2,1)S(1)} collective-permute-done((bf16[128,1088]{1,0:T(8,128)(2,1)S(1)}, bf16[128,1088]{1,0:T(8,128)(2,1)S(1)}, u32[]{:S(2)}, u32[]{:S(2)}) %collective-permute-start.58) | collective-permute-done | bytes 278560 | tf_op jit(solution)/shard_map/ppermute | solution.py:62
  246.1 4.9 %out_grads.1 = (bf16[8,136,384]{2,1,0:T(8,128)(2,1)}, f32[2,1088]{1,0:T(2,128)}) custom-call(s32[100]{0:T(128)} %copy-done.10, bf16[128,1088]{1,0:T(8,128)(2,1)} %copy-done.30, bf16[128,1088]{1,0:T(8,128)(2,1)} %collective-permute-done.67.refs_2_, bf16[128,1088]{1,0:T(8,128)(2,1)} %collective-permute-done.68.refs_3_, bf16[128,1088]{1,0:T(8,128)(2,1)} %copy-done.81, ...), custom_call_target="tpu_custom_call" | custom-call | flops 17500000256 | bytes 350000 | tf_op jit(solution)/shard_map/out_grads/pallas_call | solution.py:44
  252.5 3.8 %all-to-all-start.2 = ((bf16[8,136,384]{2,1,0:T(8,128)(2,1)}), bf16[8,136,384]{2,1,0:T(8,128)(2,1)S(1)}, u32[]{:S(2)}, u32[]{:S(2)}) async-start(bf16[8,136,384]{2,1,0:T(8,128)(2,1)} %get-tuple-element.207), calls=%async_computation.4 | async-start | bytes 1671168 | tf_op jit(solution)/shard_map/all_to_all | solution.py:1011
  256.3 2.0 collective-permute-start.75
  258.4 3.9 %finish.1 = (bf16[2,272,128]{2,1,0:T(8,128)(2,1)}, bf16[2,272,128]{2,1,0:T(8,128)(2,1)}, bf16[2,272,128]{2,1,0:T(8,128)(2,1)}, bf16[2,272,128]{2,1,0:T(8,128)(2,1)}) custom-call(s32[100]{0:T(128)} %copy-done.10, f32[128,1088]{1,0:T(8,128)} %copy-done.63, bf16[128,1088]{1,0:T(8,128)(2,1)} %copy-done.85, bf16[128,1088]{1,0:T(8,128)(2,1)} %copy-done.86, ...), custom_call_target="tpu_custom_call" | custom-call | flops 12499999744 | bytes 250000 | tf_op jit(solution)/shard_map/finish/pallas_call | solution.py:44
  262.2 1.6 collective-permute-start.63
  263.8 3.3 %collective-permute-start.64 = (bf16[2,272,128]{2,1,0:T(8,128)(2,1)}, bf16[2,272,128]{2,1,0:T(8,128)(2,1)S(1)}, u32[]{:S(2)}, u32[]{:S(2)}) collective-permute-start(bf16[2,272,128]{2,1,0:T(8,128)(2,1)} %get-tuple-element.190), channel_id=1, source_target_pairs={{2,0},{10,1},{18,2},{26,3},{0,4},{8,5},{16,6},{24,7},{6,8},{14,9},... | collective-permute-start | bytes 417800 | tf_op jit(solution)/shard_map/ppermute | solution.py:1045
  267.1 2.6 collective-permute-start.65
  269.7 8.9 %collective-permute-start.66 = (bf16[2,272,128]{2,1,0:T(8,128)(2,1)}, bf16[2,272,128]{2,1,0:T(8,128)(2,1)S(1)}, u32[]{:S(2)}, u32[]{:S(2)}) collective-permute-start(bf16[2,272,128]{2,1,0:T(8,128)(2,1)} %get-tuple-element.192), channel_id=1, source_target_pairs={{6,0},{14,1},{22,2},{30,3},{4,4},{12,5},{20,6},{28,7},{2,8},{10,9}... | collective-permute-start | bytes 417800 | tf_op jit(solution)/shard_map/ppermute | solution.py:1045
  281.3 1.5 collective-permute-start.78
  282.8 1.4 collective-permute-start.79
  285.1 2.9 collective-permute-start.89
  288.0 3.3 %collective-permute-start.90 = (bf16[136,336]{1,0:T(8,128)(2,1)S(1)}, bf16[136,336]{1,0:T(8,128)(2,1)S(1)}, u32[]{:S(2)}, u32[]{:S(2)}) collective-permute-start(bf16[136,336]{1,0:T(8,128)(2,1)S(1)} %get-tuple-element.214), channel_id=1, source_target_pairs={{0,2},{1,3},{2,0},{3,1},{4,6},{5,7},{6,4},{7,5},{8,10},{9,11},{10,... | collective-permute-start | bytes 274184 | tf_op jit(solution)/shard_map/ppermute | solution.py:66
  291.3 2.8 collective-permute-start.91
  296.5 2.6 collective-permute-start.80
  301.7 1.8 collective-permute-start.83
  303.5 1.7 collective-permute-start.84
  305.2 1.8 collective-permute-start.81
  307.0 1.5 out_land.1
  309.1 1.7 collective-permute-done.81.refs_2_
  313.9 2.2 qkv_land.1
  316.1 2.8 mlp_land.1
  (380 shorter events, 69.4 us)
Async XLA Ops:
  7.2 126.7 %all-gather.3.cloned.1.call-start = ((), (), s32[]{:S(2)}) async-start(), calls=%async_computation.7 | async-start | bytes 3133440 | tf_op jit(solution)/shard_map/all_gather | solution.py:838
  9.8 10.0 %collective-permute-start.4 = (bf16[128,272]{1,0:T(8,128)(2,1)S(1)}, bf16[128,272]{1,0:T(8,128)(2,1)S(1)}, u32[]{:S(2)}, u32[]{:S(2)}) collective-permute-start(bf16[128,272]{1,0:T(8,128)(2,1)S(1)} %get-tuple-element.122), channel_id=1, source_target_pairs={{0,4},{4,0},{8,12},{12,8},{1,5},{5,1},{9,13},{13,9},{2,6},{6,2},{1... | collective-permute-start | bytes 208904 | tf_op jit(solution)/shard_map/ppermute | solution.py:62
  12.8 9.8 %collective-permute-start.5 = (bf16[128,272]{1,0:T(8,128)(2,1)S(1)}, bf16[128,272]{1,0:T(8,128)(2,1)S(1)}, u32[]{:S(2)}, u32[]{:S(2)}) collective-permute-start(bf16[128,272]{1,0:T(8,128)(2,1)S(1)} %get-tuple-element.123), channel_id=1, source_target_pairs={{0,8},{4,12},{8,0},{12,4},{1,9},{5,13},{9,1},{13,5},{2,10},{6,14},... | collective-permute-start | bytes 208904 | tf_op jit(solution)/shard_map/ppermute | solution.py:62
  14.4 11.3 %collective-permute-start.6 = (bf16[128,272]{1,0:T(8,128)(2,1)S(1)}, bf16[128,272]{1,0:T(8,128)(2,1)S(1)}, u32[]{:S(2)}, u32[]{:S(2)}) collective-permute-start(bf16[128,272]{1,0:T(8,128)(2,1)S(1)} %get-tuple-element.124), channel_id=1, source_target_pairs={{0,12},{4,8},{8,4},{12,0},{1,13},{5,9},{9,5},{13,1},{2,14},{6,10},... | collective-permute-start | bytes 208904 | tf_op jit(solution)/shard_map/ppermute | solution.py:62
  15.1 17.8 %collective-permute-start.1 = (bf16[2,272,128]{2,1,0:T(8,128)(2,1)S(1)}, bf16[2,272,128]{2,1,0:T(8,128)(2,1)S(1)}, u32[]{:S(2)}, u32[]{:S(2)}) collective-permute-start(bf16[2,272,128]{2,1,0:T(8,128)(2,1)S(1)} %get-tuple-element.119), channel_id=1, source_target_pairs={{0,2},{1,10},{2,18},{3,26},{4,0},{5,8},{6,16},{7,24},{8,6},{9,14},... | collective-permute-start | bytes 417800 | tf_op jit(solution)/shard_map/ppermute | solution.py:792
  18.2 20.2 %collective-permute-start = (bf16[2,272,128]{2,1,0:T(8,128)(2,1)S(1)}, bf16[2,272,128]{2,1,0:T(8,128)(2,1)S(1)}, u32[]{:S(2)}, u32[]{:S(2)}) collective-permute-start(bf16[2,272,128]{2,1,0:T(8,128)(2,1)S(1)} %get-tuple-element.118.refs_3_), channel_id=1, source_target_pairs={{0,0},{1,8},{2,16},{3,24},{4,2},{5,10},{6,18},{7,26},{8,4},{9,12},... | collective-permute-start | bytes 417800 | tf_op jit(solution)/shard_map/ppermute | solution.py:792
  19.9 15.0 %collective-permute-start.2 = (bf16[2,272,128]{2,1,0:T(8,128)(2,1)S(1)}, bf16[2,272,128]{2,1,0:T(8,128)(2,1)S(1)}, u32[]{:S(2)}, u32[]{:S(2)}) collective-permute-start(bf16[2,272,128]{2,1,0:T(8,128)(2,1)S(1)} %get-tuple-element.120), channel_id=1, source_target_pairs={{0,4},{1,12},{2,20},{3,28},{4,6},{5,14},{6,22},{7,30},{8,0},{9,8},... | collective-permute-start | bytes 417800 | tf_op jit(solution)/shard_map/ppermute | solution.py:792
  22.7 15.7 %collective-permute-start.3 = (bf16[2,272,128]{2,1,0:T(8,128)(2,1)S(1)}, bf16[2,272,128]{2,1,0:T(8,128)(2,1)S(1)}, u32[]{:S(2)}, u32[]{:S(2)}) collective-permute-start(bf16[2,272,128]{2,1,0:T(8,128)(2,1)S(1)} %get-tuple-element.121), channel_id=1, source_target_pairs={{0,6},{1,14},{2,22},{3,30},{4,4},{5,12},{6,20},{7,28},{8,2},{9,10}... | collective-permute-start | bytes 417800 | tf_op jit(solution)/shard_map/ppermute | solution.py:792
  26.4 25.8 %collective-permute-start.8 = (bf16[176,1088]{1,0:T(8,128)(2,1)S(1)}, bf16[176,1088]{1,0:T(8,128)(2,1)S(1)}, u32[]{:S(2)}, u32[]{:S(2)}) collective-permute-start(bf16[176,1088]{1,0:T(8,128)(2,1)S(1)} %join_lanes.1.refs_4_.refs_1_), channel_id=1, source_target_pairs={{0,3},{1,0},{2,1},{3,2},{4,7},{5,4},{6,5},{7,6},{8,11},{9,8},{10,9... | collective-permute-start | bytes 1148936 | tf_op jit(solution)/shard_map/ppermute | solution.py:66
  32.9 19.4 %collective-permute-start.7 = (bf16[176,1088]{1,0:T(8,128)(2,1)S(1)}, bf16[176,1088]{1,0:T(8,128)(2,1)S(1)}, u32[]{:S(2)}, u32[]{:S(2)}) collective-permute-start(bf16[176,1088]{1,0:T(8,128)(2,1)S(1)} %join_lanes.1.refs_4_.refs_1_), channel_id=1, source_target_pairs={{0,1},{1,2},{2,3},{3,0},{4,5},{5,6},{6,7},{7,4},{8,9},{9,10},{10,1... | collective-permute-start | bytes 1148936 | tf_op jit(solution)/shard_map/ppermute | solution.py:66
  34.9 9.4 %collective-permute-start.9 = (bf16[2,136,272]{2,1,0:T(8,128)(2,1)S(1)}, bf16[2,136,272]{2,1,0:T(8,128)(2,1)S(1)}, u32[]{:S(2)}, u32[]{:S(2)}) collective-permute-start(bf16[2,136,272]{2,1,0:T(8,128)(2,1)S(1)} %get-tuple-element.125), channel_id=1, source_target_pairs={{0,4},{4,0},{8,12},{12,8},{1,5},{5,1},{9,13},{13,9},{2,6},{6,2},{1... | collective-permute-start | bytes 443912 | tf_op jit(solution)/shard_map/ppermute | solution.py:62
  38.3 11.3 %collective-permute-start.10 = (bf16[2,136,272]{2,1,0:T(8,128)(2,1)S(1)}, bf16[2,136,272]{2,1,0:T(8,128)(2,1)S(1)}, u32[]{:S(2)}, u32[]{:S(2)}) collective-permute-start(bf16[2,136,272]{2,1,0:T(8,128)(2,1)S(1)} %get-tuple-element.126), channel_id=1, source_target_pairs={{0,8},{4,12},{8,0},{12,4},{1,9},{5,13},{9,1},{13,5},{2,10},{6,14},... | collective-permute-start | bytes 443912 | tf_op jit(solution)/shard_map/ppermute | solution.py:62
  38.4 13.1 %collective-permute-start.11 = (bf16[2,136,272]{2,1,0:T(8,128)(2,1)S(1)}, bf16[2,136,272]{2,1,0:T(8,128)(2,1)S(1)}, u32[]{:S(2)}, u32[]{:S(2)}) collective-permute-start(bf16[2,136,272]{2,1,0:T(8,128)(2,1)S(1)} %get-tuple-element.127), channel_id=1, source_target_pairs={{0,12},{4,8},{8,4},{12,0},{1,13},{5,9},{9,5},{13,1},{2,14},{6,10},... | collective-permute-start | bytes 443912 | tf_op jit(solution)/shard_map/ppermute | solution.py:62
  44.3 31.9 %collective-permute-start.20 = (s32[2,1024]{1,0:T(2,128)S(1)}, s32[2,1024]{1,0:T(2,128)S(1)}, u32[]{:S(2)}, u32[]{:S(2)}) collective-permute-start(s32[2,1024]{1,0:T(2,128)S(1)} %copy-done.43), channel_id=1, source_target_pairs={{0,16},{16,0},{1,17},{17,1},{2,18},{18,2},{3,19},{19,3},{4,20},{20... | collective-permute-start | bytes 24584 | tf_op jit(solution)/shard_map/ppermute | solution.py:58
  49.7 21.8 %collective-permute-start.19 = (bf16[176,1088]{1,0:T(8,128)(2,1)S(1)}, bf16[176,1088]{1,0:T(8,128)(2,1)S(1)}, u32[]{:S(2)}, u32[]{:S(2)}) collective-permute-start(bf16[176,1088]{1,0:T(8,128)(2,1)S(1)} %join_lanes.1.refs_4_.refs_1_), channel_id=1, source_target_pairs={{0,2},{1,3},{2,0},{3,1},{4,6},{5,7},{6,4},{7,5},{8,10},{9,11},{10,... | collective-permute-start | bytes 1148936 | tf_op jit(solution)/shard_map/ppermute | solution.py:66
  53.3 18.2 %collective-permute-start.14 = (bf16[128,1088]{1,0:T(8,128)(2,1)S(1)}, bf16[128,1088]{1,0:T(8,128)(2,1)}, u32[]{:S(2)}, u32[]{:S(2)}) collective-permute-start(bf16[128,1088]{1,0:T(8,128)(2,1)S(1)} %get-tuple-element.128.refs_5_.refs_1_.refs_2_.refs_14_), channel_id=1, source_target_pairs={{0,12},{4,8},{8,4},{12,0},{1,13},{5,9},{9,5},{13,1},{2,14},{6,10},... | collective-permute-start | bytes 835592 | tf_op jit(solution)/shard_map/ppermute | solution.py:62
  56.3 15.7 %collective-permute-start.13 = (bf16[128,1088]{1,0:T(8,128)(2,1)S(1)}, bf16[128,1088]{1,0:T(8,128)(2,1)}, u32[]{:S(2)}, u32[]{:S(2)}) collective-permute-start(bf16[128,1088]{1,0:T(8,128)(2,1)S(1)} %get-tuple-element.128.refs_5_.refs_1_.refs_2_.refs_14_), channel_id=1, source_target_pairs={{0,8},{4,12},{8,0},{12,4},{1,9},{5,13},{9,1},{13,5},{2,10},{6,14},... | collective-permute-start | bytes 835592 | tf_op jit(solution)/shard_map/ppermute | solution.py:62
  56.3 15.8 %collective-permute-start.12 = (bf16[128,1088]{1,0:T(8,128)(2,1)S(1)}, bf16[128,1088]{1,0:T(8,128)(2,1)}, u32[]{:S(2)}, u32[]{:S(2)}) collective-permute-start(bf16[128,1088]{1,0:T(8,128)(2,1)S(1)} %get-tuple-element.128.refs_5_.refs_1_.refs_2_.refs_14_), channel_id=1, source_target_pairs={{0,4},{4,0},{8,12},{12,8},{1,5},{5,1},{9,13},{13,9},{2,6},{6,2},{1... | collective-permute-start | bytes 835592 | tf_op jit(solution)/shard_map/ppermute | solution.py:62
  76.2 17.5 %collective-permute-start.23 = (bf16[176,1088]{1,0:T(8,128)(2,1)S(1)}, bf16[176,1088]{1,0:T(8,128)(2,1)S(1)}, u32[]{:S(2)}, u32[]{:S(2)}) collective-permute-start(bf16[176,1088]{1,0:T(8,128)(2,1)S(1)} %get-tuple-element.133.refs_1_), channel_id=1, source_target_pairs={{0,12},{4,8},{8,4},{12,0},{1,13},{5,9},{9,5},{13,1},{2,14},{6,10},... | collective-permute-start | bytes 1148936 | tf_op jit(solution)/shard_map/ppermute | solution.py:62
  76.8 19.8 %collective-permute-start.22 = (bf16[176,1088]{1,0:T(8,128)(2,1)S(1)}, bf16[176,1088]{1,0:T(8,128)(2,1)S(1)}, u32[]{:S(2)}, u32[]{:S(2)}) collective-permute-start(bf16[176,1088]{1,0:T(8,128)(2,1)S(1)} %get-tuple-element.133.refs_1_), channel_id=1, source_target_pairs={{0,8},{4,12},{8,0},{12,4},{1,9},{5,13},{9,1},{13,5},{2,10},{6,14},... | collective-permute-start | bytes 1148936 | tf_op jit(solution)/shard_map/ppermute | solution.py:62
  78.3 18.3 %collective-permute-start.21 = (bf16[176,1088]{1,0:T(8,128)(2,1)S(1)}, bf16[176,1088]{1,0:T(8,128)(2,1)S(1)}, u32[]{:S(2)}, u32[]{:S(2)}) collective-permute-start(bf16[176,1088]{1,0:T(8,128)(2,1)S(1)} %get-tuple-element.133.refs_1_), channel_id=1, source_target_pairs={{0,4},{4,0},{8,12},{12,8},{1,5},{5,1},{9,13},{13,9},{2,6},{6,2},{1... | collective-permute-start | bytes 1148936 | tf_op jit(solution)/shard_map/ppermute | solution.py:62
  90.1 9.9 %all-to-all-start = ((bf16[8,128,128]{2,1,0:T(8,128)(2,1)}), bf16[8,128,128]{2,1,0:T(8,128)(2,1)S(1)}, u32[]{:S(2)}, u32[]{:S(2)}) async-start(bf16[8,128,128]{2,1,0:T(8,128)(2,1)} %get-tuple-element.131.refs_9_), calls=%async_computation | async-start | bytes 524288 | tf_op jit(solution)/shard_map/all_to_all | solution.py:859
  93.5 185.2 %reduce-scatter.5.cloned.1.call-start = ((), (), s32[]{:S(2)}) async-start(), calls=%async_computation.6 | async-start | bytes 3133440 | tf_op jit(solution)/shard_map/reduce_scatter | solution.py:943
  102.0 13.0 %collective-permute-start.37 = (bf16[128,1088]{1,0:T(8,128)(2,1)S(1)}, bf16[128,1088]{1,0:T(8,128)(2,1)S(1)}, u32[]{:S(2)}, u32[]{:S(2)}) collective-permute-start(bf16[128,1088]{1,0:T(8,128)(2,1)S(1)} %take_tokens.1.refs_5_.refs_1_.refs_4_.refs_6_), channel_id=1, source_target_pairs={{0,12},{4,8},{8,4},{12,0},{1,13},{5,9},{9,5},{13,1},{2,14},{6,10},... | collective-permute-start | bytes 835592 | tf_op jit(solution)/shard_map/ppermute | solution.py:62
  102.7 16.3 %collective-permute-start.36 = (bf16[128,1088]{1,0:T(8,128)(2,1)S(1)}, bf16[128,1088]{1,0:T(8,128)(2,1)S(1)}, u32[]{:S(2)}, u32[]{:S(2)}) collective-permute-start(bf16[128,1088]{1,0:T(8,128)(2,1)S(1)} %take_tokens.1.refs_5_.refs_1_.refs_4_.refs_6_), channel_id=1, source_target_pairs={{0,8},{4,12},{8,0},{12,4},{1,9},{5,13},{9,1},{13,5},{2,10},{6,14},... | collective-permute-start | bytes 835592 | tf_op jit(solution)/shard_map/ppermute | solution.py:62
  104.2 14.9 %collective-permute-start.35 = (bf16[128,1088]{1,0:T(8,128)(2,1)S(1)}, bf16[128,1088]{1,0:T(8,128)(2,1)S(1)}, u32[]{:S(2)}, u32[]{:S(2)}) collective-permute-start(bf16[128,1088]{1,0:T(8,128)(2,1)S(1)} %take_tokens.1.refs_5_.refs_1_.refs_4_.refs_6_), channel_id=1, source_target_pairs={{0,4},{4,0},{8,12},{12,8},{1,5},{5,1},{9,13},{13,9},{2,6},{6,2},{1... | collective-permute-start | bytes 835592 | tf_op jit(solution)/shard_map/ppermute | solution.py:62
  112.7 12.7 %collective-permute-start.30 = (bf16[128,1088]{1,0:T(8,128)(2,1)}, bf16[128,1088]{1,0:T(8,128)(2,1)S(1)}, u32[]{:S(2)}, u32[]{:S(2)}) collective-permute-start(bf16[128,1088]{1,0:T(8,128)(2,1)} %get-tuple-element.142.refs_5_.refs_10_.refs_1_), channel_id=1, source_target_pairs={{0,12},{4,8},{8,4},{12,0},{1,13},{5,9},{9,5},{13,1},{2,14},{6,10},... | collective-permute-start | bytes 835592 | tf_op jit(solution)/shard_map/ppermute | solution.py:62
  113.5 17.4 %collective-permute-start.29 = (bf16[128,1088]{1,0:T(8,128)(2,1)}, bf16[128,1088]{1,0:T(8,128)(2,1)S(1)}, u32[]{:S(2)}, u32[]{:S(2)}) collective-permute-start(bf16[128,1088]{1,0:T(8,128)(2,1)} %get-tuple-element.142.refs_5_.refs_10_.refs_1_), channel_id=1, source_target_pairs={{0,8},{4,12},{8,0},{12,4},{1,9},{5,13},{9,1},{13,5},{2,10},{6,14},... | collective-permute-start | bytes 835592 | tf_op jit(solution)/shard_map/ppermute | solution.py:62
  114.9 16.0 %collective-permute-start.28 = (bf16[128,1088]{1,0:T(8,128)(2,1)}, bf16[128,1088]{1,0:T(8,128)(2,1)}, u32[]{:S(2)}, u32[]{:S(2)}) collective-permute-start(bf16[128,1088]{1,0:T(8,128)(2,1)} %get-tuple-element.142.refs_5_.refs_10_.refs_1_), channel_id=1, source_target_pairs={{0,4},{4,0},{8,12},{12,8},{1,5},{5,1},{9,13},{13,9},{2,6},{6,2},{1... | collective-permute-start | bytes 835592 | tf_op jit(solution)/shard_map/ppermute | solution.py:62
  119.9 11.6 %collective-permute-start.38 = (bf16[128,1088]{1,0:T(8,128)(2,1)S(1)}, bf16[128,1088]{1,0:T(8,128)(2,1)S(1)}, u32[]{:S(2)}, u32[]{:S(2)}) collective-permute-start(bf16[128,1088]{1,0:T(8,128)(2,1)S(1)} %get-tuple-element.143), channel_id=1, source_target_pairs={{0,16},{16,0},{1,17},{17,1},{2,18},{18,2},{3,19},{19,3},{4,20},{20... | collective-permute-start | bytes 835592 | tf_op jit(solution)/shard_map/ppermute | solution.py:58
  119.9 11.6 %collective-permute-start.39 = (bf16[128,1088]{1,0:T(8,128)(2,1)S(1)}, bf16[128,1088]{1,0:T(8,128)(2,1)S(1)}, u32[]{:S(2)}, u32[]{:S(2)}) collective-permute-start(bf16[128,1088]{1,0:T(8,128)(2,1)S(1)} %get-tuple-element.144), channel_id=1, source_target_pairs={{0,16},{16,0},{1,17},{17,1},{2,18},{18,2},{3,19},{19,3},{4,20},{20... | collective-permute-start | bytes 835592 | tf_op jit(solution)/shard_map/ppermute | solution.py:58
  130.9 9.3 %collective-permute-start.31 = (bf16[128,1088]{1,0:T(8,128)(2,1)}, bf16[128,1088]{1,0:T(8,128)(2,1)S(1)}, u32[]{:S(2)}, u32[]{:S(2)}) collective-permute-start(bf16[128,1088]{1,0:T(8,128)(2,1)} %get-tuple-element.142.refs_5_.refs_10_.refs_1_), channel_id=1, source_target_pairs={{0,16},{16,0},{1,17},{17,1},{2,18},{18,2},{3,19},{19,3},{4,20},{20... | collective-permute-start | bytes 835592 | tf_op jit(solution)/shard_map/ppermute | solution.py:58
  131.4 8.8 %collective-permute-start.34 = (bf16[128,1088]{1,0:T(8,128)(2,1)S(1)}, bf16[128,1088]{1,0:T(8,128)(2,1)}, u32[]{:S(2)}, u32[]{:S(2)}) collective-permute-start(bf16[128,1088]{1,0:T(8,128)(2,1)S(1)} %collective-permute-done.30.refs_4_), channel_id=1, source_target_pairs={{0,16},{16,0},{1,17},{17,1},{2,18},{18,2},{3,19},{19,3},{4,20},{20... | collective-permute-start | bytes 835592 | tf_op jit(solution)/shard_map/ppermute | solution.py:58
  173.8 10.6 %collective-permute-start.46 = (bf16[128,1088]{1,0:T(8,128)(2,1)}, bf16[128,1088]{1,0:T(8,128)(2,1)S(1)}, u32[]{:S(2)}, u32[]{:S(2)}) collective-permute-start(bf16[128,1088]{1,0:T(8,128)(2,1)} %copy-done.35), channel_id=1, source_target_pairs={{0,4},{4,0},{8,12},{12,8},{1,5},{5,1},{9,13},{13,9},{2,6},{6,2},{1... | collective-permute-start | bytes 835592 | tf_op jit(solution)/shard_map/ppermute | solution.py:62
  175.3 15.3 %collective-permute-start.47 = (bf16[128,1088]{1,0:T(8,128)(2,1)}, bf16[128,1088]{1,0:T(8,128)(2,1)S(1)}, u32[]{:S(2)}, u32[]{:S(2)}) collective-permute-start(bf16[128,1088]{1,0:T(8,128)(2,1)} %copy-done.34), channel_id=1, source_target_pairs={{0,8},{4,12},{8,0},{12,4},{1,9},{5,13},{9,1},{13,5},{2,10},{6,14},... | collective-permute-start | bytes 835592 | tf_op jit(solution)/shard_map/ppermute | solution.py:62
  176.8 13.8 %collective-permute-start.48 = (bf16[128,1088]{1,0:T(8,128)(2,1)S(1)}, bf16[128,1088]{1,0:T(8,128)(2,1)S(1)}, u32[]{:S(2)}, u32[]{:S(2)}) collective-permute-start(bf16[128,1088]{1,0:T(8,128)(2,1)S(1)} %get-tuple-element.156), channel_id=1, source_target_pairs={{0,12},{4,8},{8,4},{12,0},{1,13},{5,9},{9,5},{13,1},{2,14},{6,10},... | collective-permute-start | bytes 835592 | tf_op jit(solution)/shard_map/ppermute | solution.py:62
  183.9 16.8 %collective-permute-start.49 = (bf16[128,1088]{1,0:T(8,128)(2,1)}, bf16[128,1088]{1,0:T(8,128)(2,1)}, u32[]{:S(2)}, u32[]{:S(2)}) collective-permute-start(bf16[128,1088]{1,0:T(8,128)(2,1)} %get-tuple-element.171), channel_id=1, source_target_pairs={{0,16},{16,0},{1,17},{17,1},{2,18},{18,2},{3,19},{19,3},{4,20},{20... | collective-permute-start | bytes 835592 | tf_op jit(solution)/shard_map/ppermute | solution.py:58
  183.9 17.4 %collective-permute-start.50 = (bf16[128,1088]{1,0:T(8,128)(2,1)}, bf16[128,1088]{1,0:T(8,128)(2,1)}, u32[]{:S(2)}, u32[]{:S(2)}) collective-permute-start(bf16[128,1088]{1,0:T(8,128)(2,1)} %get-tuple-element.172), channel_id=1, source_target_pairs={{0,16},{16,0},{1,17},{17,1},{2,18},{18,2},{3,19},{19,3},{4,20},{20... | collective-permute-start | bytes 835592 | tf_op jit(solution)/shard_map/ppermute | solution.py:58
  184.4 17.1 %collective-permute-start.51 = (bf16[128,1088]{1,0:T(8,128)(2,1)}, bf16[128,1088]{1,0:T(8,128)(2,1)}, u32[]{:S(2)}, u32[]{:S(2)}) collective-permute-start(bf16[128,1088]{1,0:T(8,128)(2,1)} %get-tuple-element.173), channel_id=1, source_target_pairs={{0,16},{16,0},{1,17},{17,1},{2,18},{18,2},{3,19},{19,3},{4,20},{20... | collective-permute-start | bytes 835592 | tf_op jit(solution)/shard_map/ppermute | solution.py:58
  190.7 10.9 %collective-permute-start.52 = (bf16[128,1088]{1,0:T(8,128)(2,1)}, bf16[128,1088]{1,0:T(8,128)(2,1)}, u32[]{:S(2)}, u32[]{:S(2)}) collective-permute-start(bf16[128,1088]{1,0:T(8,128)(2,1)} %get-tuple-element.174), channel_id=1, source_target_pairs={{0,16},{16,0},{1,17},{17,1},{2,18},{18,2},{3,19},{19,3},{4,20},{20... | collective-permute-start | bytes 835592 | tf_op jit(solution)/shard_map/ppermute | solution.py:58
  194.5 10.1 %all-to-all-start.1 = ((bf16[8,128,128]{2,1,0:T(8,128)(2,1)}), bf16[8,128,128]{2,1,0:T(8,128)(2,1)S(1)}, u32[]{:S(2)}, u32[]{:S(2)}) async-start(bf16[8,128,128]{2,1,0:T(8,128)(2,1)} %get-tuple-element.161), calls=%async_computation.1 | async-start | bytes 524288 | tf_op jit(solution)/shard_map/all_to_all | solution.py:958
  197.9 96.3 %reduce-scatter.3.cloned.1.call-start = ((), (), s32[]{:S(2)}) async-start(), calls=%async_computation.5 | async-start | bytes 1474560 | tf_op jit(solution)/shard_map/reduce_scatter | solution.py:991
  198.0 25.4 %collective-permute-start.69 = (bf16[128,1088]{1,0:T(8,128)(2,1)S(1)}, bf16[128,1088]{1,0:T(8,128)(2,1)S(1)}, u32[]{:S(2)}, u32[]{:S(2)}) collective-permute-start(bf16[128,1088]{1,0:T(8,128)(2,1)S(1)} %get-tuple-element.196.refs_1_), channel_id=1, source_target_pairs={{0,12},{4,8},{8,4},{12,0},{1,13},{5,9},{9,5},{13,1},{2,14},{6,10},... | collective-permute-start | bytes 835592 | tf_op jit(solution)/shard_map/ppermute | solution.py:62
  200.7 23.0 %collective-permute-start.68 = (bf16[128,1088]{1,0:T(8,128)(2,1)S(1)}, bf16[128,1088]{1,0:T(8,128)(2,1)}, u32[]{:S(2)}, u32[]{:S(2)}) collective-permute-start(bf16[128,1088]{1,0:T(8,128)(2,1)S(1)} %get-tuple-element.196.refs_1_), channel_id=1, source_target_pairs={{0,8},{4,12},{8,0},{12,4},{1,9},{5,13},{9,1},{13,5},{2,10},{6,14},... | collective-permute-start | bytes 835592 | tf_op jit(solution)/shard_map/ppermute | solution.py:62
  201.3 22.5 %collective-permute-start.67 = (bf16[128,1088]{1,0:T(8,128)(2,1)S(1)}, bf16[128,1088]{1,0:T(8,128)(2,1)}, u32[]{:S(2)}, u32[]{:S(2)}) collective-permute-start(bf16[128,1088]{1,0:T(8,128)(2,1)S(1)} %get-tuple-element.196.refs_1_), channel_id=1, source_target_pairs={{0,4},{4,0},{8,12},{12,8},{1,5},{5,1},{9,13},{13,9},{2,6},{6,2},{1... | collective-permute-start | bytes 835592 | tf_op jit(solution)/shard_map/ppermute | solution.py:62
  228.5 9.9 %collective-permute-start.57 = (bf16[128,1088]{1,0:T(8,128)(2,1)S(1)}, bf16[128,1088]{1,0:T(8,128)(2,1)S(1)}, u32[]{:S(2)}, u32[]{:S(2)}) collective-permute-start(bf16[128,1088]{1,0:T(8,128)(2,1)S(1)} %get-tuple-element.182), channel_id=1, source_target_pairs={{0,4},{4,0},{8,12},{12,8},{1,5},{5,1},{9,13},{13,9},{2,6},{6,2},{1... | collective-permute-start | bytes 835592 | tf_op jit(solution)/shard_map/ppermute | solution.py:62
  229.1 16.2 %collective-permute-start.58 = (bf16[128,1088]{1,0:T(8,128)(2,1)S(1)}, bf16[128,1088]{1,0:T(8,128)(2,1)S(1)}, u32[]{:S(2)}, u32[]{:S(2)}) collective-permute-start(bf16[128,1088]{1,0:T(8,128)(2,1)S(1)} %get-tuple-element.183), channel_id=1, source_target_pairs={{0,8},{4,12},{8,0},{12,4},{1,9},{5,13},{9,1},{13,5},{2,10},{6,14},... | collective-permute-start | bytes 835592 | tf_op jit(solution)/shard_map/ppermute | solution.py:62
  229.8 15.5 %collective-permute-start.59 = (bf16[128,1088]{1,0:T(8,128)(2,1)S(1)}, bf16[128,1088]{1,0:T(8,128)(2,1)S(1)}, u32[]{:S(2)}, u32[]{:S(2)}) collective-permute-start(bf16[128,1088]{1,0:T(8,128)(2,1)S(1)} %get-tuple-element.184), channel_id=1, source_target_pairs={{0,12},{4,8},{8,4},{12,0},{1,13},{5,9},{9,5},{13,1},{2,14},{6,10},... | collective-permute-start | bytes 835592 | tf_op jit(solution)/shard_map/ppermute | solution.py:62
  232.1 26.3 %collective-permute-start.60 = (bf16[128,1088]{1,0:T(8,128)(2,1)S(1)}, bf16[128,1088]{1,0:T(8,128)(2,1)}, u32[]{:S(2)}, u32[]{:S(2)}) collective-permute-start(bf16[128,1088]{1,0:T(8,128)(2,1)S(1)} %get-tuple-element.185), channel_id=1, source_target_pairs={{0,4},{4,0},{8,12},{12,8},{1,5},{5,1},{9,13},{13,9},{2,6},{6,2},{1... | collective-permute-start | bytes 835592 | tf_op jit(solution)/shard_map/ppermute | solution.py:62
  232.7 25.6 %collective-permute-start.61 = (bf16[128,1088]{1,0:T(8,128)(2,1)S(1)}, bf16[128,1088]{1,0:T(8,128)(2,1)}, u32[]{:S(2)}, u32[]{:S(2)}) collective-permute-start(bf16[128,1088]{1,0:T(8,128)(2,1)S(1)} %get-tuple-element.186), channel_id=1, source_target_pairs={{0,8},{4,12},{8,0},{12,4},{1,9},{5,13},{9,1},{13,5},{2,10},{6,14},... | collective-permute-start | bytes 835592 | tf_op jit(solution)/shard_map/ppermute | solution.py:62
  238.4 20.0 %collective-permute-start.62 = (bf16[128,1088]{1,0:T(8,128)(2,1)S(1)}, bf16[128,1088]{1,0:T(8,128)(2,1)}, u32[]{:S(2)}, u32[]{:S(2)}) collective-permute-start(bf16[128,1088]{1,0:T(8,128)(2,1)S(1)} %get-tuple-element.187), channel_id=1, source_target_pairs={{0,12},{4,8},{8,4},{12,0},{1,13},{5,9},{9,5},{13,1},{2,14},{6,10},... | collective-permute-start | bytes 835592 | tf_op jit(solution)/shard_map/ppermute | solution.py:62
  252.5 31.8 %all-to-all-start.2 = ((bf16[8,136,384]{2,1,0:T(8,128)(2,1)}), bf16[8,136,384]{2,1,0:T(8,128)(2,1)S(1)}, u32[]{:S(2)}, u32[]{:S(2)}) async-start(bf16[8,136,384]{2,1,0:T(8,128)(2,1)} %get-tuple-element.207), calls=%async_computation.4 | async-start | bytes 1671168 | tf_op jit(solution)/shard_map/all_to_all | solution.py:1011
  256.3 22.2 %collective-permute-start.75 = (f32[12,1088]{1,0:T(8,128)S(1)}, f32[12,1088]{1,0:T(8,128)S(1)}, u32[]{:S(2)}, u32[]{:S(2)}) collective-permute-start(f32[12,1088]{1,0:T(8,128)S(1)} %add.17), channel_id=1, source_target_pairs={{0,4},{4,0},{8,12},{12,8},{1,5},{5,1},{9,13},{13,9},{2,6},{6,2},{1... | collective-permute-start | bytes 156680 | tf_op jit(solution)/shard_map/ppermute | solution.py:62
  262.2 18.4 %collective-permute-start.63 = (bf16[2,272,128]{2,1,0:T(8,128)(2,1)}, bf16[2,272,128]{2,1,0:T(8,128)(2,1)S(1)}, u32[]{:S(2)}, u32[]{:S(2)}) collective-permute-start(bf16[2,272,128]{2,1,0:T(8,128)(2,1)} %get-tuple-element.189), channel_id=1, source_target_pairs={{0,0},{8,1},{16,2},{24,3},{2,4},{10,5},{18,6},{26,7},{4,8},{12,9},... | collective-permute-start | bytes 417800 | tf_op jit(solution)/shard_map/ppermute | solution.py:1045
  263.8 17.5 %collective-permute-start.64 = (bf16[2,272,128]{2,1,0:T(8,128)(2,1)}, bf16[2,272,128]{2,1,0:T(8,128)(2,1)S(1)}, u32[]{:S(2)}, u32[]{:S(2)}) collective-permute-start(bf16[2,272,128]{2,1,0:T(8,128)(2,1)} %get-tuple-element.190), channel_id=1, source_target_pairs={{2,0},{10,1},{18,2},{26,3},{0,4},{8,5},{16,6},{24,7},{6,8},{14,9},... | collective-permute-start | bytes 417800 | tf_op jit(solution)/shard_map/ppermute | solution.py:1045
  267.1 15.7 %collective-permute-start.65 = (bf16[2,272,128]{2,1,0:T(8,128)(2,1)}, bf16[2,272,128]{2,1,0:T(8,128)(2,1)S(1)}, u32[]{:S(2)}, u32[]{:S(2)}) collective-permute-start(bf16[2,272,128]{2,1,0:T(8,128)(2,1)} %get-tuple-element.191), channel_id=1, source_target_pairs={{4,0},{12,1},{20,2},{28,3},{6,4},{14,5},{22,6},{30,7},{0,8},{8,9},... | collective-permute-start | bytes 417800 | tf_op jit(solution)/shard_map/ppermute | solution.py:1045
  269.7 15.4 %collective-permute-start.66 = (bf16[2,272,128]{2,1,0:T(8,128)(2,1)}, bf16[2,272,128]{2,1,0:T(8,128)(2,1)S(1)}, u32[]{:S(2)}, u32[]{:S(2)}) collective-permute-start(bf16[2,272,128]{2,1,0:T(8,128)(2,1)} %get-tuple-element.192), channel_id=1, source_target_pairs={{6,0},{14,1},{22,2},{30,3},{4,4},{12,5},{20,6},{28,7},{2,8},{10,9}... | collective-permute-start | bytes 417800 | tf_op jit(solution)/shard_map/ppermute | solution.py:1045
  278.6 9.4 %collective-permute-start.76 = (f32[12,1088]{1,0:T(8,128)S(1)}, f32[12,1088]{1,0:T(8,128)S(1)}, u32[]{:S(2)}, u32[]{:S(2)}) collective-permute-start(f32[12,1088]{1,0:T(8,128)S(1)} %add.18.refs_1_), channel_id=1, source_target_pairs={{0,8},{4,12},{8,0},{12,4},{1,9},{5,13},{9,1},{13,5},{2,10},{6,14},... | collective-permute-start | bytes 156680 | tf_op jit(solution)/shard_map/ppermute | solution.py:62
  280.7 10.6 %collective-permute-start.77 = (bf16[2,136,272]{2,1,0:T(8,128)(2,1)S(1)}, bf16[2,136,272]{2,1,0:T(8,128)(2,1)S(1)}, u32[]{:S(2)}, u32[]{:S(2)}) collective-permute-start(bf16[2,136,272]{2,1,0:T(8,128)(2,1)S(1)} %get-tuple-element.204), channel_id=1, source_target_pairs={{0,4},{4,0},{8,12},{12,8},{1,5},{5,1},{9,13},{13,9},{2,6},{6,2},{1... | collective-permute-start | bytes 443912 | tf_op jit(solution)/shard_map/ppermute | solution.py:62
  281.3 12.9 %collective-permute-start.78 = (bf16[2,136,272]{2,1,0:T(8,128)(2,1)S(1)}, bf16[2,136,272]{2,1,0:T(8,128)(2,1)S(1)}, u32[]{:S(2)}, u32[]{:S(2)}) collective-permute-start(bf16[2,136,272]{2,1,0:T(8,128)(2,1)S(1)} %get-tuple-element.205), channel_id=1, source_target_pairs={{0,8},{4,12},{8,0},{12,4},{1,9},{5,13},{9,1},{13,5},{2,10},{6,14},... | collective-permute-start | bytes 443912 | tf_op jit(solution)/shard_map/ppermute | solution.py:62
  282.8 11.4 %collective-permute-start.79 = (bf16[2,136,272]{2,1,0:T(8,128)(2,1)S(1)}, bf16[2,136,272]{2,1,0:T(8,128)(2,1)S(1)}, u32[]{:S(2)}, u32[]{:S(2)}) collective-permute-start(bf16[2,136,272]{2,1,0:T(8,128)(2,1)S(1)} %get-tuple-element.206), channel_id=1, source_target_pairs={{0,12},{4,8},{8,4},{12,0},{1,13},{5,9},{9,5},{13,1},{2,14},{6,10},... | collective-permute-start | bytes 443912 | tf_op jit(solution)/shard_map/ppermute | solution.py:62
  285.1 13.9 %collective-permute-start.89 = (bf16[136,336]{1,0:T(8,128)(2,1)S(1)}, bf16[136,336]{1,0:T(8,128)(2,1)S(1)}, u32[]{:S(2)}, u32[]{:S(2)}) collective-permute-start(bf16[136,336]{1,0:T(8,128)(2,1)S(1)} %get-tuple-element.213), channel_id=1, source_target_pairs={{0,1},{1,2},{2,3},{3,0},{4,5},{5,6},{6,7},{7,4},{8,9},{9,10},{10,1... | collective-permute-start | bytes 274184 | tf_op jit(solution)/shard_map/ppermute | solution.py:66
  288.0 11.1 %collective-permute-start.90 = (bf16[136,336]{1,0:T(8,128)(2,1)S(1)}, bf16[136,336]{1,0:T(8,128)(2,1)S(1)}, u32[]{:S(2)}, u32[]{:S(2)}) collective-permute-start(bf16[136,336]{1,0:T(8,128)(2,1)S(1)} %get-tuple-element.214), channel_id=1, source_target_pairs={{0,2},{1,3},{2,0},{3,1},{4,6},{5,7},{6,4},{7,5},{8,10},{9,11},{10,... | collective-permute-start | bytes 274184 | tf_op jit(solution)/shard_map/ppermute | solution.py:66
  301.2 14.8 %collective-permute-start.93 = (bf16[2,136,272]{2,1,0:T(8,128)(2,1)S(1)}, bf16[2,136,272]{2,1,0:T(8,128)(2,1)S(1)}, u32[]{:S(2)}, u32[]{:S(2)}) collective-permute-start(bf16[2,136,272]{2,1,0:T(8,128)(2,1)S(1)} %get-tuple-element.216.refs_1_), channel_id=1, source_target_pairs={{0,16},{16,0},{1,17},{17,1},{2,18},{18,2},{3,19},{19,3},{4,20},{20... | collective-permute-start | bytes 443912 | tf_op jit(solution)/shard_map/ppermute | solution.py:58
  (129 other events, 943.7 us)
Sparse Core Ops, SparseCore 0:
  76.3 57.5 all-gather.2
  173.9 54.0 reduce-scatter.4
  232.2 31.6 reduce-scatter.2
